TPU v7x, 128 devices: a whole 4x4x4 slice. The times are simulated.
128 devices in a mesh: dp: 64 (over y, x, z_hi, core), seq: 2 (over z_lo).
Axes of the slice: x: 4, y: 4, z: 4 (z_hi: 2, z_lo: 2; z = z_hi * 2 + z_lo), core: 2. Of those that a mesh axis runs over, the one named last changes fastest.
Arguments:
- inputs: bfloat16 [64, 258, 768], P('dp', 'seq'), may hold values from -6 to 6
- skipped: bfloat16 [64, 258, 768], P('dp', 'seq'), may hold values from -6 to 6
- cotangent: bfloat16 [64, 258, 768], P('dp', 'seq'), may hold values from -6 to 6
- timestep: int32 [64], P('dp'), may hold values from 0 to 999
- class_ids: int32 [64], P('dp'), may hold values from 0 to 1000
- time_weight: float32 [1000], replicated, may hold values from 0.3 to 3
- class_weight: float32 [1001], replicated, may hold values from 0.3 to 3
- skip_weight: bfloat16 [1179648], P(('dp', 'seq')), may hold values from -0.15625 to 0.15625
- skip_bias: bfloat16 [768], P(('dp', 'seq')), may hold values from -1.796875 to 1.796875
- first_gain: bfloat16 [768], P(('dp', 'seq')), may hold values from 0.25 to 1.75
- first_shift: bfloat16 [768], P(('dp', 'seq')), may hold values from -1.796875 to 1.796875
- triple_weight: bfloat16 [1769472], P(('dp', 'seq')), may hold values from -0.21875 to 0.21875
- merge_weight: bfloat16 [589824], P(('dp', 'seq')), may hold values from -1.75 to 1.75
- merge_bias: bfloat16 [768], P(('dp', 'seq')), may hold values from -1.796875 to 1.796875
- second_gain: bfloat16 [768], P(('dp', 'seq')), may hold values from 0.25 to 1.75
- second_shift: bfloat16 [768], P(('dp', 'seq')), may hold values from -1.796875 to 1.796875
- expand_weight: bfloat16 [2359296], P(('dp', 'seq')), may hold values from -0.21875 to 0.21875
- expand_bias: bfloat16 [3072], P(('dp', 'seq')), may hold values from -1.796875 to 1.796875
- contract_weight: bfloat16 [2359296], P(('dp', 'seq')), may hold values from -0.109375 to 0.109375
- contract_bias: bfloat16 [768], P(('dp', 'seq')), may hold values from -1.796875 to 1.796875
Outputs:
- block_output: bfloat16 [64, 258, 768], P('dp', 'seq')
- input_grad: bfloat16 [64, 258, 768], P('dp', 'seq')
- skip_grad: bfloat16 [64, 258, 768], P('dp', 'seq')
- skip_weight_grad: float32 [1179648], P(('dp', 'seq'))
- skip_bias_grad: float32 [768], P(('dp', 'seq'))
- first_gain_grad: float32 [768], P(('dp', 'seq'))
- first_shift_grad: float32 [768], P(('dp', 'seq'))
- triple_weight_grad: float32 [1769472], P(('dp', 'seq'))
- merge_weight_grad: float32 [589824], P(('dp', 'seq'))
- merge_bias_grad: float32 [768], P(('dp', 'seq'))
- second_gain_grad: float32 [768], P(('dp', 'seq'))
- second_shift_grad: float32 [768], P(('dp', 'seq'))
- expand_weight_grad: float32 [2359296], P(('dp', 'seq'))
- expand_bias_grad: float32 [3072], P(('dp', 'seq'))
- contract_weight_grad: float32 [2359296], P(('dp', 'seq'))
- contract_bias_grad: float32 [768], P(('dp', 'seq'))
All inputs are finite; a program needn't handle non-finite values.
Results may differ from a plain program's by a relative error of at most 0.017.
Values may be sent and summed in bfloat16 or wider, within the bound.
No kernel may reach another device: no remote copies, remote signals or barrier semaphores. Data moves between devices by JAX's collectives and lax.ppermute only.
A program may use at most 192 MiB of HBM per device.

v0:
```python
import math

import jax
import jax.numpy as jnp
from jax import lax
from jax.sharding import PartitionSpec as P

D = 768
HEADS = 12
HEAD_DIM = 64
FF = 3072


epsilon = 1e-05


def product(left, right):
    return jnp.dot(left, right, preferred_element_type=jnp.float32)


def left_contract(left, right):
    return lax.dot_general(
        left, right, (((0,), (0,)), ((), ())), preferred_element_type=jnp.float32
    )


def right_contract(left, right):
    return lax.dot_general(
        left, right, (((1,), (1,)), ((), ())), preferred_element_type=jnp.float32
    )


def norm_forward(values, gain, shift):
    mean_value = jnp.mean(values, axis=-1, keepdims=True)
    centered = values - mean_value
    variance = jnp.mean(centered * centered, axis=-1, keepdims=True)
    inverse = lax.rsqrt(variance + epsilon)
    scaled = centered * inverse
    return (scaled * gain + shift, scaled, inverse)


def norm_backward(incoming, scaled, inverse, gain):
    weighted = incoming * gain
    first_mean = jnp.mean(weighted, axis=-1, keepdims=True)
    second_mean = jnp.mean(weighted * scaled, axis=-1, keepdims=True)
    value_grad = inverse * (weighted - first_mean - scaled * second_mean)
    return (value_grad, jnp.sum(incoming * scaled, axis=0), jnp.sum(incoming, axis=0))


def gelu_exact(values):
    return 0.5 * values * (1.0 + lax.erf(values * (1.0 / math.sqrt(2.0))))


def gelu_slope(values):
    cumulative = 0.5 * (1.0 + lax.erf(values * (1.0 / math.sqrt(2.0))))
    density = jnp.exp(-0.5 * values * values) * (1.0 / math.sqrt(2.0 * math.pi))
    return cumulative + values * density


def shape_weights(flat_all):
    target_shapes = (
        (2 * D, D),
        (D,),
        (D,),
        (D,),
        (D, 3 * D),
        (D, D),
        (D,),
        (D,),
        (D,),
        (D, FF),
        (FF,),
        (FF, D),
        (D,),
    )
    return tuple(
        (
            flat_piece.reshape(target_shape)
            for flat_piece, target_shape in zip(flat_all, target_shapes)
        )
    )


def pick_table(indices, table):
    match = indices[:, None] == jnp.arange(table.shape[0], dtype=jnp.int32)[None, :]
    return jnp.sum(jnp.where(match, table[None, :], 0.0), axis=1)


def per_device(
    inputs,
    skipped,
    cotangent,
    timestep,
    class_ids,
    time_weight,
    class_weight,
    skip_weight,
    skip_bias,
    first_gain,
    first_shift,
    triple_weight,
    merge_weight,
    merge_bias,
    second_gain,
    second_shift,
    expand_weight,
    expand_bias,
    contract_weight,
    contract_bias,
):
    gathered = (
        lax.all_gather(skip_weight, ("dp", "seq"), axis=0, tiled=True),
        lax.all_gather(skip_bias, ("dp", "seq"), axis=0, tiled=True),
        lax.all_gather(first_gain, ("dp", "seq"), axis=0, tiled=True),
        lax.all_gather(first_shift, ("dp", "seq"), axis=0, tiled=True),
        lax.all_gather(triple_weight, ("dp", "seq"), axis=0, tiled=True),
        lax.all_gather(merge_weight, ("dp", "seq"), axis=0, tiled=True),
        lax.all_gather(merge_bias, ("dp", "seq"), axis=0, tiled=True),
        lax.all_gather(second_gain, ("dp", "seq"), axis=0, tiled=True),
        lax.all_gather(second_shift, ("dp", "seq"), axis=0, tiled=True),
        lax.all_gather(expand_weight, ("dp", "seq"), axis=0, tiled=True),
        lax.all_gather(expand_bias, ("dp", "seq"), axis=0, tiled=True),
        lax.all_gather(contract_weight, ("dp", "seq"), axis=0, tiled=True),
        lax.all_gather(contract_bias, ("dp", "seq"), axis=0, tiled=True),
    )
    (
        skip_mat,
        skip_add,
        first_scale,
        first_move,
        triple_mat,
        merge_mat,
        merge_add,
        second_scale,
        second_move,
        expand_mat,
        expand_add,
        contract_mat,
        contract_add,
    ) = shape_weights(gathered)
    images, half_len = (inputs.shape[0], inputs.shape[1])
    tok_rows = images * half_len
    score_scale = 1.0 / math.sqrt(HEAD_DIM)
    joined = jnp.concatenate([inputs.reshape(tok_rows, D), skipped.reshape(tok_rows, D)], axis=1)
    united = product(joined, skip_mat) + skip_add.astype(jnp.float32)
    normed, first_hat, first_inv = norm_forward(
        united, first_scale.astype(jnp.float32), first_move.astype(jnp.float32)
    )
    normed_low = normed.astype(jnp.bfloat16)
    triple = product(normed_low, triple_mat).astype(jnp.bfloat16)
    query = triple[:, :D].reshape(images, half_len, HEADS, HEAD_DIM)
    key_all, value_all = (
        lax.all_gather(
            triple[:, D : 2 * D].reshape(images, half_len, D), "seq", axis=1, tiled=True
        ),
        lax.all_gather(triple[:, 2 * D :].reshape(images, half_len, D), "seq", axis=1, tiled=True),
    )
    seq_len = key_all.shape[1]
    key_heads = key_all.reshape(images, seq_len, HEADS, HEAD_DIM)
    value_heads = value_all.reshape(images, seq_len, HEADS, HEAD_DIM)
    scores = (
        jnp.einsum("iqhd,ikhd->ihqk", query, key_heads, preferred_element_type=jnp.float32)
        * score_scale
    )
    largest = jnp.max(scores, axis=-1, keepdims=True)
    powered = jnp.exp(scores - largest)
    totals = jnp.sum(powered, axis=-1, keepdims=True)
    log_total = largest + jnp.log(totals)
    attention = (powered / totals).astype(jnp.bfloat16)
    mixed_heads = jnp.einsum(
        "ihqk,ikhd->iqhd", attention, value_heads, preferred_element_type=jnp.float32
    )
    mixed_low = mixed_heads.reshape(tok_rows, D).astype(jnp.bfloat16)
    middle = united + product(mixed_low, merge_mat) + merge_add.astype(jnp.float32)
    normed_two, second_hat, second_inv = norm_forward(
        middle, second_scale.astype(jnp.float32), second_move.astype(jnp.float32)
    )
    normed_two_low = normed_two.astype(jnp.bfloat16)
    before = product(normed_two_low, expand_mat) + expand_add.astype(jnp.float32)
    active = gelu_exact(before).astype(jnp.bfloat16)
    output = middle + product(active, contract_mat) + contract_add.astype(jnp.float32)
    image_scale = pick_table(timestep, time_weight) * pick_table(class_ids, class_weight)
    out_grad = (cotangent.astype(jnp.float32) * image_scale[:, None, None]).reshape(tok_rows, D)
    regathered = (
        lax.all_gather(skip_weight, ("dp", "seq"), axis=0, tiled=True),
        lax.all_gather(skip_bias, ("dp", "seq"), axis=0, tiled=True),
        lax.all_gather(first_gain, ("dp", "seq"), axis=0, tiled=True),
        lax.all_gather(first_shift, ("dp", "seq"), axis=0, tiled=True),
        lax.all_gather(triple_weight, ("dp", "seq"), axis=0, tiled=True),
        lax.all_gather(merge_weight, ("dp", "seq"), axis=0, tiled=True),
        lax.all_gather(merge_bias, ("dp", "seq"), axis=0, tiled=True),
        lax.all_gather(second_gain, ("dp", "seq"), axis=0, tiled=True),
        lax.all_gather(second_shift, ("dp", "seq"), axis=0, tiled=True),
        lax.all_gather(expand_weight, ("dp", "seq"), axis=0, tiled=True),
        lax.all_gather(expand_bias, ("dp", "seq"), axis=0, tiled=True),
        lax.all_gather(contract_weight, ("dp", "seq"), axis=0, tiled=True),
        lax.all_gather(contract_bias, ("dp", "seq"), axis=0, tiled=True),
    )
    (
        skip_mat,
        skip_add,
        first_scale,
        first_move,
        triple_mat,
        merge_mat,
        merge_add,
        second_scale,
        second_move,
        expand_mat,
        expand_add,
        contract_mat,
        contract_add,
    ) = shape_weights(regathered)
    after_low = out_grad.astype(jnp.bfloat16)
    contract_bias_grad = jnp.sum(after_low.astype(jnp.float32), axis=0)
    contract_weight_grad = left_contract(active, after_low)
    before_low = (right_contract(after_low, contract_mat) * gelu_slope(before)).astype(jnp.bfloat16)
    expand_bias_grad = jnp.sum(before_low.astype(jnp.float32), axis=0)
    expand_weight_grad = left_contract(normed_two_low, before_low)
    back_two, second_gain_grad, second_shift_grad = norm_backward(
        right_contract(before_low, expand_mat),
        second_hat,
        second_inv,
        second_scale.astype(jnp.float32),
    )
    middle_grad = out_grad + back_two
    attend_low = middle_grad.astype(jnp.bfloat16)
    merge_bias_grad = jnp.sum(attend_low.astype(jnp.float32), axis=0)
    merge_weight_grad = left_contract(mixed_low, attend_low)
    mixed_grad = right_contract(attend_low, merge_mat).astype(jnp.bfloat16)
    mixed_grad = mixed_grad.reshape(images, half_len, HEADS, HEAD_DIM)
    scores_again = (
        jnp.einsum("iqhd,ikhd->ihqk", query, key_heads, preferred_element_type=jnp.float32)
        * score_scale
    )
    soft_again = jnp.exp(scores_again - log_total)
    soft_low = soft_again.astype(jnp.bfloat16)
    soft_grad = jnp.einsum(
        "iqhd,ikhd->ihqk", mixed_grad, value_heads, preferred_element_type=jnp.float32
    )
    inner_sum = jnp.sum(soft_again * soft_grad, axis=-1, keepdims=True)
    scores_grad = (soft_again * (soft_grad - inner_sum)).astype(jnp.bfloat16)
    query_grad = (
        jnp.einsum("ihqk,ikhd->iqhd", scores_grad, key_heads, preferred_element_type=jnp.float32)
        * score_scale
    )
    query_grad = query_grad.reshape(tok_rows, D).astype(jnp.bfloat16)
    key_part = (
        jnp.einsum("ihqk,iqhd->ikhd", scores_grad, query, preferred_element_type=jnp.float32)
        * score_scale
    )
    value_part = jnp.einsum(
        "ihqk,iqhd->ikhd", soft_low, mixed_grad, preferred_element_type=jnp.float32
    )
    key_grad, value_grad = (
        lax.psum_scatter(
            key_part.reshape(images, seq_len, D).astype(jnp.bfloat16),
            "seq",
            scatter_dimension=1,
            tiled=True,
        ).astype(jnp.float32),
        lax.psum_scatter(
            value_part.reshape(images, seq_len, D).astype(jnp.bfloat16),
            "seq",
            scatter_dimension=1,
            tiled=True,
        ).astype(jnp.float32),
    )
    triple_grad = jnp.concatenate(
        [
            query_grad,
            key_grad.reshape(tok_rows, D).astype(jnp.bfloat16),
            value_grad.reshape(tok_rows, D).astype(jnp.bfloat16),
        ],
        axis=1,
    )
    triple_weight_grad = left_contract(normed_low, triple_grad)
    back_one, first_gain_grad, first_shift_grad = norm_backward(
        right_contract(triple_grad, triple_mat),
        first_hat,
        first_inv,
        first_scale.astype(jnp.float32),
    )
    united_low = (middle_grad + back_one).astype(jnp.bfloat16)
    skip_bias_grad = jnp.sum(united_low.astype(jnp.float32), axis=0)
    skip_weight_grad = left_contract(joined, united_low)
    joined_grad = right_contract(united_low, skip_mat)
    input_grad = joined_grad[:, :D].reshape(images, half_len, D).astype(jnp.bfloat16)
    skip_grad = joined_grad[:, D:].reshape(images, half_len, D).astype(jnp.bfloat16)
    owned = (
        lax.psum_scatter(
            skip_weight_grad.reshape(-1), ("dp", "seq"), scatter_dimension=0, tiled=True
        ),
        lax.psum_scatter(skip_bias_grad, ("dp", "seq"), scatter_dimension=0, tiled=True),
        lax.psum_scatter(first_gain_grad, ("dp", "seq"), scatter_dimension=0, tiled=True),
        lax.psum_scatter(first_shift_grad, ("dp", "seq"), scatter_dimension=0, tiled=True),
        lax.psum_scatter(
            triple_weight_grad.reshape(-1), ("dp", "seq"), scatter_dimension=0, tiled=True
        ),
        lax.psum_scatter(
            merge_weight_grad.reshape(-1), ("dp", "seq"), scatter_dimension=0, tiled=True
        ),
        lax.psum_scatter(merge_bias_grad, ("dp", "seq"), scatter_dimension=0, tiled=True),
        lax.psum_scatter(second_gain_grad, ("dp", "seq"), scatter_dimension=0, tiled=True),
        lax.psum_scatter(second_shift_grad, ("dp", "seq"), scatter_dimension=0, tiled=True),
        lax.psum_scatter(
            expand_weight_grad.reshape(-1), ("dp", "seq"), scatter_dimension=0, tiled=True
        ),
        lax.psum_scatter(expand_bias_grad, ("dp", "seq"), scatter_dimension=0, tiled=True),
        lax.psum_scatter(
            contract_weight_grad.reshape(-1), ("dp", "seq"), scatter_dimension=0, tiled=True
        ),
        lax.psum_scatter(contract_bias_grad, ("dp", "seq"), scatter_dimension=0, tiled=True),
    )
    block_output = output.reshape(images, half_len, D).astype(jnp.bfloat16)
    return (block_output, input_grad, skip_grad) + tuple(owned)


def solution(mesh):
    placed = (
        P("dp", "seq", None),
        P("dp", "seq", None),
        P("dp", "seq", None),
        P("dp"),
        P("dp"),
        P(),
        P(),
        P(("dp", "seq")),
        P(("dp", "seq")),
        P(("dp", "seq")),
        P(("dp", "seq")),
        P(("dp", "seq")),
        P(("dp", "seq")),
        P(("dp", "seq")),
        P(("dp", "seq")),
        P(("dp", "seq")),
        P(("dp", "seq")),
        P(("dp", "seq")),
        P(("dp", "seq")),
        P(("dp", "seq")),
    )
    return jax.shard_map(
        per_device,
        mesh=mesh,
        in_specs=placed,
        out_specs=(
            P("dp", "seq", None),
            P("dp", "seq", None),
            P("dp", "seq", None),
            P(("dp", "seq")),
            P(("dp", "seq")),
            P(("dp", "seq")),
            P(("dp", "seq")),
            P(("dp", "seq")),
            P(("dp", "seq")),
            P(("dp", "seq")),
            P(("dp", "seq")),
            P(("dp", "seq")),
            P(("dp", "seq")),
            P(("dp", "seq")),
            P(("dp", "seq")),
            P(("dp", "seq")),
        ),
        check_vma=False,
    )
```

profile of v0, /device:TPU:1, one launch (start us, length us, event | category | flops | bytes accessed | tf_op | source)
XLA Modules:
  0.0 1968.3 jit_solution(14658970070117068668)
XLA Ops:
  20.0 69.2 %all-reduce.25 = (bf16[768]{0:T(1024)(128)(2,1)S(1)}, bf16[768]{0:T(1024)(128)(2,1)S(1)}, bf16[768]{0:T(1024)(128)(2,1)S(1)}, bf16[768]{0:T(1024)(128)(2,1)S(1)}...) all-reduce(bf16[768]{0:T(1024)(128)(2,1)S(1)} %dynamic-update-slice, ...), channel_id=1, replica_groups=mesh['dp'=64,'seq'=2] {'dp','seq'}, use_global_device_ids=true, to_apply=%add | all-reduce | flops 8448 | bytes 33792
  95.1 219.3 %all-gather.20.cloned.1.call-done = bf16[128,1,4608]{2,1,0:T(2,128)(2,1)} async-done(((bf16[1,1,4608]{2,1,0:T(2,128)(2,1)}), bf16[128,1,4608]{2,1,0:T(2,128)(2,1)}) %all-gather.20.cloned.1.call-update) | async-done | bytes 1179664 | tf_op jit(solution)/shard_map/all_gather | solution.py:117
  314.5 8.2 reduce.11
  322.6 2.0 reshape.294
  324.6 291.9 %all-gather.12.cloned.1.call-done = bf16[1179648]{0:T(1024)(128)(2,1)} async-done(((bf16[9216]{0:T(1024)(128)(2,1)}), bf16[1179648]{0:T(1024)(128)(2,1)}) %all-gather.12.cloned.1.call-update) | async-done | bytes 2359312 | tf_op jit(solution)/shard_map/all_gather | solution.py:112
  616.6 4.2 reshape.287
  621.7 307.3 %all-gather.18.cloned.1.call-done = bf16[128,1,13824]{2,1,0:T(2,128)(2,1)} async-done(((bf16[1,1,13824]{2,1,0:T(2,128)(2,1)}), bf16[128,1,13824]{2,1,0:T(2,128)(2,1)}) %all-gather.18.cloned.1.call-update) | async-done | bytes 3538960 | tf_op jit(solution)/shard_map/all_gather | solution.py:116
  929.1 71.1 %reduce.10 = bf16[128,13824]{1,0:T(8,128)(2,1)} reduce(bf16[128,1,13824]{2,1,0:T(2,128)(2,1)} %all-gather.18.cloned.1.call-done, bf16[]{:T(256)} %constant.122), dimensions={1}, to_apply=%all-gather.2.reduce_sub_computation | reduce | bytes 7077890 | tf_op jit(solution)/shard_map/all_gather | solution.py:116
  1000.2 7.2 reshape.288
  1007.5 2.7 convolution_convert_fusion
  1010.3 6.7 all-gather.4
  1019.0 7.7 all-gather.3
  1034.7 202.9 %all-gather.14.cloned.1.call-done = bf16[2359296]{0:T(1024)(128)(2,1)} async-done(((bf16[18432]{0:T(1024)(128)(2,1)}), bf16[2359296]{0:T(1024)(128)(2,1)}) %all-gather.14.cloned.1.call-update) | async-done | bytes 4718608 | tf_op jit(solution)/shard_map/all_gather | solution.py:121
  1237.6 8.2 reshape.295
  1245.8 4.4 convolution_add_fusion
  1250.2 298.2 %all-gather.16.cloned.1.call-done = bf16[2359296]{0:T(1024)(128)(2,1)} async-done(((bf16[18432]{0:T(1024)(128)(2,1)}), bf16[2359296]{0:T(1024)(128)(2,1)}) %all-gather.16.cloned.1.call-update) | async-done | bytes 4718608 | tf_op jit(solution)/shard_map/all_gather | solution.py:123
  1548.4 9.2 reshape.296
  1557.7 5.4 convert_reduce_fusion
  1563.0 2.3 multiply_reduce_fusion.2
  1570.1 2.6 convolution_convert_fusion.2
  1574.1 5.2 fusion.25
  1585.7 10.9 reshape.303
  1598.2 5.8 copy.62
  1604.8 28.3 %all-reduce.32.cloned.1.call-done = (bf16[1,258,768]{1,2,0:T(8,128)(2,1)}, bf16[1,258,768]{1,2,0:T(8,128)(2,1)}) async-done(((bf16[1,258,768]{1,2,0:T(8,128)(2,1)}, bf16[1,258,768]{1,2,0:T(8,128)(2,1)}), (bf16[1,258,768]{1,2,0:T(8,128)(2,1)}, bf16[1,258,768]{1,2,0:T(8,128)(2,1)})) %all-reduce.32.cloned.1.call-update) | async-done | bytes 792592
  1635.6 3.4 multiply_reduce_fusion.3
  1639.1 4.2 fusion.18
  1643.5 3.1 fusion.21
  1646.6 5.7 reshape.299
  1652.3 7.9 reshape.300
  1661.0 4.6 fusion.17
  1665.6 67.3 %all-reduce.23 = (f32[768]{0:T(1024)S(1)}, f32[768]{0:T(1024)S(1)}, f32[768]{0:T(1024)S(1)}, f32[768]{0:T(1024)S(1)}, f32[768]{0:T(1024)S(1)}, /*index=5*/f32[76...) all-reduce(f32[768]{0:T(1024)S(1)} %get-tuple-element.49, ...), channel_id=7, replica_groups=mesh['dp'=64,'seq'=2] {'dp','seq'}, use_global_device_ids=true, to_apply=%region_17.18.clone | all-reduce | flops 8448 | bytes 67584
  1739.3 214.6 %all-reduce.30.cloned.1.call-done = (f32[1179648]{0:T(1024)}, f32[1769472]{0:T(1024)}, f32[589824]{0:T(1024)}, f32[2359296]{0:T(1024)}, f32[2359296]{0:T(1024)}) async-done(((f32[1179648]{0:T(1024)}, f32[1769472]{0:T(1024)}, f32[589824]{0:T(1024)}, f32[2359296]{0:T(1024)}, f32[2359296]{0:T(1024)}), (f32[1179648]{0:T(1024)}, f32[1769472]{0:T(1024)}, f32[589824]{0:T(1024)}, f32[2359296]{0:T(1024)}, ...) | async-done | bytes 33030160
  (186 shorter events, 58.0 us)
Async XLA Ops:
  7.2 307.3 %all-gather.20.cloned.1.call-start = ((), (), s32[]{:S(2)}) async-start(), calls=%async_computation.4 | async-start | bytes 2377728 | tf_op jit(solution)/shard_map/all_gather | solution.py:117
  8.6 608.0 %all-gather.12.cloned.1.call-start = ((), (), s32[]{:S(2)}) async-start(), calls=%async_computation | async-start | bytes 2377728 | tf_op jit(solution)/shard_map/all_gather | solution.py:112
  9.3 919.7 %all-gather.18.cloned.1.call-start = ((), (), s32[]{:S(2)}) async-start(), calls=%async_computation.3 | async-start | bytes 7133184 | tf_op jit(solution)/shard_map/all_gather | solution.py:116
  10.8 1226.8 %all-gather.14.cloned.1.call-start = ((), (), s32[]{:S(2)}) async-start(), calls=%async_computation.1 | async-start | bytes 4755456 | tf_op jit(solution)/shard_map/all_gather | solution.py:121
  11.4 1537.0 %all-gather.16.cloned.1.call-start = ((), (), s32[]{:S(2)}) async-start(), calls=%async_computation.2 | async-start | bytes 4755456 | tf_op jit(solution)/shard_map/all_gather | solution.py:123
  12.0 1621.1 %all-reduce.32.cloned.1.call-start = ((), (), s32[]{:S(2)}) async-start(), calls=%async_computation.6 | async-start | bytes 2359296
  89.2 918.2 %copy-start.25 = (f32[768]{0:T(1024)}, f32[768]{0:T(1024)S(1)}, u32[]{:S(2)}) copy-start(f32[768]{0:T(1024)S(1)} %convert_element_type.177) | copy-start | bytes 9220
  89.3 918.2 %copy-start.27 = (f32[768]{0:T(1024)}, f32[768]{0:T(1024)S(1)}, u32[]{:S(2)}) copy-start(f32[768]{0:T(1024)S(1)} %convert_element_type.178) | copy-start | bytes 9220
  89.3 1156.5 %copy-start.29 = (f32[768]{0:T(1024)}, f32[768]{0:T(1024)S(1)}, u32[]{:S(2)}) copy-start(f32[768]{0:T(1024)S(1)} %convert_element_type.188) | copy-start | bytes 9220
  324.6 296.2 %copy-start.20 = (bf16[1,129,768]{2,1,0:T(8,128)(2,1)S(1)}, bf16[1,129,768]{2,1,0:T(8,128)(2,1)}, u32[]{:S(2)}) copy-start(bf16[1,129,768]{2,1,0:T(8,128)(2,1)} %param.21) | copy-start | bytes 594436
  324.6 296.2 %copy-start.22 = (bf16[1,129,768]{2,1,0:T(8,128)(2,1)S(1)}, bf16[1,129,768]{2,1,0:T(8,128)(2,1)}, u32[]{:S(2)}) copy-start(bf16[1,129,768]{2,1,0:T(8,128)(2,1)} %param.20) | copy-start | bytes 594436
  620.8 379.4 %copy-start.1 = (bf16[1536,768]{1,0:T(8,128)(2,1)}, bf16[1536,768]{1,0:T(8,128)(2,1)S(1)}, u32[]{:S(2)}) copy-start(bf16[1536,768]{1,0:T(8,128)(2,1)S(1)} %reshape.287) | copy-start | bytes 7077892
  621.5 386.0 %copy-start.34 = (f32[129]{0:T(256)}, f32[129]{0:T(256)S(1)}, u32[]{:S(2)}) copy-start(f32[129]{0:T(256)S(1)} %broadcast_multiply_fusion.5) | copy-start | bytes 1552
  621.7 385.8 %copy-start.39 = (f32[129]{0:T(256)}, f32[129]{0:T(256)S(1)}, u32[]{:S(2)}) copy-start(f32[129]{0:T(256)S(1)} %add_rsqrt_fusion.1) | copy-start | bytes 1552
  1019.0 11.9 copy-start.12
  1033.8 212.0 %copy-start.31 = (f32[129]{0:T(256)}, f32[129]{0:T(256)S(1)}, u32[]{:S(2)}) copy-start(f32[129]{0:T(256)S(1)} %broadcast_multiply_fusion.4) | copy-start | bytes 1552
  1034.0 211.8 %copy-start.36 = (f32[129]{0:T(256)}, f32[129]{0:T(256)S(1)}, u32[]{:S(2)}) copy-start(f32[129]{0:T(256)S(1)} %add_rsqrt_fusion) | copy-start | bytes 1552
  1250.2 307.4 %copy-start.19 = (bf16[1,129,768]{2,1,0:T(8,128)(2,1)S(1)}, bf16[1,129,768]{2,1,0:T(8,128)(2,1)}, u32[]{:S(2)}) copy-start(bf16[1,129,768]{2,1,0:T(8,128)(2,1)} %param.22) | copy-start | bytes 594436
  1557.6 5.4 copy-start
  1557.6 5.4 copy-start.32
  1557.6 5.4 copy-start.37
  1582.5 371.4 %all-reduce.30.cloned.1.call-start = ((), (), s32[]{:S(2)}) async-start(), calls=%async_computation.5 | async-start | bytes 66060288
  1585.7 10.9 copy-start.15
  1585.7 10.9 copy-start.30
  1585.7 10.9 copy-start.33
  1585.7 10.9 copy-start.38
  1598.2 5.9 copy-start.5
  1598.2 5.9 copy-start.10
  1604.0 31.5 %copy-start.26 = (f32[768]{0:T(1024)S(1)}, f32[768]{0:T(1024)}, u32[]{:S(2)}) copy-start(f32[768]{0:T(1024)} %copy-done.25) | copy-start | bytes 9220
  1604.0 31.5 %copy-start.35 = (f32[129]{0:T(256)S(1)}, f32[129]{0:T(256)}, u32[]{:S(2)}) copy-start(f32[129]{0:T(256)} %copy-done.34) | copy-start | bytes 1552
  1604.1 31.5 %copy-start.40 = (f32[129]{0:T(256)S(1)}, f32[129]{0:T(256)}, u32[]{:S(2)}) copy-start(f32[129]{0:T(256)} %copy-done.39) | copy-start | bytes 1552
  1661.0 76.6 %copy-start.2 = (bf16[1536,768]{1,0:T(8,128)(2,1)S(1)}, bf16[1536,768]{1,0:T(8,128)(2,1)}, u32[]{:S(2)}) copy-start(bf16[1536,768]{1,0:T(8,128)(2,1)} %copy-done.1) | copy-start | bytes 7077892
  (22 other events, 64.8 us)
Sparse Core Ops, SparseCore 0:
  10.3 304.1 all-gather.19
  316.1 300.3 all-gather.11
  618.9 310.1 all-gather.17
  930.6 306.9 all-gather.13
  1239.1 309.2 all-gather.15
  1582.6 50.4 all-reduce.31
  1660.4 293.4 all-reduce.29
where the time goes:
time: 1980 us; the launch traced here: 1970 us
  waiting for transfers between devices  1560 us (79%)
  blocking collectives  151 us (8%)
  local copies, waits for them, and re-layouts  97.9 us (5%)
  other arithmetic  85.9 us (4%)
  matrix products  50.7 us (3%)
    all_gather x1, waiting for transfers between devices, per_device(): lax.all_gather(triple_weight, ('dp', 'seq'), axis=0, tiled=True)  307 us
    all_gather x1, waiting for transfers between devices, per_device(): lax.all_gather(contract_weight, ('dp', 'seq'), axis=0, tiled=True)  298 us
    all_gather x1, waiting for transfers between devices, per_device(): lax.all_gather(skip_weight, ('dp', 'seq'), axis=0, tiled=True)  292 us
    unnamed x9, waiting for transfers between devices  245 us
    all_gather x1, waiting for transfers between devices, per_device(): lax.all_gather(merge_weight, ('dp', 'seq'), axis=0, tiled=True)  219 us
    all_gather x1, waiting for transfers between devices, per_device(): lax.all_gather(expand_weight, ('dp', 'seq'), axis=0, tiled=True)  203 us
    unnamed x2, blocking collectives  136 us
    all_gather x1, other arithmetic, per_device(): lax.all_gather(triple_weight, ('dp', 'seq'), axis=0, tiled=True)  71.1 us
  transfers between devices with their start and end apart: 7, of which 7 were waited for; matrix products, arithmetic and copies ran while one was open for 8% of the time, Pallas kernels for 0%

commit v1 on v0

v1 whole, which is shorter than its diff:
```python
import math

import jax
import jax.numpy as jnp
from jax import lax
from jax.sharding import PartitionSpec as P

D = 768
HEADS = 12
HEAD_DIM = 64
FF = 3072


epsilon = 1e-05


def product(left, right):
    return jnp.dot(left, right, preferred_element_type=jnp.float32)


def left_contract(left, right):
    return lax.dot_general(
        left, right, (((0,), (0,)), ((), ())), preferred_element_type=jnp.float32
    )


def right_contract(left, right):
    return lax.dot_general(
        left, right, (((1,), (1,)), ((), ())), preferred_element_type=jnp.float32
    )


def norm_forward(values, gain, shift):
    mean_value = jnp.mean(values, axis=-1, keepdims=True)
    centered = values - mean_value
    variance = jnp.mean(centered * centered, axis=-1, keepdims=True)
    inverse = lax.rsqrt(variance + epsilon)
    scaled = centered * inverse
    return (scaled * gain + shift, scaled, inverse)


def norm_backward(incoming, scaled, inverse, gain):
    weighted = incoming * gain
    first_mean = jnp.mean(weighted, axis=-1, keepdims=True)
    second_mean = jnp.mean(weighted * scaled, axis=-1, keepdims=True)
    value_grad = inverse * (weighted - first_mean - scaled * second_mean)
    return (value_grad, jnp.sum(incoming * scaled, axis=0), jnp.sum(incoming, axis=0))


def gelu_exact(values):
    return 0.5 * values * (1.0 + lax.erf(values * (1.0 / math.sqrt(2.0))))


def gelu_slope(values):
    cumulative = 0.5 * (1.0 + lax.erf(values * (1.0 / math.sqrt(2.0))))
    density = jnp.exp(-0.5 * values * values) * (1.0 / math.sqrt(2.0 * math.pi))
    return cumulative + values * density


def pick_table(indices, table):
    match = indices[:, None] == jnp.arange(table.shape[0], dtype=jnp.int32)[None, :]
    return jnp.sum(jnp.where(match, table[None, :], 0.0), axis=1)


HALF = D // 2
PLANE = ("y", "x")
COLUMN = ("h", "c", "l")
ROWS = (12, 6, 6, 6, 6, 6, 6, 6, 6, 24, 4)
VECTORS = (6, 6, 6, 6, 6, 6, 24, 6)


def swap(block, axis):
    return lax.ppermute(block, axis, [(0, 1), (1, 0)])


def cut(block, axis):
    at, parts = 0, []
    for rows in ROWS:
        size = rows if axis == 1 else 8 * rows
        parts.append(lax.slice_in_dim(block, at, at + size, axis=axis))
        at += size
    return parts


def gather_all(weights, vectors):
    skip, triple, merge, expand, contract = weights
    row = jnp.pad(jnp.concatenate(vectors)[None, :], ((0, ROWS[10] - 1), (0, HALF - sum(VECTORS))))

    def half(side):
        columns = lambda block: block[:, side * HALF : (side + 1) * HALF]
        pieces = [columns(skip)]
        pieces += [columns(triple[:, k * D : (k + 1) * D]) for k in range(3)]
        pieces += [columns(merge)]
        pieces += [expand[:, (4 * side + k) * HALF : (4 * side + k + 1) * HALF] for k in range(4)]
        pieces += [columns(contract), row]
        return jnp.concatenate(pieces, axis=0)

    packed = jnp.stack([half(0), half(1)])
    to_all = jnp.broadcast_to(packed[None, :, None], (2, 2, 2) + packed.shape[1:]).reshape((8,) + packed.shape[1:])
    column = lax.all_to_all(to_all, COLUMN, 0, 0, tiled=True)
    group = jnp.concatenate([p.reshape(-1, HALF) for p in cut(column, 1)], axis=0)
    own = lax.all_gather(group, PLANE, axis=0, tiled=False).reshape((16,) + group.shape)
    other = swap(own, "c")
    core = lax.axis_index("c")
    first = cut2(jnp.where(core == 0, own, other))
    second = cut2(jnp.where(core == 0, other, own))
    pair = lambda k: jnp.concatenate([first[k], second[k]], axis=1)
    flat = first[10].reshape(128, ROWS[10], HALF)[:, 0]
    spots, at = [], 0
    for size in VECTORS:
        spots.append(flat[:, at : at + size].reshape(-1))
        at += size
    triple_mat = jnp.concatenate([pair(1), pair(2), pair(3)], axis=1)
    expand_mat = jnp.concatenate([first[k] for k in range(5, 9)] + [second[k] for k in range(5, 9)], axis=1)
    return (pair(0), triple_mat, pair(4), expand_mat, pair(9)), spots


def cut2(block):
    at, parts = 0, []
    for rows in ROWS:
        parts.append(block[:, at : at + 8 * rows].reshape(-1, HALF))
        at += 8 * rows
    return parts


def scatter_all(grads, vector_grads):
    skip, triple, merge, expand, contract = grads
    rows = [v.reshape(128, -1) for v in vector_grads]
    flat = jnp.pad(jnp.concatenate(rows, axis=1)[:, None], ((0, 0), (0, ROWS[10] - 1), (0, HALF - sum(VECTORS))))

    def half(side):
        columns = lambda block: block[:, side * HALF : (side + 1) * HALF]
        pieces = [columns(skip)]
        pieces += [columns(triple[:, k * D : (k + 1) * D]) for k in range(3)]
        pieces += [columns(merge)]
        pieces += [expand[:, (4 * side + k) * HALF : (4 * side + k + 1) * HALF] for k in range(4)]
        pieces += [columns(contract), flat if side == 0 else jnp.zeros_like(flat)]
        return jnp.concatenate([p.reshape(16, -1, HALF) for p in pieces], axis=1).astype(jnp.bfloat16)

    core = lax.axis_index("c")
    low, high = half(0), half(1)
    own = jnp.where(core == 0, low, high)
    sent = jnp.where(core == 0, high, low)
    chip = (own.astype(jnp.float32) + swap(sent, "c").astype(jnp.float32)).astype(jnp.bfloat16)
    plane = lax.psum_scatter(chip.reshape(-1, HALF), PLANE, scatter_dimension=0, tiled=True)
    column = jnp.concatenate([p.reshape(2, 2, 2, -1, HALF) for p in cut(plane, 0)], axis=3)
    column = column.transpose(0, 2, 1, 3, 4).reshape((4, 2) + column.shape[3:])
    parts = lax.all_to_all(column, ("h", "l"), 0, 0, tiled=True)
    total = jnp.sum(parts.astype(jnp.float32), axis=0)
    mine = jnp.where(core == 0, total[0], total[1])
    theirs = swap(jnp.where(core == 0, total[1], total[0]), "c")
    low = jnp.where(core == 0, mine, theirs)
    high = jnp.where(core == 0, theirs, mine)
    firsts, seconds, at = [], [], 0
    for size in ROWS:
        firsts.append(low[at : at + size])
        seconds.append(high[at : at + size])
        at += size
    pair = lambda k: jnp.concatenate([firsts[k], seconds[k]], axis=1)
    triple_out = jnp.concatenate([pair(1), pair(2), pair(3)], axis=1)
    expand_out = jnp.concatenate(firsts[5:9] + seconds[5:9], axis=1)
    weights = [p.reshape(-1) for p in (pair(0), triple_out, pair(4), expand_out, pair(9))]
    spots, at = [], 0
    for size in VECTORS:
        spots.append(firsts[10][0, at : at + size])
        at += size
    return weights, spots


def per_device(
    inputs,
    skipped,
    cotangent,
    timestep,
    class_ids,
    time_weight,
    class_weight,
    skip_weight,
    skip_bias,
    first_gain,
    first_shift,
    triple_weight,
    merge_weight,
    merge_bias,
    second_gain,
    second_shift,
    expand_weight,
    expand_bias,
    contract_weight,
    contract_bias,
):
    (skip_mat, triple_mat, merge_mat, expand_mat, contract_mat), spots = gather_all(
        (
            skip_weight.reshape(-1, D),
            triple_weight.reshape(-1, 3 * D),
            merge_weight.reshape(-1, D),
            expand_weight.reshape(-1, FF),
            contract_weight.reshape(-1, D),
        ),
        (skip_bias, first_gain, first_shift, merge_bias, second_gain, second_shift, expand_bias, contract_bias),
    )
    skip_add, first_scale, first_move, merge_add, second_scale, second_move, expand_add, contract_add = spots
    images, half_len = (inputs.shape[0], inputs.shape[1])
    tok_rows = images * half_len
    score_scale = 1.0 / math.sqrt(HEAD_DIM)
    joined = jnp.concatenate([inputs.reshape(tok_rows, D), skipped.reshape(tok_rows, D)], axis=1)
    united = product(joined, skip_mat) + skip_add.astype(jnp.float32)
    normed, first_hat, first_inv = norm_forward(
        united, first_scale.astype(jnp.float32), first_move.astype(jnp.float32)
    )
    normed_low = normed.astype(jnp.bfloat16)
    triple = product(normed_low, triple_mat).astype(jnp.bfloat16)
    query = triple[:, :D].reshape(images, half_len, HEADS, HEAD_DIM)
    pair_all = triple[:, D:].reshape(images, half_len, 2 * D)
    pair_all = jnp.concatenate([pair_all, swap(pair_all, "l")], axis=1)
    key_all, value_all = pair_all[:, :, :D], pair_all[:, :, D:]
    seq_len = key_all.shape[1]
    key_heads = key_all.reshape(images, seq_len, HEADS, HEAD_DIM)
    value_heads = value_all.reshape(images, seq_len, HEADS, HEAD_DIM)
    scores = (
        jnp.einsum("iqhd,ikhd->ihqk", query, key_heads, preferred_element_type=jnp.float32)
        * score_scale
    )
    largest = jnp.max(scores, axis=-1, keepdims=True)
    powered = jnp.exp(scores - largest)
    totals = jnp.sum(powered, axis=-1, keepdims=True)
    log_total = largest + jnp.log(totals)
    attention = (powered / totals).astype(jnp.bfloat16)
    mixed_heads = jnp.einsum(
        "ihqk,ikhd->iqhd", attention, value_heads, preferred_element_type=jnp.float32
    )
    mixed_low = mixed_heads.reshape(tok_rows, D).astype(jnp.bfloat16)
    middle = united + product(mixed_low, merge_mat) + merge_add.astype(jnp.float32)
    normed_two, second_hat, second_inv = norm_forward(
        middle, second_scale.astype(jnp.float32), second_move.astype(jnp.float32)
    )
    normed_two_low = normed_two.astype(jnp.bfloat16)
    before = product(normed_two_low, expand_mat) + expand_add.astype(jnp.float32)
    active = gelu_exact(before).astype(jnp.bfloat16)
    output = middle + product(active, contract_mat) + contract_add.astype(jnp.float32)
    image_scale = pick_table(timestep, time_weight) * pick_table(class_ids, class_weight)
    out_grad = (cotangent.astype(jnp.float32) * image_scale[:, None, None]).reshape(tok_rows, D)
    after_low = out_grad.astype(jnp.bfloat16)
    contract_bias_grad = jnp.sum(after_low.astype(jnp.float32), axis=0)
    contract_weight_grad = left_contract(active, after_low)
    before_low = (right_contract(after_low, contract_mat) * gelu_slope(before)).astype(jnp.bfloat16)
    expand_bias_grad = jnp.sum(before_low.astype(jnp.float32), axis=0)
    expand_weight_grad = left_contract(normed_two_low, before_low)
    back_two, second_gain_grad, second_shift_grad = norm_backward(
        right_contract(before_low, expand_mat),
        second_hat,
        second_inv,
        second_scale.astype(jnp.float32),
    )
    middle_grad = out_grad + back_two
    attend_low = middle_grad.astype(jnp.bfloat16)
    merge_bias_grad = jnp.sum(attend_low.astype(jnp.float32), axis=0)
    merge_weight_grad = left_contract(mixed_low, attend_low)
    mixed_grad = right_contract(attend_low, merge_mat).astype(jnp.bfloat16)
    mixed_grad = mixed_grad.reshape(images, half_len, HEADS, HEAD_DIM)
    scores_again = (
        jnp.einsum("iqhd,ikhd->ihqk", query, key_heads, preferred_element_type=jnp.float32)
        * score_scale
    )
    soft_again = jnp.exp(scores_again - log_total)
    soft_low = soft_again.astype(jnp.bfloat16)
    soft_grad = jnp.einsum(
        "iqhd,ikhd->ihqk", mixed_grad, value_heads, preferred_element_type=jnp.float32
    )
    inner_sum = jnp.sum(soft_again * soft_grad, axis=-1, keepdims=True)
    scores_grad = (soft_again * (soft_grad - inner_sum)).astype(jnp.bfloat16)
    query_grad = (
        jnp.einsum("ihqk,ikhd->iqhd", scores_grad, key_heads, preferred_element_type=jnp.float32)
        * score_scale
    )
    query_grad = query_grad.reshape(tok_rows, D).astype(jnp.bfloat16)
    key_part = (
        jnp.einsum("ihqk,iqhd->ikhd", scores_grad, query, preferred_element_type=jnp.float32)
        * score_scale
    )
    value_part = jnp.einsum(
        "ihqk,iqhd->ikhd", soft_low, mixed_grad, preferred_element_type=jnp.float32
    )
    pair_part = jnp.concatenate(
        [key_part.reshape(images, seq_len, D), value_part.reshape(images, seq_len, D)], axis=2
    )
    came = swap(pair_part[:, half_len:].astype(jnp.bfloat16), "l")
    pair_grad = pair_part[:, :half_len] + came.astype(jnp.float32)
    triple_grad = jnp.concatenate(
        [query_grad, pair_grad.reshape(tok_rows, 2 * D).astype(jnp.bfloat16)], axis=1
    )
    triple_weight_grad = left_contract(normed_low, triple_grad)
    back_one, first_gain_grad, first_shift_grad = norm_backward(
        right_contract(triple_grad, triple_mat),
        first_hat,
        first_inv,
        first_scale.astype(jnp.float32),
    )
    united_low = (middle_grad + back_one).astype(jnp.bfloat16)
    skip_bias_grad = jnp.sum(united_low.astype(jnp.float32), axis=0)
    skip_weight_grad = left_contract(joined, united_low)
    joined_grad = right_contract(united_low, skip_mat)
    input_grad = joined_grad[:, :D].reshape(images, half_len, D).astype(jnp.bfloat16)
    skip_grad = joined_grad[:, D:].reshape(images, half_len, D).astype(jnp.bfloat16)
    weight_grads, spot_grads = scatter_all(
        (skip_weight_grad, triple_weight_grad, merge_weight_grad, expand_weight_grad, contract_weight_grad),
        (
            skip_bias_grad,
            first_gain_grad,
            first_shift_grad,
            merge_bias_grad,
            second_gain_grad,
            second_shift_grad,
            expand_bias_grad,
            contract_bias_grad,
        ),
    )
    owned = (
        weight_grads[0],
        spot_grads[0],
        spot_grads[1],
        spot_grads[2],
        weight_grads[1],
        weight_grads[2],
        spot_grads[3],
        spot_grads[4],
        spot_grads[5],
        weight_grads[3],
        spot_grads[6],
        weight_grads[4],
        spot_grads[7],
    )
    block_output = output.reshape(images, half_len, D).astype(jnp.bfloat16)
    return (block_output, input_grad, skip_grad) + tuple(owned)


def solution(mesh):
    fine = jax.sharding.Mesh(mesh.devices.reshape(4, 4, 2, 2, 2), ("y", "x", "h", "c", "l"))
    images = ("y", "x", "h", "c")
    everything = images + ("l",)
    tokens, shard = P(images, "l", None), P(everything)
    return jax.shard_map(
        per_device,
        mesh=fine,
        in_specs=(tokens,) * 3 + (P(images),) * 2 + (P(),) * 2 + (shard,) * 13,
        out_specs=(tokens,) * 3 + (shard,) * 13,
        check_vma=False,
    )
```

time: 1980 us -> 399 us (0.20)
  waiting for transfers between devices: 1560 us -> 180 us
  blocking collectives: 151 us -> 16.7 us
  other arithmetic: 85.9 us -> 26.1 us
    all_gather x5 -> x1, waiting for transfers between devices: 1320 us -> 71.2 us  [gather_all(): lax.all_gather(group, PLANE, axis=0, tiled=False)]
    unnamed x9 -> x2, waiting for transfers between devices: 245 us -> 0.03 us
    unnamed x2 -> x0, blocking collectives: 136 us -> none
    reduce_scatter x0 -> x1, waiting for transfers between devices: none -> 83.3 us  [scatter_all(): lax.psum_scatter(chip.reshape(-1, HALF), PLANE, scatter_dimension=0, tile...]
    all_gather x2 -> x0, other arithmetic: 79.3 us -> none  [the longest x1 71.1 us: per_device(): lax.all_gather(triple_weight, ('dp', 'seq'), axis=0, tiled=True)]
    reshape x10 -> x43, local copies, waits for them, and re-layouts: 57.1 us -> 18.3 us  [the longest x8 6.08 us: scatter_all(): rows = [v.reshape(128, -1) for v in vector_grads]]
    slice x0 -> x32, local copies, waits for them, and re-layouts: none -> 35.5 us  [the longest x7 18 us: cut2(): parts.append(block[:, at:at + 8 * rows].reshape(-1, HALF))]
    ppermute x0 -> x5, waiting for transfers between devices: none -> 23.1 us  [swap(): return lax.ppermute(block, axis, [(0, 1), (1, 0)])]
  transfers between devices with their start and end apart: 7 -> 8, of which waited for: 7 -> 6; matrix products, arithmetic and copies ran while one was open for 8% -> 10% of each run, Pallas kernels for 0% -> 0%
where the time goes in v1:
time: 399 us; the launch traced here: 398 us
  waiting for transfers between devices  180 us (45%)
  local copies, waits for them, and re-layouts  99.4 us (25%)
  matrix products  46 us (12%)
  other arithmetic  26.1 us (7%)
  between operations  18.2 us (5%)
  blocking collectives  16.7 us (4%)
  starting transfers between devices  11.1 us (3%)
    reduce_scatter x1, waiting for transfers between devices, scatter_all(): lax.psum_scatter(chip.reshape(-1, HALF), PLANE, scatter_dimension=0, tile...  83.3 us
    all_gather x1, waiting for transfers between devices, gather_all(): lax.all_gather(group, PLANE, axis=0, tiled=False)  71.2 us
    unnamed x213, local copies, waits for them, and re-layouts  23.1 us
    ppermute x5, waiting for transfers between devices, swap(): return lax.ppermute(block, axis, [(0, 1), (1, 0)])  23.1 us
    slice x7, local copies, waits for them, and re-layouts, cut2(): parts.append(block[:, at:at + 8 * rows].reshape(-1, HALF))  18 us
    all_to_all x1, blocking collectives, gather_all(): column = lax.all_to_all(to_all, COLUMN, 0, 0, tiled=True)  16.7 us
    dot_general x5, matrix products, left_contract(): lax.dot_general(left, right, (((0,), (0,)), ((), ())), preferred_element_...  13.3 us
    dot_general x5, matrix products, right_contract(): lax.dot_general(left, right, (((1,), (1,)), ((), ())), preferred_element_...  11.4 us
  transfers between devices with their start and end apart: 8, of which 6 were waited for; matrix products, arithmetic and copies ran while one was open for 10% of the time, Pallas kernels for 0%

profile of v1, /device:TPU:1, one launch (start us, length us, event | category | flops | bytes accessed | tf_op | source)
XLA Modules:
  0.0 397.8 jit_solution(10950036587514414678)
XLA Ops:
  11.2 5.4 %concatenate.70 = bf16[66]{0:T(256)(128)(2,1)S(1)} concatenate(bf16[6]{0:T(256)(128)(2,1)} %param.28, bf16[6]{0:T(256)(128)(2,1)} %param.29, bf16[6]{0:T(256)(128)(2,1)} %param.30, bf16[6]{0:T(256)(128)(2,1)} %param.33, bf16[6]{0:T(256)(128)(2,1)} %param.34, bf16[6]{0:T(256)(128)(2,1)} %param.35, bf16[24]{0:T(256)(128)(2,1)} %param.37, bf16[6]{0:T(256)(128)(2,1)} %param.39), dimensions={0} | concatenate | bytes 264 | tf_op jit(solution)/shard_map/concatenate | solution.py:87
  18.2 16.7 %all_to_all.10 = bf16[8,88,384]{2,1,0:T(8,128)(2,1)S(1)} all-to-all(bf16[8,88,384]{2,1,0:T(8,128)(2,1)S(1)} %bitcast.197), channel_id=1, replica_groups=mesh['y'=4,'x'=4,'h'=2,'c'=2,'l'=2] {'h','c','l'}, dimensions={0} | all-to-all | bytes 1081344 | tf_op jit(solution)/shard_map/all_to_all | solution.py:100
  36.4 71.2 %all-gather.3.cloned.1.call-done = bf16[11264,384]{1,0:T(8,128)(2,1)} async-done(((bf16[704,384]{1,0:T(8,128)(2,1)}), bf16[11264,384]{1,0:T(8,128)(2,1)}) %all-gather.3.cloned.1.call-update) | async-done | bytes 8650768 | tf_op jit(solution)/shard_map/all_gather | solution.py:102
  112.1 9.7 %collective-permute-done = bf16[16,704,384]{2,1,0:T(8,128)(2,1)} collective-permute-done((bf16[16,704,384]{2,1,0:T(8,128)(2,1)}, bf16[16,704,384]{2,1,0:T(8,128)(2,1)}, u32[]{:S(2)}, u32[]{:S(2)}) %collective-permute-start) | collective-permute-done | bytes 8650784 | tf_op jit(solution)/shard_map/ppermute | solution.py:73
  121.8 9.5 %broadcast_select_fusion.2 = (bf16[16,704,384]{2,1,0:T(8,128)(2,1)S(1)}, bf16[16,704,384]{2,1,0:T(8,128)(2,1)}) fusion(bf16[16,704,384]{2,1,0:T(8,128)(2,1)} %bitcast.149, bf16[16,704,384]{2,1,0:T(8,128)(2,1)} %collective-permute-done, pred[]{:T(512)S(6)} %eq.32), kind=kLoop, calls=%fused_computation.3 | loop fusion | flops 8650752 | bytes 34603008 | tf_op jit(solution)/shard_map/jit(_where)/select_n | solution.py:105
  131.4 3.4 copy-done
  135.9 2.4 slice.609
  138.3 2.4 slice.610
  140.7 4.3 %fusion.44 = (bf16[16,48,384]{2,1,0:T(8,128)(2,1)S(1)}, bf16[16,48,384]{2,1,0:T(8,128)(2,1)S(1)}, bf16[16,48,384]{2,1,0:T(8,128)(2,1)S(1)}, bf16[16,48,384]{2,1,...) fusion(bf16[16,704,384]{2,1,0:T(8,128)(2,1)} %get-tuple-element.29), kind=kLoop, calls=%fused_computation.200 | loop fusion | bytes 9437184 | tf_op jit(solution)/shard_map/slice | solution.py:121
  146.4 2.2 fusion.45
  149.1 2.5 fusion.58
  161.3 3.3 slice.641
  164.6 3.4 slice.640
  176.2 1.9 multiply_reduce_fusion.1
  181.8 3.5 convolution_add_fusion
  185.5 2.7 fusion.60
  188.2 5.1 %multiply_reduce_fusion.2 = (bf16[768]{0:T(1024)(128)(2,1)}, f32[129]{0:T(256)S(1)}, f32[129]{0:T(256)S(1)}, bf16[768]{0:T(1024)(128)(2,1)}, f32[129,768]{1,0:T(8,128)S(1)}) fusion(f32[129,768]{1,0:T(8,128)S(1)} %get-tuple-element.138, f32[129]{0:T(256)S(1)} %add_rsqrt_fusion, f32[129]{0:T(256)S(1)} %broadcast_multiply_fusion.4, f32[768]{0:T(1024)S(1)} %reshape.662, ...), kind=kOutput, calls=%fused_computation.66 | convolution fusion | flops 609588224 | bytes 6311952 | tf_op jit(solution)/shard_map/dot_general | solution.py:28
  196.9 1.9 copy.82
  198.7 2.8 fusion.9
  207.0 3.7 convolution_convert_fusion
  210.7 3.7 convolution_convert_fusion.1
  217.8 5.1 %fusion.46 = (bf16[3072,384]{1,0:T(8,128)(2,1)}, bf16[3072,384]{1,0:T(8,128)(2,1)}) fusion(bf16[3072,768]{1,0:T(8,128)(2,1)} %convolution_convert_fusion), kind=kLoop, calls=%fused_computation.202 | loop fusion | bytes 9437184 | tf_op jit(solution)/shard_map/slice | solution.py:132
  229.0 4.7 %fusion.47 = (bf16[768,384]{1,0:T(8,128)(2,1)}, bf16[768,384]{1,0:T(8,128)(2,1)}, bf16[768,384]{1,0:T(8,128)(2,1)}, bf16[768,384]{1,0:T(8,128)(2,1)}, bf16[768,3...) fusion(bf16[768,3072]{1,0:T(8,128)(2,1)} %convolution_convert_fusion.1), kind=kLoop, calls=%fused_computation.203 | loop fusion | bytes 9437184 | tf_op jit(solution)/shard_map/slice | solution.py:136
  236.4 2.4 convolution_convert_fusion.2
  250.2 2.0 convolution_convert_fusion.4
  261.5 13.2 %collective-permute-done.3 = bf16[16,704,384]{2,1,0:T(8,128)(2,1)S(1)} collective-permute-done((bf16[16,704,384]{2,1,0:T(8,128)(2,1)S(1)}, bf16[16,704,384]{2,1,0:T(8,128)(2,1)S(1)}, u32[]{:S(2)}, u32[]{:S(2)}) %collective-permute-start.3) | collective-permute-done | bytes 8650784 | tf_op jit(solution)/shard_map/ppermute | solution.py:73
  274.7 5.6 %add_convert_fusion = bf16[16,704,384]{2,1,0:T(8,128)(2,1)} fusion(bf16[16,704,384]{2,1,0:T(8,128)(2,1)S(1)} %collective-permute-done.3, bf16[16,704,384]{2,1,0:T(8,128)(2,1)S(1)} %constant_dynamic-update-slice_fusion.25, bf16[16,704,384]{2,1,0:T(8,128)(2,1)S(1)} %broadcast_dynamic-update-slice_fusion, pred[]{:T(512)S(6)} %eq.32), kind=kLoop, calls=%fused_computation | loop fusion | flops 21626880 | bytes 34603008 | tf_op jit(solution)/shard_map/convert_element_type | solution.py:144
  281.3 83.3 %reduce-scatter.2.cloned.1.call-done = bf16[704,384]{1,0:T(8,128)(2,1)} async-done(((bf16[11264,384]{1,0:T(8,128)(2,1)}), bf16[704,384]{1,0:T(8,128)(2,1)}) %reduce-scatter.2.cloned.1.call-update) | async-done | bytes 540688 | tf_op jit(solution)/shard_map/reduce_scatter | solution.py:145
  370.6 4.0 %all-to-all-start.1 = ((bf16[4,2,88,384]{3,2,1,0:T(8,128)(2,1)}), bf16[4,2,88,384]{3,2,1,0:T(8,128)(2,1)S(1)}, u32[]{:S(2)}, u32[]{:S(2)}) async-start(bf16[4,2,88,384]{3,2,1,0:T(8,128)(2,1)} %bitcast.76), calls=%async_computation.2 | async-start | bytes 1081344 | tf_op jit(solution)/shard_map/all_to_all | solution.py:148
  374.6 3.8 fusion.21
  379.3 2.6 all-to-all-done.1
  382.1 3.3 collective-permute-start.4
  (358 shorter events, 87.9 us)
Async XLA Ops:
  7.2 102.4 %copy-start.78 = (f32[1001]{0:T(1024)S(1)}, f32[1001]{0:T(1024)}, u32[]{:S(2)}) copy-start(f32[1001]{0:T(1024)} %param.26) | copy-start | bytes 12016
  7.2 103.0 %copy-start.79 = (f32[1000]{0:T(1024)S(1)}, f32[1000]{0:T(1024)}, u32[]{:S(2)}) copy-start(f32[1000]{0:T(1024)} %param.25) | copy-start | bytes 12004
  7.2 100.4 %all-gather.3.cloned.1.call-start = ((), (), s32[]{:S(2)}) async-start(), calls=%async_computation.4 | async-start | bytes 9191424 | tf_op jit(solution)/shard_map/all_gather | solution.py:102
  36.4 328.2 %reduce-scatter.2.cloned.1.call-start = ((), (), s32[]{:S(2)}) async-start(), calls=%async_computation.3 | async-start | bytes 9191424 | tf_op jit(solution)/shard_map/reduce_scatter | solution.py:145
  107.6 14.2 %collective-permute-start = (bf16[16,704,384]{2,1,0:T(8,128)(2,1)}, bf16[16,704,384]{2,1,0:T(8,128)(2,1)}, u32[]{:S(2)}, u32[]{:S(2)}) collective-permute-start(bf16[16,704,384]{2,1,0:T(8,128)(2,1)} %bitcast.148), channel_id=1, source_target_pairs={{0,2},{2,0},{1,3},{3,1},{4,6},{6,4},{5,7},{7,5},{8,10},{10,8},{9,1... | collective-permute-start | bytes 25952264 | tf_op jit(solution)/shard_map/ppermute | solution.py:73
  140.7 5.7 %copy-start.1 = (bf16[16,704,384]{2,1,0:T(8,128)(2,1)S(1)}, bf16[16,704,384]{2,1,0:T(8,128)(2,1)}, u32[]{:S(2)}) copy-start(bf16[16,704,384]{2,1,0:T(8,128)(2,1)} %copy-done) | copy-start | bytes 25952260
  148.8 4.9 %copy-start.58 = (f32[768]{0:T(1024)}, f32[768]{0:T(1024)S(1)}, u32[]{:S(2)}) copy-start(f32[768]{0:T(1024)S(1)} %reshape.659) | copy-start | bytes 9220
  151.6 83.3 %copy-start.9 = (f32[129,768]{1,0:T(8,128)}, f32[129,768]{1,0:T(8,128)S(1)}, u32[]{:S(2)}) copy-start(f32[129,768]{1,0:T(8,128)S(1)} %get-tuple-element.134) | copy-start | bytes 1188868
  153.8 5.6 %copy-start.33 = (bf16[16,48,384]{2,1,0:T(8,128)(2,1)S(1)}, bf16[16,48,384]{2,1,0:T(8,128)(2,1)}, u32[]{:S(2)}) copy-start(bf16[16,48,384]{2,1,0:T(8,128)(2,1)} %get-tuple-element.38) | copy-start | bytes 1769476
  155.4 17.4 %collective-permute-start.1 = (bf16[1,129,1536]{2,1,0:T(8,128)(2,1)}, bf16[1,129,1536]{2,1,0:T(8,128)(2,1)}, u32[]{:S(2)}, u32[]{:S(2)}) collective-permute-start(bf16[1,129,1536]{2,1,0:T(8,128)(2,1)} %slice_bitcast_fusion), channel_id=1, source_target_pairs={{0,1},{1,0},{2,3},{3,2},{4,5},{5,4},{6,7},{7,6},{8,9},{9,8},{10,11... | collective-permute-start | bytes 1188872 | tf_op jit(solution)/shard_map/ppermute | solution.py:73
  169.9 6.3 %copy-start.18 = (bf16[129,768]{0,1:T(8,128)(2,1)}, bf16[129,768]{0,1:T(8,128)(2,1)S(1)}, u32[]{:S(2)}) copy-start(bf16[129,768]{0,1:T(8,128)(2,1)S(1)} %copy.81) | copy-start | bytes 594436
  181.5 29.1 %copy-start.2 = (f32[129,768]{1,0:T(8,128)}, f32[129,768]{1,0:T(8,128)S(1)}, u32[]{:S(2)}) copy-start(f32[129,768]{1,0:T(8,128)S(1)} %get-tuple-element.138) | copy-start | bytes 1188868
  181.5 11.8 %copy-start.64 = (f32[129]{0:T(256)}, f32[129]{0:T(256)S(1)}, u32[]{:S(2)}) copy-start(f32[129]{0:T(256)S(1)} %broadcast_multiply_fusion.4) | copy-start | bytes 1552
  181.8 11.5 %copy-start.69 = (f32[129]{0:T(256)}, f32[129]{0:T(256)S(1)}, u32[]{:S(2)}) copy-start(f32[129]{0:T(256)S(1)} %add_rsqrt_fusion) | copy-start | bytes 1552
  188.2 5.9 %copy-start.21 = (bf16[129,3072]{1,0:T(8,128)(2,1)}, bf16[129,3072]{1,0:T(8,128)(2,1)S(1)}, u32[]{:S(2)}) copy-start(bf16[129,3072]{1,0:T(8,128)(2,1)S(1)} %get-tuple-element.144) | copy-start | bytes 2377732
  217.2 5.6 %copy-start.14 = (bf16[768,768]{1,0:T(8,128)(2,1)S(1)}, bf16[768,768]{1,0:T(8,128)(2,1)}, u32[]{:S(2)}) copy-start(bf16[768,768]{1,0:T(8,128)(2,1)} %convolution_convert_fusion.6) | copy-start | bytes 3538948
  217.2 6.8 %copy-start.77 = (bf16[3072]{0:T(1024)(128)(2,1)S(1)}, bf16[3072]{0:T(1024)(128)(2,1)}, u32[]{:S(2)}) copy-start(bf16[3072]{0:T(1024)(128)(2,1)} %get-tuple-element.143) | copy-start | bytes 18436
  217.2 7.5 %copy-start.76 = (bf16[768]{0:T(1024)(128)(2,1)S(1)}, bf16[768]{0:T(1024)(128)(2,1)}, u32[]{:S(2)}) copy-start(bf16[768]{0:T(1024)(128)(2,1)} %get-tuple-element.24) | copy-start | bytes 4612
  217.2 8.3 %copy-start.74 = (bf16[768]{0:T(1024)(128)(2,1)S(1)}, bf16[768]{0:T(1024)(128)(2,1)}, u32[]{:S(2)}) copy-start(bf16[768]{0:T(1024)(128)(2,1)} %get-tuple-element.16) | copy-start | bytes 4612
  217.2 9.0 %copy-start.75 = (bf16[768]{0:T(1024)(128)(2,1)S(1)}, bf16[768]{0:T(1024)(128)(2,1)}, u32[]{:S(2)}) copy-start(bf16[768]{0:T(1024)(128)(2,1)} %get-tuple-element.88) | copy-start | bytes 4612
  217.2 9.8 %copy-start.73 = (bf16[768]{0:T(1024)(128)(2,1)S(1)}, bf16[768]{0:T(1024)(128)(2,1)}, u32[]{:S(2)}) copy-start(bf16[768]{0:T(1024)(128)(2,1)} %get-tuple-element.22) | copy-start | bytes 4612
  217.2 16.5 %collective-permute-start.2 = (bf16[1,129,1536]{2,1,0:T(8,128)(2,1)}, bf16[1,129,1536]{2,1,0:T(8,128)(2,1)}, u32[]{:S(2)}, u32[]{:S(2)}) collective-permute-start(bf16[1,129,1536]{2,1,0:T(8,128)(2,1)} %fusion.25), channel_id=1, source_target_pairs={{0,1},{1,0},{2,3},{3,2},{4,5},{5,4},{6,7},{7,6},{8,9},{9,8},{10,11... | collective-permute-start | bytes 1188872 | tf_op jit(solution)/shard_map/ppermute | solution.py:73
  228.9 5.9 %copy-start.50 = (bf16[129,768]{1,0:T(8,128)(2,1)}, bf16[129,768]{1,0:T(8,128)(2,1)S(1)}, u32[]{:S(2)}) copy-start(bf16[129,768]{1,0:T(8,128)(2,1)S(1)} %copy.77) | copy-start | bytes 594436
  229.0 5.9 %copy-start.13 = (bf16[768,2304]{1,0:T(8,128)(2,1)S(1)}, bf16[768,2304]{1,0:T(8,128)(2,1)}, u32[]{:S(2)}) copy-start(bf16[768,2304]{1,0:T(8,128)(2,1)} %copy-done.12) | copy-start | bytes 10616836
  229.0 5.9 %copy-start.59 = (f32[768]{0:T(1024)S(1)}, f32[768]{0:T(1024)}, u32[]{:S(2)}) copy-start(f32[768]{0:T(1024)} %copy-done.58) | copy-start | bytes 9220
  229.0 5.9 %copy-start.68 = (f32[129]{0:T(256)S(1)}, f32[129]{0:T(256)}, u32[]{:S(2)}) copy-start(f32[129]{0:T(256)} %copy-done.67) | copy-start | bytes 1552
  229.0 5.9 %copy-start.72 = (f32[129]{0:T(256)S(1)}, f32[129]{0:T(256)}, u32[]{:S(2)}) copy-start(f32[129]{0:T(256)} %copy-done.71) | copy-start | bytes 1552
  260.3 14.4 %collective-permute-start.3 = (bf16[16,704,384]{2,1,0:T(8,128)(2,1)S(1)}, bf16[16,704,384]{2,1,0:T(8,128)(2,1)S(1)}, u32[]{:S(2)}, u32[]{:S(2)}) collective-permute-start(bf16[16,704,384]{2,1,0:T(8,128)(2,1)S(1)} %broadcast_select_fusion), channel_id=1, source_target_pairs={{0,2},{2,0},{1,3},{3,1},{4,6},{6,4},{5,7},{7,5},{8,10},{10,8},{9,1... | collective-permute-start | bytes 25952264 | tf_op jit(solution)/shard_map/ppermute | solution.py:73
  280.3 94.3 %copy-start.3 = (f32[129,768]{1,0:T(8,128)S(1)}, f32[129,768]{1,0:T(8,128)}, u32[]{:S(2)}) copy-start(f32[129,768]{1,0:T(8,128)} %copy-done.2) | copy-start | bytes 1188868
  280.3 94.3 %copy-start.6 = (f32[129,3072]{1,0:T(8,128)S(1)}, f32[129,3072]{1,0:T(8,128)}, u32[]{:S(2)}) copy-start(f32[129,3072]{1,0:T(8,128)} %copy-done.4) | copy-start | bytes 4755460
  370.6 11.4 %all-to-all-start.1 = ((bf16[4,2,88,384]{3,2,1,0:T(8,128)(2,1)}), bf16[4,2,88,384]{3,2,1,0:T(8,128)(2,1)S(1)}, u32[]{:S(2)}, u32[]{:S(2)}) async-start(bf16[4,2,88,384]{3,2,1,0:T(8,128)(2,1)} %bitcast.76), calls=%async_computation.2 | async-start | bytes 1081344 | tf_op jit(solution)/shard_map/all_to_all | solution.py:148
  382.1 4.3 %collective-permute-start.4 = (f32[88,384]{1,0:T(8,128)S(1)}, f32[88,384]{1,0:T(8,128)S(1)}, u32[]{:S(2)}, u32[]{:S(2)}) collective-permute-start(f32[88,384]{1,0:T(8,128)S(1)} %select_bitcast_fusion), channel_id=1, source_target_pairs={{0,2},{2,0},{1,3},{3,1},{4,6},{6,4},{5,7},{7,5},{8,10},{10,8},{9,1... | collective-permute-start | bytes 405512 | tf_op jit(solution)/shard_map/ppermute | solution.py:73
  (56 other events, 145.4 us)
Sparse Core Ops, SparseCore 0:
  36.5 71.1 all-gather.2
  280.4 84.0 reduce-scatter.1

commit v2 on v1

v2 whole, which is shorter than its diff:
```python
import functools
import math

import jax
import jax.numpy as jnp
from jax import lax
from jax.experimental import pallas as pl
from jax.experimental.pallas import tpu as pltpu
from jax.sharding import PartitionSpec as P

D = 768
HEADS = 12
HEAD_DIM = 64
FF = 3072
HALF = D // 2
STRIPS = FF // D
TOKENS = 129
PAD = 144
KEYS = 2 * PAD
PLANES = 16
PLANE = ("y", "x")
COLUMN = ("h", "c", "l")
SKIP, MERGE, SPOTS, TRIPLE = 0, 96, 144, 160
FIRST_ROWS = 304
ONE_ROWS = 160
TWO_ROWS = 144
EXPAND, CONTRACT = 0, 192
SECOND_ROWS = 384
ONE_PACK = (12, 6, 1)
TWO_PACK = (6, 6, 6)
SECOND_PACK = (6, 6, 6, 6, 24)
SPOT_WIDTH = 66
epsilon = 1e-05
score_scale = 1.0 / math.sqrt(HEAD_DIM)
BF, F32 = jnp.bfloat16, jnp.float32
ROOM = 56 * 2**20


def mm(left, right):
    return jnp.dot(left, right, preferred_element_type=F32)


def mm_t(left, right):
    return lax.dot_general(left, right, (((1,), (1,)), ((), ())), preferred_element_type=F32)


def t_mm(left, right):
    return lax.dot_general(left, right, (((0,), (0,)), ((), ())), preferred_element_type=F32)


def order(core, one, two):
    return jnp.where(core == 0, one, two), jnp.where(core == 0, two, one)


def split(core, block):
    return order(core, block[:, :HALF], block[:, HALF:])


def norm_stats(values):
    mean_value = jnp.mean(values, axis=-1, keepdims=True)
    centered = values - mean_value
    variance = jnp.mean(centered * centered, axis=-1, keepdims=True)
    inverse = lax.rsqrt(variance + epsilon)
    return centered * inverse, inverse


def norm_backward(incoming, scaled, inverse, gain):
    weighted = incoming * gain
    first_mean = jnp.mean(weighted, axis=-1, keepdims=True)
    second_mean = jnp.mean(weighted * scaled, axis=-1, keepdims=True)
    value_grad = inverse * (weighted - first_mean - scaled * second_mean)
    return (
        value_grad,
        jnp.sum(incoming * scaled, axis=0, keepdims=True),
        jnp.sum(incoming, axis=0, keepdims=True),
    )


def padded(block):
    return jnp.concatenate([block, jnp.zeros((PAD - TOKENS, block.shape[1]), block.dtype)], axis=0)


def load(pairs, sems):
    copies = [pltpu.make_async_copy(s, d, sems.at[k]) for k, (s, d) in enumerate(pairs)]
    for copy in copies:
        copy.start()
    return copies


def matrix(ref, at, rows):
    return ref[:, at : at + rows, :].reshape(PLANES * rows, HALF)


def spot_masks(width):
    lanes = lax.broadcasted_iota(jnp.int32, (128, D), 0)
    spots = lax.broadcasted_iota(jnp.int32, (128, D), 1)
    return lanes, lax.rem(spots, width), lax.div(spots, width)


def steps_to(place_ref, plane):
    return (plane // 4 - place_ref[1]) & 3, (plane % 4 - place_ref[2]) & 3


def wait(copies):
    for copy in copies:
        copy.wait()


def spots_kernel(first_ref, out_ref, rows_ref, sems):
    wait(load([(first_ref.at[:, SPOTS : SPOTS + 16, :], rows_ref)], sems))
    held = rows_ref[:, :, :128].astype(F32)[:, :8].reshape(128, 128).astype(BF)
    for j in range(7):
        lanes, place, owner = spot_masks(6)
        one_hot = (lanes - 6 * j == place).astype(BF)
        spread = jnp.where(owner == lanes, mm(held, one_hot), 0.0)
        out_ref[j : j + 1, :] = jnp.sum(spread, axis=0, keepdims=True)
    out_ref[7:8, :] = jnp.zeros((1, D), F32)
    lanes, place, owner = spot_masks(24)
    spread = mm(held, (lanes - 42 == place).astype(BF))
    for m in range(STRIPS):
        out_ref[8 + m : 9 + m, :] = jnp.sum(jnp.where(owner + 32 * m == lanes, spread, 0.0), axis=0, keepdims=True)
    out_ref[12:16, :] = jnp.zeros((4, D), F32)


def first_kernel(core_ref, in_ref, skip_ref, own_ref, other_ref, spots_ref, united_ref, normed_ref, query_ref, pair_ref, so, ss, to, ts, sems):
    core = core_ref[0]
    copies = load(
        [
            (own_ref.at[:, SKIP : SKIP + 96, :], so),
            (other_ref.at[:, SKIP : SKIP + 96, :], ss),
            (own_ref.at[:, TRIPLE : TRIPLE + 144, :], to),
            (other_ref.at[:, TRIPLE : TRIPLE + 144, :], ts),
        ],
        sems,
    )
    joined = jnp.concatenate([padded(in_ref[...]), padded(skip_ref[...])], axis=1)
    copies[0].wait()
    one = mm(joined, matrix(so, 0, 96))
    copies[1].wait()
    two = mm(joined, matrix(ss, 0, 96))
    united = jnp.concatenate(order(core, one, two), axis=1) + spots_ref[0:1, :]
    united_ref[...] = united
    scaled, _ = norm_stats(united)
    normed = (scaled * spots_ref[1:2, :] + spots_ref[2:3, :]).astype(BF)
    normed_ref[...] = normed
    copies[2].wait()
    copies[3].wait()
    for k in range(3):
        one = mm(normed, matrix(to, 48 * k, 48))
        two = mm(normed, matrix(ts, 48 * k, 48))
        block = jnp.concatenate(order(core, one, two), axis=1).astype(BF)
        if k == 0:
            query_ref[...] = block
        else:
            pair_ref[:, (k - 1) * D : k * D] = block


def key_mask():
    spots = lax.broadcasted_iota(jnp.int32, (1, KEYS), 1)
    return (spots < TOKENS) | ((spots >= PAD) & (spots < PAD + TOKENS))


def attend_kernel(core_ref, query_ref, pair_ref, came_ref, united_ref, own_ref, other_ref, spots_ref, mixed_ref, middle_ref, normed_ref, total_ref, mo, ms, sems):
    core = core_ref[0]
    copies = load(
        [(own_ref.at[:, MERGE : MERGE + 48, :], mo), (other_ref.at[:, MERGE : MERGE + 48, :], ms)], sems
    )
    mask = key_mask()
    total_ref[...] = jnp.zeros((PAD, 128), F32)
    for pair in range(HEADS // 2):
        at = slice(128 * pair, 128 * pair + 128)
        late = slice(D + 128 * pair, D + 128 * pair + 128)
        query = query_ref[:, at]
        keys = jnp.concatenate([pair_ref[:, at], came_ref[:, at]], axis=0)
        values = jnp.concatenate([pair_ref[:, late], came_ref[:, late]], axis=0)
        done = []
        for side in range(2):
            head = slice(HEAD_DIM * side, HEAD_DIM * side + HEAD_DIM)
            scores = mm_t(query[:, head], keys[:, head]) * score_scale
            scores = jnp.where(mask, scores, -1e30)
            largest = jnp.max(scores, axis=-1, keepdims=True)
            powered = jnp.exp(scores - largest)
            totals = jnp.sum(powered, axis=-1, keepdims=True)
            total_ref[:, 2 * pair + side : 2 * pair + side + 1] = largest + jnp.log(totals)
            soft_low = (powered / totals).astype(BF)
            done.append(mm(soft_low, values[:, head]))
        mixed_ref[:, at] = jnp.concatenate(done, axis=1).astype(BF)
    mixed = mixed_ref[...]
    copies[0].wait()
    copies[1].wait()
    one, two = mm(mixed, matrix(mo, 0, 48)), mm(mixed, matrix(ms, 0, 48))
    middle = united_ref[...] + jnp.concatenate(order(core, one, two), axis=1) + spots_ref[3:4, :]
    middle_ref[...] = middle
    scaled, _ = norm_stats(middle)
    normed_ref[...] = (scaled * spots_ref[4:5, :] + spots_ref[5:6, :]).astype(BF)


def forward_kernel(core_ref, scale_ref, normed_ref, middle_ref, cotangent_ref, own_ref, other_ref, spots_ref, out_ref, middle_grad_ref, vector_ref, grad_own, grad_sent, eo, es, co, cs, before_ref, active_ref, low_ref, go, gs, sems, out_sems):
    core = core_ref[0]
    copies = load(
        [
            (own_ref.at[:, EXPAND : EXPAND + 192, :], eo),
            (other_ref.at[:, EXPAND : EXPAND + 192, :], es),
            (own_ref.at[:, CONTRACT : CONTRACT + 192, :], co),
            (other_ref.at[:, CONTRACT : CONTRACT + 192, :], cs),
        ],
        sems,
    )
    normed = normed_ref[...]
    out_grad = padded(cotangent_ref[...].astype(F32) * scale_ref[0])
    after = out_grad.astype(BF)
    vector_ref[...] = jnp.zeros((16, D), F32)
    vector_ref[6:7, :] = jnp.sum(after.astype(F32), axis=0, keepdims=True)
    copies[0].wait()
    copies[1].wait()
    for k in range(STRIPS):
        one, two = order(core, mm(normed, matrix(eo, 48 * k, 48)), mm(normed, matrix(es, 48 * k, 48)))
        for side, block in ((0, one), (1, two)):
            at = side * STRIPS * HALF + k * HALF
            bias = spots_ref[8 + at // D : 9 + at // D, at % D : at % D + HALF]
            block = block + bias
            before_ref[:, at : at + HALF] = block
            active_ref[:, at : at + HALF] = (0.5 * block * (1.0 + lax.erf(block * (1.0 / math.sqrt(2.0))))).astype(BF)
    copies[2].wait()
    copies[3].wait()
    active = active_ref[...]
    one, two = mm(active, matrix(co, 0, 192)), mm(active, matrix(cs, 0, 192))
    output = middle_ref[...] + jnp.concatenate(order(core, one, two), axis=1) + spots_ref[6:7, :]
    out_ref[...] = output[:TOKENS].astype(BF)
    after_own, after_other = split(core, after)
    for j in range(2 * STRIPS):
        at, planes = slice(HALF * j, HALF * j + HALF), slice(2 * j, 2 * j + 2)
        one, two = split(core, t_mm(active_ref[:, at], after).astype(BF))
        go[planes, CONTRACT : CONTRACT + 192, :] = one.reshape(2, 192, HALF)
        gs[planes, CONTRACT : CONTRACT + 192, :] = two.reshape(2, 192, HALF)
        back = mm_t(after_own, co[planes, :, :].reshape(HALF, HALF)) + mm_t(after_other, cs[planes, :, :].reshape(HALF, HALF))
        before = before_ref[:, at]
        cumulative = 0.5 * (1.0 + lax.erf(before * (1.0 / math.sqrt(2.0))))
        density = jnp.exp(-0.5 * before * before) * (1.0 / math.sqrt(2.0 * math.pi))
        low = (back * (cumulative + before * density)).astype(BF)
        low_ref[:, at] = low
        row = 8 + j // 2
        vector_ref[row : row + 1, HALF * (j % 2) : HALF * (j % 2) + HALF] = jnp.sum(low.astype(F32), axis=0, keepdims=True)
    incoming = jnp.zeros((PAD, D), F32)
    for k in range(STRIPS):
        one, two = order(
            core,
            low_ref[:, k * HALF : (k + 1) * HALF],
            low_ref[:, (STRIPS + k) * HALF : (STRIPS + k + 1) * HALF],
        )
        go[:, EXPAND + 48 * k : EXPAND + 48 * (k + 1), :] = t_mm(normed, one).astype(BF).reshape(PLANES, 48, HALF)
        gs[:, EXPAND + 48 * k : EXPAND + 48 * (k + 1), :] = t_mm(normed, two).astype(BF).reshape(PLANES, 48, HALF)
        incoming = incoming + mm_t(one, matrix(eo, 48 * k, 48)) + mm_t(two, matrix(es, 48 * k, 48))
    sends = load([(gs, grad_sent), (go, grad_own)], out_sems)
    scaled, inverse = norm_stats(middle_ref[...])
    back_two, gain_grad, shift_grad = norm_backward(incoming, scaled, inverse, spots_ref[4:5, :])
    vector_ref[4:5, :] = gain_grad
    vector_ref[5:6, :] = shift_grad
    middle_grad_ref[...] = out_grad + back_two
    for copy in sends:
        copy.wait()


def backward_kernel(core_ref, middle_grad_ref, query_ref, pair_ref, came_ref, total_ref, own_ref, other_ref, query_grad_ref, pair_grad_ref, sent_ref, mixed_grad_ref, mo, ms, sems):
    core = core_ref[0]
    copies = load(
        [(own_ref.at[:, MERGE : MERGE + 48, :], mo), (other_ref.at[:, MERGE : MERGE + 48, :], ms)], sems
    )
    attend_own, attend_other = split(core, middle_grad_ref[...].astype(BF))
    mask = key_mask()
    copies[0].wait()
    copies[1].wait()
    mixed_grad_ref[...] = (mm_t(attend_own, matrix(mo, 0, 48)) + mm_t(attend_other, matrix(ms, 0, 48))).astype(BF)
    for pair in range(HEADS // 2):
        at = slice(128 * pair, 128 * pair + 128)
        late = slice(D + 128 * pair, D + 128 * pair + 128)
        query, mixed_grad = query_ref[:, at], mixed_grad_ref[:, at]
        keys = jnp.concatenate([pair_ref[:, at], came_ref[:, at]], axis=0)
        values = jnp.concatenate([pair_ref[:, late], came_ref[:, late]], axis=0)
        query_parts, key_parts, value_parts = [], [], []
        for side in range(2):
            head = slice(HEAD_DIM * side, HEAD_DIM * side + HEAD_DIM)
            scores = mm_t(query[:, head], keys[:, head]) * score_scale
            scores = jnp.where(mask, scores, -1e30)
            soft = jnp.exp(scores - total_ref[:, 2 * pair + side : 2 * pair + side + 1])
            soft_grad = mm_t(mixed_grad[:, head], values[:, head])
            inner = jnp.sum(soft * soft_grad, axis=-1, keepdims=True)
            scores_grad = (soft * (soft_grad - inner)).astype(BF)
            query_parts.append(mm(scores_grad, keys[:, head]))
            key_parts.append(t_mm(scores_grad, query[:, head]))
            value_parts.append(t_mm(soft.astype(BF), mixed_grad[:, head]))
        query_grad_ref[:, at] = (jnp.concatenate(query_parts, axis=1) * score_scale).astype(BF)
        key_grad = jnp.concatenate(key_parts, axis=1) * score_scale
        value_grad = jnp.concatenate(value_parts, axis=1)
        pair_grad_ref[:, at] = key_grad[:PAD]
        pair_grad_ref[:, late] = value_grad[:PAD]
        sent_ref[:, at] = key_grad[PAD:].astype(BF)
        sent_ref[:, late] = value_grad[PAD:].astype(BF)


def scatter(place_ref, refs, blocks, at, planes, by_y):
    rows = blocks[0].shape[0] // len(planes)
    for n, plane in enumerate(planes):
        step_y, step_x = steps_to(place_ref, plane)
        spot = 4 * step_y + step_x if by_y else 4 * step_x + step_y
        for ref, block in zip(refs, blocks):
            ref[spot, at : at + rows, :] = block[n * rows : (n + 1) * rows]


def triple_kernel(place_ref, united_ref, normed_ref, middle_grad_ref, query_grad_ref, pair_grad_ref, came_ref, own_ref, other_ref, spots_ref, low_ref, vector_ref, grad_own, grad_sent, to, ts, go, gs, sems, out_sems):
    core = place_ref[0]
    copies = load(
        [(own_ref.at[:, TRIPLE : TRIPLE + 144, :], to), (other_ref.at[:, TRIPLE : TRIPLE + 144, :], ts)], sems
    )
    middle_grad = middle_grad_ref[...]
    normed = normed_ref[...]
    incoming = jnp.zeros((PAD, D), F32)
    wait(copies)
    for k in range(3):
        if k == 0:
            block = query_grad_ref[...]
        else:
            at = slice((k - 1) * D, k * D)
            block = (pair_grad_ref[:, at] + came_ref[:, at].astype(F32)).astype(BF)
        one, two = split(core, block)
        grads = split(core, t_mm(normed, block).astype(BF))
        scatter(place_ref, (go, gs), grads, 48 * k, range(PLANES), True)
        incoming = incoming + mm_t(one, matrix(to, 48 * k, 48)) + mm_t(two, matrix(ts, 48 * k, 48))
    sends = load([(gs, grad_sent), (go, grad_own)], out_sems)
    scaled, inverse = norm_stats(united_ref[...])
    back_one, gain_grad, shift_grad = norm_backward(incoming, scaled, inverse, spots_ref[1:2, :])
    united_low = (middle_grad + back_one).astype(BF)
    low_ref[...] = united_low
    vector_ref[0:1, :] = jnp.sum(united_low.astype(F32), axis=0, keepdims=True)
    vector_ref[1:2, :] = gain_grad
    vector_ref[2:3, :] = shift_grad
    vector_ref[3:8, :] = jnp.zeros((5, D), F32)
    wait(sends)


def skip_kernel(place_ref, in_ref, skip_ref, mixed_ref, middle_grad_ref, low_ref, early_ref, vector_ref, own_ref, other_ref, in_grad_ref, skip_grad_ref, grad_own, grad_sent, so, ss, go, gs, sems, out_sems):
    core = place_ref[0]
    copies = load(
        [(own_ref.at[:, SKIP : SKIP + 96, :], so), (other_ref.at[:, SKIP : SKIP + 96, :], ss)], sems
    )
    attend = middle_grad_ref[...].astype(BF)
    merge_bias_grad = jnp.sum(attend.astype(F32), axis=0, keepdims=True)
    grads = split(core, t_mm(mixed_ref[...], attend).astype(BF))
    scatter(place_ref, (go, gs), grads, MERGE, range(PLANES), False)
    vectors = [vector_ref[j : j + 1, :] for j in range(3)] + [merge_bias_grad] + [early_ref[j : j + 1, :] for j in (4, 5, 6)]
    rows = jnp.zeros((128, 128), F32)
    for j, vector in enumerate(vectors):
        lanes, place, owner = spot_masks(6)
        spread = jnp.where(owner == lanes, vector, 0.0).astype(BF)
        rows = rows + mm_t(spread, (lanes - 6 * j == place).astype(BF))
    lanes, place, owner = spot_masks(24)
    for m in range(STRIPS):
        spread = jnp.where(owner + 32 * m == lanes, early_ref[8 + m : 9 + m, :], 0.0).astype(BF)
        rows = rows + mm_t(spread, (lanes - 42 == place).astype(BF))
    rows = rows.reshape(PLANES, 8, 128)
    rows = jnp.concatenate([rows, jnp.zeros((PLANES, 8, 128), F32)], axis=1)
    rows = jnp.concatenate([rows, jnp.zeros((PLANES, 16, HALF - 128), F32)], axis=2).reshape(PLANES * 16, HALF).astype(BF)
    scatter(place_ref, (go, gs), (rows, rows), SPOTS, range(PLANES), False)
    united_low = low_ref[...]
    low_own, low_other = split(core, united_low)
    wait(copies)
    for half, block_ref, grad_ref in ((0, in_ref, in_grad_ref), (1, skip_ref, skip_grad_ref)):
        block = padded(block_ref[...])
        for part in range(2):
            first = 8 * half + 4 * part
            at = slice(HALF * part, HALF * part + HALF)
            grads = split(core, t_mm(block[:, at], united_low).astype(BF))
            scatter(place_ref, (go, gs), grads, SKIP, range(first, first + 4), False)
            planes = slice(first, first + 4)
            back = mm_t(low_own, so[planes, :, :].reshape(HALF, HALF)) + mm_t(low_other, ss[planes, :, :].reshape(HALF, HALF))
            grad_ref[:, at] = back[:TOKENS].astype(BF)
    wait(load([(gs, grad_sent), (go, grad_own)], out_sems))


def call(kernel, name, args, outs, scratch, flops):
    place = {
        "s": pl.BlockSpec(memory_space=pltpu.SMEM),
        "v": pl.BlockSpec(memory_space=pltpu.VMEM),
        "a": pl.BlockSpec(memory_space=pl.ANY),
    }
    moved = sum(a.size * a.dtype.itemsize for a, _ in args)
    return pl.pallas_call(
        kernel,
        out_shape=[jax.ShapeDtypeStruct(shape, dtype) for shape, dtype, _ in outs],
        in_specs=[place[w] for _, w in args],
        out_specs=[place[w] for _, _, w in outs],
        scratch_shapes=scratch,
        compiler_params=pltpu.CompilerParams(vmem_limit_bytes=ROOM),
        cost_estimate=pl.CostEstimate(flops=int(flops), bytes_accessed=int(moved), transcendentals=0),
        name=name,
    )(*[a for a, _ in args])


def swap(block, axis):
    return lax.ppermute(block, axis, [(0, 1), (1, 0)])


def step(block, axis, steps):
    return lax.ppermute(block, axis, [((i + steps) % 4, i) for i in range(4)])


def sum_part(kept, came, first, second):
    kept, came = (a.reshape((4, 4) + a.shape[1:]) for a in (kept, came))
    chip = [kept[k].astype(F32) + came[k].astype(F32) for k in range(4)]
    line = chip[0]
    for k in (1, 2, 3):
        line = line + step(chip[k].astype(BF), first, 4 - k).astype(F32)
    total = line[0]
    for k in (1, 2, 3):
        total = total + step(line[k].astype(BF), second, 4 - k).astype(F32)
    return total.astype(BF)


def halves(matrix_rows, strips):
    cut = [matrix_rows[:, k * HALF : (k + 1) * HALF] for k in range(2 * strips)]
    return cut[:strips], cut[strips:]


def column_gather(first_half, second_half):
    packed = jnp.stack([first_half, second_half])
    shape = packed.shape[1:]
    to_all = jnp.broadcast_to(packed[None, :, None], (2, 2, 2) + shape).reshape((8,) + shape)
    return lax.all_to_all(to_all, COLUMN, 0, 0, tiled=True)


def regroup(block, pack):
    at, parts = 0, []
    for rows in pack:
        parts.append(block[:, at : at + rows].reshape(-1, HALF))
        at += rows
    return parts


def pick_table(indices, table):
    match = indices[:, None] == jnp.arange(table.shape[0], dtype=jnp.int32)[None, :]
    return jnp.sum(jnp.where(match, table[None, :], 0.0), axis=1)


def per_device(
    inputs,
    skipped,
    cotangent,
    timestep,
    class_ids,
    time_weight,
    class_weight,
    skip_weight,
    skip_bias,
    first_gain,
    first_shift,
    triple_weight,
    merge_weight,
    merge_bias,
    second_gain,
    second_shift,
    expand_weight,
    expand_bias,
    contract_weight,
    contract_bias,
):
    core_index = lax.axis_index("c").astype(jnp.int32)
    core = core_index[None]
    place = jnp.stack([core_index, lax.axis_index("y").astype(jnp.int32), lax.axis_index("x").astype(jnp.int32)])

    scale = pick_table(timestep, time_weight) * pick_table(class_ids, class_weight)

    skip0, skip1 = halves(skip_weight.reshape(-1, D), 1)
    triple_cut = triple_weight.reshape(-1, 3 * D)
    triple0 = [triple_cut[:, k * D : k * D + HALF] for k in range(3)]
    triple1 = [triple_cut[:, k * D + HALF : (k + 1) * D] for k in range(3)]
    merge0, merge1 = halves(merge_weight.reshape(-1, D), 1)
    expand0, expand1 = halves(expand_weight.reshape(-1, FF), STRIPS)
    contract0, contract1 = halves(contract_weight.reshape(-1, D), 1)
    vectors = jnp.concatenate(
        [skip_bias, first_gain, first_shift, merge_bias, second_gain, second_shift, contract_bias, expand_bias]
    )
    row = jnp.pad(vectors[None, :], ((0, 0), (0, HALF - SPOT_WIDTH)))
    column = column_gather(
        jnp.concatenate(skip0 + merge0 + [row] + triple0 + expand0 + contract0, axis=0),
        jnp.concatenate(skip1 + merge1 + [row] + triple1 + expand1 + contract1, axis=0),
    )
    group = regroup(column, ONE_PACK + TWO_PACK + SECOND_PACK)
    first = jnp.concatenate(group[:3] + [jnp.zeros((8, HALF), BF)] + group[3:6], axis=0)
    second = jnp.concatenate(group[6:], axis=0)
    first, second, scale = lax.optimization_barrier((first, second, scale))
    second_own = lax.all_gather(second, PLANE, axis=0, tiled=True).reshape(PLANES, SECOND_ROWS, HALF)
    first_own = lax.all_to_all(
        jnp.broadcast_to(first[None], (PLANES, FIRST_ROWS, HALF)), PLANE, 0, 0, tiled=True
    )
    first_other = swap(first_own, "c")

    inputs, skipped, cotangent = (a.reshape(TOKENS, D) for a in (inputs, skipped, cotangent))
    sem = pltpu.SemaphoreType.DMA
    weight = lambda rows: pltpu.VMEM((PLANES, rows, HALF), BF)
    tokens = lambda width, dtype=BF, where="v": ((PAD, width), dtype, where)

    (spots,) = call(
        spots_kernel, "vectors", [(first_own, "a")], [((16, D), F32, "v")], [weight(16), sem((1,))], 2e8
    )
    plane = lambda rows: ((PLANES, rows, HALF), BF, "a")
    united, normed, query, pair = call(
        first_kernel,
        "skip_and_triple",
        [(core, "s"), (inputs, "v"), (skipped, "v"), (first_own, "a"), (first_other, "a"), (spots, "v")],
        [tokens(D, F32), tokens(D), tokens(D), tokens(2 * D)],
        [weight(96), weight(96), weight(144), weight(144), sem((4,))],
        2 * PAD * D * (2 * D + 3 * D),
    )
    pair_came = swap(pair, "l")
    second_own, pair_came = lax.optimization_barrier((second_own, pair_came))
    second_other = swap(second_own, "c")
    mixed, middle, normed_two, totals = call(
        attend_kernel,
        "attention",
        [
            (core, "s"),
            (query, "v"),
            (pair, "v"),
            (pair_came, "v"),
            (united, "v"),
            (first_own, "a"),
            (first_other, "a"),
            (spots, "v"),
        ],
        [tokens(D), tokens(D, F32), tokens(D), tokens(128, F32)],
        [weight(48), weight(48), sem((2,))],
        2 * PAD * D * (D + 2 * KEYS),
    )
    output, middle_grad, vector_grads, second_kept, second_sent = call(
        forward_kernel,
        "feed_forward",
        [
            (core, "s"),
            (scale, "s"),
            (normed_two, "v"),
            (middle, "v"),
            (cotangent, "v"),
            (second_own, "a"),
            (second_other, "a"),
            (spots, "v"),
        ],
        [
            ((TOKENS, D), BF, "v"),
            tokens(D, F32),
            ((16, D), F32, "v"),
            plane(SECOND_ROWS),
            plane(SECOND_ROWS),
        ],
        [weight(192)] * 4
        + [pltpu.VMEM((PAD, FF), F32), pltpu.VMEM((PAD, FF), BF), pltpu.VMEM((PAD, FF), BF)]
        + [weight(SECOND_ROWS)] * 2
        + [sem((4,)), sem((2,))],
        2 * PAD * D * FF * 6,
    )
    second_came = swap(second_sent, "c")
    query_grad, pair_grad, pair_sent = call(
        backward_kernel,
        "attention_backward",
        [
            (core, "s"),
            (middle_grad, "v"),
            (query, "v"),
            (pair, "v"),
            (pair_came, "v"),
            (totals, "v"),
            (first_own, "a"),
            (first_other, "a"),
        ],
        [tokens(D), tokens(2 * D, F32), tokens(2 * D)],
        [pltpu.VMEM((PAD, D), BF), weight(48), weight(48), sem((2,))],
        2 * PAD * D * (D + 5 * KEYS),
    )
    grad_came = swap(pair_sent, "l")
    rows = PLANES * SECOND_ROWS
    second_chip = (second_kept.astype(F32) + second_came.astype(F32)).astype(BF).reshape(rows, HALF)
    second_chip, pair_grad = lax.optimization_barrier((second_chip, pair_grad))
    second_sum = lax.psum_scatter(second_chip, PLANE, scatter_dimension=0, tiled=True)
    united_low, late_grads, two_kept, two_sent = call(
        triple_kernel,
        "triple_backward",
        [
            (place, "s"),
            (united, "v"),
            (normed, "v"),
            (middle_grad, "v"),
            (query_grad, "v"),
            (pair_grad, "v"),
            (grad_came, "v"),
            (first_own, "a"),
            (first_other, "a"),
            (spots, "v"),
        ],
        [tokens(D), ((8, D), F32, "v"), plane(TWO_ROWS), plane(TWO_ROWS)],
        [weight(TWO_ROWS)] * 4 + [sem((2,)), sem((2,))],
        2 * PAD * D * (3 * D) * 2,
    )
    two_came = swap(two_sent, "c")
    input_grad, skip_grad, one_kept, one_sent = call(
        skip_kernel,
        "skip_backward",
        [
            (place, "s"),
            (inputs, "v"),
            (skipped, "v"),
            (mixed, "v"),
            (middle_grad, "v"),
            (united_low, "v"),
            (vector_grads, "v"),
            (late_grads, "v"),
            (first_own, "a"),
            (first_other, "a"),
        ],
        [((TOKENS, D), BF, "v"), ((TOKENS, D), BF, "v"), plane(ONE_ROWS), plane(ONE_ROWS)],
        [weight(96), weight(96), weight(ONE_ROWS), weight(ONE_ROWS), sem((2,)), sem((2,))],
        2 * PAD * D * (2 * D + D) * 2,
    )
    one_came = swap(one_sent, "c")
    two_sum = sum_part(two_kept, two_came, "y", "x")
    one_sum = sum_part(one_kept, one_came, "x", "y")

    pack = ONE_PACK + TWO_PACK + SECOND_PACK
    parts = []
    for block, sizes in ((one_sum, ONE_PACK), (two_sum, TWO_PACK), (second_sum, SECOND_PACK)):
        at = 0
        for size in sizes:
            parts.append(block[at : at + 8 * size].reshape(2, 2, 2, size, HALF))
            at += 8 * size
    column = jnp.concatenate(parts, axis=3).transpose(0, 2, 1, 3, 4)
    column = column.reshape((4, 2) + column.shape[3:])
    total = jnp.sum(lax.all_to_all(column, ("h", "l"), 0, 0, tiled=True).astype(F32), axis=0)
    mine, sent = order(core_index, total[0], total[1])
    low, high = order(core_index, mine, swap(sent, "c"))
    lows, highs, at = [], [], 0
    for size in pack:
        lows.append(low[at : at + size])
        highs.append(high[at : at + size])
        at += size
    skip_out = jnp.concatenate([lows[0], highs[0]], axis=1)
    merge_out = jnp.concatenate([lows[1], highs[1]], axis=1)
    vector_out = lows[2][0]
    triple_out = jnp.concatenate([b for k in range(3, 6) for b in (lows[k], highs[k])], axis=1)
    expand_out = jnp.concatenate(lows[6:10] + highs[6:10], axis=1)
    contract_out = jnp.concatenate([lows[10], highs[10]], axis=1)
    spot = lambda j: vector_out[6 * j : 6 * j + 6]
    return (
        output[None],
        input_grad[None],
        skip_grad[None],
        skip_out.reshape(-1),
        spot(0),
        spot(1),
        spot(2),
        triple_out.reshape(-1),
        merge_out.reshape(-1),
        spot(3),
        spot(4),
        spot(5),
        expand_out.reshape(-1),
        vector_out[42:66],
        contract_out.reshape(-1),
        spot(6),
    )


def solution(mesh):
    fine = jax.sharding.Mesh(mesh.devices.reshape(4, 4, 2, 2, 2), ("y", "x", "h", "c", "l"))
    images = ("y", "x", "h", "c")
    everything = images + ("l",)
    tokens, shard = P(images, "l", None), P(everything)
    return jax.shard_map(
        per_device,
        mesh=fine,
        in_specs=(tokens,) * 3 + (P(images),) * 2 + (P(),) * 2 + (shard,) * 13,
        out_specs=(tokens,) * 3 + (shard,) * 13,
        check_vma=False,
    )
```

time: 399 us -> 298 us (0.75); the launches traced: 398 us -> 292 us
  waiting for transfers between devices: 180 us -> 83.9 us
  local copies, waits for them, and re-layouts: 99.4 us -> 27.1 us
  Pallas kernels: 0 us -> 58.9 us
  matrix products: 46 us -> 0 us
  blocking collectives: 16.7 us -> 56.2 us
  starting transfers between devices: 11.1 us -> 36.7 us
  other arithmetic: 26.1 us -> 11.3 us
    reduce_scatter x1, waiting for transfers between devices: 83.3 us -> 10.9 us  [per_device(): lax.psum_scatter(second_chip, PLANE, scatter_dimension=0, tiled=True)]
    all_gather x1, waiting for transfers between devices: 71.2 us -> 0.99 us  [per_device(): lax.all_gather(second, PLANE, axis=0, tiled=True)]
    pallas_call x0 -> x7, Pallas kernels: none -> 58.9 us  [call(): pl.pallas_call(kernel, out_shape=[jax.ShapeDtypeStruct(shape, dtype) for...]
    dot_general x21 -> x0, matrix products: 46 us -> none  [the longest x5 13.3 us: left_contract(): lax.dot_general(left, right, (((0,), (0,)), ((), ())), preferred_element_...]
    all_to_all x1, blocking collectives: 16.7 us -> 56.2 us  [per_device(): lax.all_to_all(jnp.broadcast_to(first[None], (PLANES, FIRST_ROWS, HALF)),...]
    ppermute x0 -> x12, waiting for transfers between devices: none -> 33.5 us  [step(): return lax.ppermute(block, axis, [((i + steps) % 4, i) for i in range(4)])]
    slice x32 -> x20, local copies, waits for them, and re-layouts: 35.5 us -> 3.2 us  [the longest x6 1.79 us: per_device(): parts.append(block[at:at + 8 * size].reshape(2, 2, 2, size, HALF))]
    unnamed x213 -> x36, local copies, waits for them, and re-layouts: 23.1 us -> 4.86 us
  transfers between devices with their start and end apart: 8 -> 24, of which waited for: 6 -> 17; matrix products, arithmetic and copies ran while one was open for 10% -> 2% of each run, Pallas kernels for 0% -> 15%
where the time goes in v2:
time: 298 us; the launch traced here: 292 us
  waiting for transfers between devices  83.9 us (28%)
  Pallas kernels  58.9 us (20%)
  blocking collectives  56.2 us (19%)
  starting transfers between devices  36.7 us (12%)
  local copies, waits for them, and re-layouts  27.1 us (9%)
  between operations  17.8 us (6%)
  other arithmetic  11.3 us (4%)
    pallas_call x7, Pallas kernels, call(): pl.pallas_call(kernel, out_shape=[jax.ShapeDtypeStruct(shape, dtype) for...  58.9 us
    all_to_all x1, blocking collectives, per_device(): lax.all_to_all(jnp.broadcast_to(first[None], (PLANES, FIRST_ROWS, HALF)),...  56.2 us
    ppermute x12, waiting for transfers between devices, step(): return lax.ppermute(block, axis, [((i + steps) % 4, i) for i in range(4)])  33.5 us
    ppermute x8, waiting for transfers between devices, swap(): return lax.ppermute(block, axis, [(0, 1), (1, 0)])  26.5 us
    ppermute x12, starting transfers between devices, step(): return lax.ppermute(block, axis, [((i + steps) % 4, i) for i in range(4)])  15.7 us
    reduce_scatter x1, waiting for transfers between devices, per_device(): lax.psum_scatter(second_chip, PLANE, scatter_dimension=0, tiled=True)  10.9 us
    ppermute x8, starting transfers between devices, swap(): return lax.ppermute(block, axis, [(0, 1), (1, 0)])  9.56 us
    all_to_all x1, waiting for transfers between devices, per_device(): lax.all_to_all(column, ('h', 'l'), 0, 0, tiled=True).astype(F32)  7.43 us
  transfers between devices with their start and end apart: 24, of which 17 were waited for; matrix products, arithmetic and copies ran while one was open for 2% of the time, Pallas kernels for 15%

profile of v2, /device:TPU:1, one launch (start us, length us, event | category | flops | bytes accessed | tf_op | source)
XLA Modules:
  0.0 291.9 jit_solution(12057765215749674145)
XLA Ops:
  11.2 5.4 %concatenate.33 = bf16[66]{0:T(256)(128)(2,1)S(1)} concatenate(bf16[6]{0:T(256)(128)(2,1)} %param.28, bf16[6]{0:T(256)(128)(2,1)} %param.29, bf16[6]{0:T(256)(128)(2,1)} %param.30, bf16[6]{0:T(256)(128)(2,1)} %param.33, bf16[6]{0:T(256)(128)(2,1)} %param.34, bf16[6]{0:T(256)(128)(2,1)} %param.35, bf16[6]{0:T(256)(128)(2,1)} %param.39, bf16[24]{0:T(256)(128)(2,1)} %param.37), dimensions={0} | concatenate | bytes 264 | tf_op jit(solution)/shard_map/concatenate | solution.py:479
  19.4 6.8 %all-to-all-start = ((bf16[8,85,384]{2,1,0:T(8,128)(2,1)}), bf16[8,85,384]{2,1,0:T(8,128)(2,1)S(1)}, u32[]{:S(2)}, u32[]{:S(2)}) async-start(bf16[8,85,384]{2,1,0:T(8,128)(2,1)} %bitcast.4), calls=%async_computation | async-start | bytes 1081344 | tf_op jit(solution)/shard_map/all_to_all | solution.py:428
  31.4 4.5 %all-to-all-done = bf16[8,85,384]{2,1,0:T(8,128)(2,1)S(1)} async-done(((bf16[8,85,384]{2,1,0:T(8,128)(2,1)}), bf16[8,85,384]{2,1,0:T(8,128)(2,1)S(1)}, u32[]{:S(2)}, u32[]{:S(2)}) %all-to-all-start) | async-done | bytes 522272 | tf_op jit(solution)/shard_map/all_to_all | solution.py:428
  37.6 56.2 %all_to_all.15.first_ref.own_ref = bf16[16,304,384]{2,1,0:T(8,128)(2,1)} all-to-all(bf16[16,304,384]{2,1,0:T(8,128)(2,1)S(1)} %broadcast_in_dim.50), channel_id=1, replica_groups=mesh['y'=4,'x'=4,'h'=2,'c'=2,'l'=2] {'y','x'}, dimensions={0} | all-to-all | bytes 7471104 | tf_op jit(solution)/shard_map/all_to_all | solution.py:492
  93.9 2.1 collective-permute-start
  96.0 2.5 vectors.1.spots_ref
  98.4 4.0 %collective-permute-done.other_ref = bf16[16,304,384]{2,1,0:T(8,128)(2,1)} collective-permute-done((bf16[16,304,384]{2,1,0:T(8,128)(2,1)}, bf16[16,304,384]{2,1,0:T(8,128)(2,1)}, u32[]{:S(2)}, u32[]{:S(2)}) %collective-permute-start) | collective-permute-done | bytes 3735584 | tf_op jit(solution)/shard_map/ppermute | solution.py:400
  102.4 5.6 %skip_and_triple.1 = (f32[144,768]{1,0:T(8,128)}, bf16[144,768]{1,0:T(8,128)(2,1)}, bf16[144,768]{1,0:T(8,128)(2,1)}, bf16[144,1536]{1,0:T(8,128)(2,1)}) custom-call(s32[1]{0:T(128)} %bitcast.core_ref, bf16[129,768]{1,0:T(8,128)(2,1)} %bitcast.88, bf16[129,768]{1,0:T(8,128)(2,1)} %bitcast.90, bf16[16,304,384]{2,1,0:T(8,128)(2,1)} %all_to_all.15.first_ref.own_ref, ...), custom_call_target="tpu_custom_call" | custom-call | flops 849346560 | bytes 7916548 | tf_op jit(solution)/shard_map/skip_and_triple/pallas_call | solution.py:387
  108.4 11.5 %collective-permute-done.1.came_ref = bf16[144,1536]{1,0:T(8,128)(2,1)S(1)} collective-permute-done((bf16[144,1536]{1,0:T(8,128)(2,1)}, bf16[144,1536]{1,0:T(8,128)(2,1)S(1)}, u32[]{:S(2)}, u32[]{:S(2)}) %collective-permute-start.1) | collective-permute-done | bytes 442400 | tf_op jit(solution)/shard_map/ppermute | solution.py:400
  121.6 7.5 %attention.1 = (bf16[144,768]{1,0:T(8,128)(2,1)}, f32[144,768]{1,0:T(8,128)}, bf16[144,768]{1,0:T(8,128)(2,1)}, f32[144,128]{1,0:T(8,128)}) custom-call(s32[1]{0:T(128)} %bitcast.core_ref, bf16[144,768]{1,0:T(8,128)(2,1)} %get-tuple-element.49.query_ref, bf16[144,1536]{1,0:T(8,128)(2,1)} %get-tuple-element.50.pair_ref, bf16[144,1536]{1,0:T(8,128)(2,1)} %copy-done.3, ...), custom_call_target="tpu_custom_call" | custom-call | flops 297271296 | bytes 9068548 | tf_op jit(solution)/shard_map/attention/pallas_call | solution.py:387
  129.4 2.2 copy-done.6
  131.6 15.9 %feed_forward.1 = (bf16[129,768]{1,0:T(8,128)(2,1)}, f32[144,768]{1,0:T(8,128)}, f32[16,768]{1,0:T(8,128)}, bf16[16,384,384]{2,1,0:T(8,128)(2,1)}, bf16[16,384,384]{2,1,0:T(8,128)(2,1)}) custom-call(s32[1]{0:T(128)} %bitcast.core_ref, f32[1]{0:T(128)} %bitcast.9.scale_ref, bf16[144,768]{1,0:T(8,128)(2,1)} %get-tuple-element.54.normed_ref, ...), custom_call_target="tpu_custom_call" | custom-call | flops 4076863488 | bytes 10348040 | tf_op jit(solution)/shard_map/feed_forward/pallas_call | solution.py:387
  148.1 10.8 %attention_backward.1 = (bf16[144,768]{1,0:T(8,128)(2,1)}, f32[144,1536]{1,0:T(8,128)}, bf16[144,1536]{1,0:T(8,128)(2,1)}) custom-call(s32[1]{0:T(128)} %bitcast.core_ref, f32[144,768]{1,0:T(8,128)} %get-tuple-element.59.middle_grad_ref, bf16[144,768]{1,0:T(8,128)(2,1)} %get-tuple-element.49.query_ref, bf16[144,1536]{1,0:T(8,128)(2,1)} %get-tuple-element.50.pair_ref, ...), custom_call_target="tpu_custom_call" | custom-call | flops 488374272 | bytes 9093124 | tf_op jit(solution)/shard_map/attention_backward/pallas_call | solution.py:387
  158.9 6.0 %add_convert_fusion = bf16[16,384,384]{2,1,0:T(8,128)(2,1)} fusion(bf16[16,384,384]{2,1,0:T(8,128)(2,1)} %collective-permute-done.3, bf16[16,384,384]{2,1,0:T(8,128)(2,1)S(1)} %copy-done), kind=kLoop, calls=%fused_computation | loop fusion | flops 9437184 | bytes 14155776 | tf_op jit(solution)/shard_map/convert_element_type | solution.py:580
  167.8 9.9 %collective-permute-done.4.came_ref = bf16[144,1536]{1,0:T(8,128)(2,1)S(1)} collective-permute-done((bf16[144,1536]{1,0:T(8,128)(2,1)S(1)}, bf16[144,1536]{1,0:T(8,128)(2,1)S(1)}, u32[]{:S(2)}, u32[]{:S(2)}) %collective-permute-start.4) | collective-permute-done | bytes 442400 | tf_op jit(solution)/shard_map/ppermute | solution.py:400
  178.4 8.3 %triple_backward.1 = (bf16[144,768]{1,0:T(8,128)(2,1)}, f32[8,768]{1,0:T(8,128)}, bf16[16,144,384]{2,1,0:T(8,128)(2,1)}, bf16[16,144,384]{2,1,0:T(8,128)(2,1)}) custom-call(s32[3]{0:T(128)} %pad_add_fusion.place_ref, f32[144,768]{1,0:T(8,128)} %get-tuple-element.53.united_ref, bf16[144,768]{1,0:T(8,128)(2,1)} %get-tuple-element.60.normed_ref, ...), custom_call_target="tpu_custom_call" | custom-call | flops 1019215872 | bytes 10174476 | tf_op jit(solution)/shard_map/triple_backward/pallas_call | solution.py:387
  187.6 8.4 %skip_backward.1 = (bf16[129,768]{1,0:T(8,128)(2,1)}, bf16[129,768]{1,0:T(8,128)(2,1)}, bf16[16,160,384]{2,1,0:T(8,128)(2,1)}, bf16[16,160,384]{2,1,0:T(8,128)(2,1)}) custom-call(s32[3]{0:T(128)} %pad_add_fusion.place_ref, bf16[129,768]{1,0:T(8,128)(2,1)} %bitcast.89, bf16[129,768]{1,0:T(8,128)(2,1)} %bitcast.91, ...), custom_call_target="tpu_custom_call" | custom-call | flops 1019215872 | bytes 8825868 | tf_op jit(solution)/shard_map/skip_backward/pallas_call | solution.py:387
  198.0 2.5 collective-permute-start.14
  202.3 2.4 collective-permute-start.7
  204.7 9.0 %collective-permute-done.13 = bf16[4,144,384]{2,1,0:T(8,128)(2,1)S(1)} collective-permute-done((bf16[4,144,384]{2,1,0:T(8,128)(2,1)S(1)}, bf16[4,144,384]{2,1,0:T(8,128)(2,1)S(1)}, u32[]{:S(2)}, u32[]{:S(2)}) %collective-permute-start.13) | collective-permute-done | bytes 442400 | tf_op jit(solution)/shard_map/ppermute | solution.py:404
  213.6 2.2 collective-permute-start.8
  215.8 10.4 %collective-permute-done.14 = bf16[4,144,384]{2,1,0:T(8,128)(2,1)S(1)} collective-permute-done((bf16[4,144,384]{2,1,0:T(8,128)(2,1)S(1)}, bf16[4,144,384]{2,1,0:T(8,128)(2,1)S(1)}, u32[]{:S(2)}, u32[]{:S(2)}) %collective-permute-start.14) | collective-permute-done | bytes 442400 | tf_op jit(solution)/shard_map/ppermute | solution.py:404
  227.0 2.2 collective-permute-start.17
  229.2 5.7 %collective-permute-done.16 = bf16[144,384]{1,0:T(8,128)(2,1)S(1)} collective-permute-done((bf16[144,384]{1,0:T(8,128)(2,1)S(1)}, bf16[144,384]{1,0:T(8,128)(2,1)S(1)}, u32[]{:S(2)}, u32[]{:S(2)}) %collective-permute-start.16) | collective-permute-done | bytes 110624 | tf_op jit(solution)/shard_map/ppermute | solution.py:404
  236.7 1.9 collective-permute-done.18
  240.6 1.8 collective-permute-start.11
  242.5 1.9 collective-permute-done.10
  244.7 2.6 collective-permute-done.9
  247.5 10.9 %reduce-scatter.2.cloned.1.call-done = bf16[384,384]{1,0:T(8,128)(2,1)} async-done(((bf16[6144,384]{1,0:T(8,128)(2,1)}), bf16[384,384]{1,0:T(8,128)(2,1)}) %reduce-scatter.2.cloned.1.call-update) | async-done | bytes 294928 | tf_op jit(solution)/shard_map/reduce_scatter | solution.py:582
  263.3 4.6 %all-to-all-start.2 = ((bf16[4,2,85,384]{3,1,2,0:T(2,128)(2,1)}), bf16[4,2,85,384]{3,1,2,0:T(2,128)(2,1)S(1)}, u32[]{:S(2)}, u32[]{:S(2)}) async-start(bf16[4,2,85,384]{3,1,2,0:T(2,128)(2,1)} %copy.82), calls=%async_computation.3 | async-start | bytes 1044480 | tf_op jit(solution)/shard_map/all_to_all | solution.py:635
  267.8 7.4 %all-to-all-done.2 = bf16[4,2,85,384]{3,1,2,0:T(2,128)(2,1)S(1)} async-done(((bf16[4,2,85,384]{3,1,2,0:T(2,128)(2,1)}), bf16[4,2,85,384]{3,1,2,0:T(2,128)(2,1)S(1)}, u32[]{:S(2)}, u32[]{:S(2)}) %all-to-all-start.2) | async-done | bytes 522272 | tf_op jit(solution)/shard_map/all_to_all | solution.py:635
  276.0 3.1 %collective-permute-start.19 = (f32[85,384]{1,0:T(8,128)S(1)}, f32[85,384]{1,0:T(8,128)S(1)}, u32[]{:S(2)}, u32[]{:S(2)}) collective-permute-start(f32[85,384]{1,0:T(8,128)S(1)} %bitcast.96), channel_id=1, source_target_pairs={{0,2},{2,0},{1,3},{3,1},{4,6},{6,4},{5,7},{7,5},{8,10},{10,8},{9,1... | collective-permute-start | bytes 391688 | tf_op jit(solution)/shard_map/ppermute | solution.py:400
  (142 shorter events, 38.3 us)
Async XLA Ops:
  19.4 16.5 %all-to-all-start = ((bf16[8,85,384]{2,1,0:T(8,128)(2,1)}), bf16[8,85,384]{2,1,0:T(8,128)(2,1)S(1)}, u32[]{:S(2)}, u32[]{:S(2)}) async-start(bf16[8,85,384]{2,1,0:T(8,128)(2,1)} %bitcast.4), calls=%async_computation | async-start | bytes 1081344 | tf_op jit(solution)/shard_map/all_to_all | solution.py:428
  26.2 94.6 %all-gather.2.cloned.1.call-start = ((), (), s32[]{:S(2)}) async-start(), calls=%async_computation.4 | async-start | bytes 5013504 | tf_op jit(solution)/shard_map/all_gather | solution.py:491
  36.5 0.7 copy-start.5
  37.3 221.1 %reduce-scatter.2.cloned.1.call-start = ((), (), s32[]{:S(2)}) async-start(), calls=%async_computation.5 | async-start | bytes 5013504 | tf_op jit(solution)/shard_map/reduce_scatter | solution.py:582
  93.9 8.6 %collective-permute-start = (bf16[16,304,384]{2,1,0:T(8,128)(2,1)}, bf16[16,304,384]{2,1,0:T(8,128)(2,1)}, u32[]{:S(2)}, u32[]{:S(2)}) collective-permute-start(bf16[16,304,384]{2,1,0:T(8,128)(2,1)} %all_to_all.15.first_ref.own_ref), channel_id=1, source_target_pairs={{0,2},{2,0},{1,3},{3,1},{4,6},{6,4},{5,7},{7,5},{8,10},{10,8},{9,1... | collective-permute-start | bytes 11206664 | tf_op jit(solution)/shard_map/ppermute | solution.py:400
  108.0 11.8 %collective-permute-start.1 = (bf16[144,1536]{1,0:T(8,128)(2,1)}, bf16[144,1536]{1,0:T(8,128)(2,1)S(1)}, u32[]{:S(2)}, u32[]{:S(2)}) collective-permute-start(bf16[144,1536]{1,0:T(8,128)(2,1)} %get-tuple-element.50.pair_ref), channel_id=1, source_target_pairs={{0,1},{1,0},{2,3},{3,2},{4,5},{5,4},{6,7},{7,6},{8,9},{9,8},{10,11... | collective-permute-start | bytes 1327112 | tf_op jit(solution)/shard_map/ppermute | solution.py:400
  119.8 1.8 copy-start.3
  120.8 8.6 %collective-permute-start.2 = (bf16[16,384,384]{2,1,0:T(8,128)(2,1)}, bf16[16,384,384]{2,1,0:T(8,128)(2,1)S(1)}, u32[]{:S(2)}, u32[]{:S(2)}) collective-permute-start(bf16[16,384,384]{2,1,0:T(8,128)(2,1)} %bitcast.98), channel_id=1, source_target_pairs={{0,2},{2,0},{1,3},{3,1},{4,6},{6,4},{5,7},{7,5},{8,10},{10,8},{9,1... | collective-permute-start | bytes 14155784 | tf_op jit(solution)/shard_map/ppermute | solution.py:400
  129.4 2.2 copy-start.6
  147.5 11.4 %collective-permute-start.3 = (bf16[16,384,384]{2,1,0:T(8,128)(2,1)}, bf16[16,384,384]{2,1,0:T(8,128)(2,1)}, u32[]{:S(2)}, u32[]{:S(2)}) collective-permute-start(bf16[16,384,384]{2,1,0:T(8,128)(2,1)} %get-tuple-element.64), channel_id=1, source_target_pairs={{0,2},{2,0},{1,3},{3,1},{4,6},{6,4},{5,7},{7,5},{8,10},{10,8},{9,1... | collective-permute-start | bytes 14155784 | tf_op jit(solution)/shard_map/ppermute | solution.py:400
  148.1 10.8 %copy-start = (bf16[16,384,384]{2,1,0:T(8,128)(2,1)S(1)}, bf16[16,384,384]{2,1,0:T(8,128)(2,1)}, u32[]{:S(2)}) copy-start(bf16[16,384,384]{2,1,0:T(8,128)(2,1)} %get-tuple-element.63) | copy-start | bytes 14155780
  164.9 1.0 copy-start.7
  165.9 11.7 %collective-permute-start.4 = (bf16[144,1536]{1,0:T(8,128)(2,1)S(1)}, bf16[144,1536]{1,0:T(8,128)(2,1)S(1)}, u32[]{:S(2)}, u32[]{:S(2)}) collective-permute-start(bf16[144,1536]{1,0:T(8,128)(2,1)S(1)} %copy-done.7), channel_id=1, source_target_pairs={{0,1},{1,0},{2,3},{3,2},{4,5},{5,4},{6,7},{7,6},{8,9},{9,8},{10,11... | collective-permute-start | bytes 1327112 | tf_op jit(solution)/shard_map/ppermute | solution.py:400
  177.6 0.8 copy-start.4
  186.7 9.7 %collective-permute-start.12 = (bf16[16,144,384]{2,1,0:T(8,128)(2,1)}, bf16[16,144,384]{2,1,0:T(8,128)(2,1)S(1)}, u32[]{:S(2)}, u32[]{:S(2)}) collective-permute-start(bf16[16,144,384]{2,1,0:T(8,128)(2,1)} %get-tuple-element.76), channel_id=1, source_target_pairs={{0,2},{2,0},{1,3},{3,1},{4,6},{6,4},{5,7},{7,5},{8,10},{10,8},{9,1... | collective-permute-start | bytes 5308424 | tf_op jit(solution)/shard_map/ppermute | solution.py:400
  187.6 8.8 %copy-start.2 = (bf16[16,144,384]{2,1,0:T(8,128)(2,1)S(1)}, bf16[16,144,384]{2,1,0:T(8,128)(2,1)}, u32[]{:S(2)}) copy-start(bf16[16,144,384]{2,1,0:T(8,128)(2,1)} %get-tuple-element.75) | copy-start | bytes 5308420
  196.1 5.6 %copy-start.1 = (bf16[16,160,384]{2,1,0:T(8,128)(2,1)S(1)}, bf16[16,160,384]{2,1,0:T(8,128)(2,1)}, u32[]{:S(2)}) copy-start(bf16[16,160,384]{2,1,0:T(8,128)(2,1)} %get-tuple-element.73) | copy-start | bytes 5898244
  196.1 5.6 %collective-permute-start.5 = (bf16[16,160,384]{2,1,0:T(8,128)(2,1)}, bf16[16,160,384]{2,1,0:T(8,128)(2,1)S(1)}, u32[]{:S(2)}, u32[]{:S(2)}) collective-permute-start(bf16[16,160,384]{2,1,0:T(8,128)(2,1)} %get-tuple-element.74), channel_id=1, source_target_pairs={{0,2},{2,0},{1,3},{3,1},{4,6},{6,4},{5,7},{7,5},{8,10},{10,8},{9,1... | collective-permute-start | bytes 5898248 | tf_op jit(solution)/shard_map/ppermute | solution.py:400
  196.8 16.9 %collective-permute-start.13 = (bf16[4,144,384]{2,1,0:T(8,128)(2,1)S(1)}, bf16[4,144,384]{2,1,0:T(8,128)(2,1)S(1)}, u32[]{:S(2)}, u32[]{:S(2)}) collective-permute-start(bf16[4,144,384]{2,1,0:T(8,128)(2,1)S(1)} %get-tuple-element.85), channel_id=1, source_target_pairs={{96,0},{0,32},{32,64},{64,96},{97,1},{1,33},{33,65},{65,97},{98,2}... | collective-permute-start | bytes 1327112 | tf_op jit(solution)/shard_map/ppermute | solution.py:404
  198.0 28.2 %collective-permute-start.14 = (bf16[4,144,384]{2,1,0:T(8,128)(2,1)S(1)}, bf16[4,144,384]{2,1,0:T(8,128)(2,1)S(1)}, u32[]{:S(2)}, u32[]{:S(2)}) collective-permute-start(bf16[4,144,384]{2,1,0:T(8,128)(2,1)S(1)} %get-tuple-element.87), channel_id=1, source_target_pairs={{64,0},{96,32},{0,64},{32,96},{65,1},{97,33},{1,65},{33,97},{66,2}... | collective-permute-start | bytes 1327112 | tf_op jit(solution)/shard_map/ppermute | solution.py:404
  200.5 25.7 %collective-permute-start.15 = (bf16[4,144,384]{2,1,0:T(8,128)(2,1)S(1)}, bf16[4,144,384]{2,1,0:T(8,128)(2,1)S(1)}, u32[]{:S(2)}, u32[]{:S(2)}) collective-permute-start(bf16[4,144,384]{2,1,0:T(8,128)(2,1)S(1)} %get-tuple-element.86), channel_id=1, source_target_pairs={{32,0},{64,32},{96,64},{0,96},{33,1},{65,33},{97,65},{1,97},{34,2}... | collective-permute-start | bytes 1327112 | tf_op jit(solution)/shard_map/ppermute | solution.py:404
  202.0 36.6 %collective-permute-start.6 = (bf16[4,160,384]{2,1,0:T(8,128)(2,1)S(1)}, bf16[4,160,384]{2,1,0:T(8,128)(2,1)S(1)}, u32[]{:S(2)}, u32[]{:S(2)}) collective-permute-start(bf16[4,160,384]{2,1,0:T(8,128)(2,1)S(1)} %get-tuple-element.82), channel_id=1, source_target_pairs={{24,0},{0,8},{8,16},{16,24},{25,1},{1,9},{9,17},{17,25},{26,2},{2,... | collective-permute-start | bytes 1474568 | tf_op jit(solution)/shard_map/ppermute | solution.py:404
  202.3 36.4 %collective-permute-start.7 = (bf16[4,160,384]{2,1,0:T(8,128)(2,1)S(1)}, bf16[4,160,384]{2,1,0:T(8,128)(2,1)S(1)}, u32[]{:S(2)}, u32[]{:S(2)}) collective-permute-start(bf16[4,160,384]{2,1,0:T(8,128)(2,1)S(1)} %get-tuple-element.84), channel_id=1, source_target_pairs={{16,0},{24,8},{0,16},{8,24},{17,1},{25,9},{1,17},{9,25},{18,2},{26... | collective-permute-start | bytes 1474568 | tf_op jit(solution)/shard_map/ppermute | solution.py:404
  213.6 25.0 %collective-permute-start.8 = (bf16[4,160,384]{2,1,0:T(8,128)(2,1)S(1)}, bf16[4,160,384]{2,1,0:T(8,128)(2,1)S(1)}, u32[]{:S(2)}, u32[]{:S(2)}) collective-permute-start(bf16[4,160,384]{2,1,0:T(8,128)(2,1)S(1)} %get-tuple-element.83), channel_id=1, source_target_pairs={{8,0},{16,8},{24,16},{0,24},{9,1},{17,9},{25,17},{1,25},{10,2},{18... | collective-permute-start | bytes 1474568 | tf_op jit(solution)/shard_map/ppermute | solution.py:404
  226.5 8.4 %collective-permute-start.16 = (bf16[144,384]{1,0:T(8,128)(2,1)S(1)}, bf16[144,384]{1,0:T(8,128)(2,1)S(1)}, u32[]{:S(2)}, u32[]{:S(2)}) collective-permute-start(bf16[144,384]{1,0:T(8,128)(2,1)S(1)} %get-tuple-element.99), channel_id=1, source_target_pairs={{24,0},{0,8},{8,16},{16,24},{25,1},{1,9},{9,17},{17,25},{26,2},{2,... | collective-permute-start | bytes 331784 | tf_op jit(solution)/shard_map/ppermute | solution.py:404
  227.0 9.7 %collective-permute-start.17 = (bf16[144,384]{1,0:T(8,128)(2,1)S(1)}, bf16[144,384]{1,0:T(8,128)(2,1)S(1)}, u32[]{:S(2)}, u32[]{:S(2)}) collective-permute-start(bf16[144,384]{1,0:T(8,128)(2,1)S(1)} %get-tuple-element.101), channel_id=1, source_target_pairs={{16,0},{24,8},{0,16},{8,24},{17,1},{25,9},{1,17},{9,25},{18,2},{26... | collective-permute-start | bytes 331784 | tf_op jit(solution)/shard_map/ppermute | solution.py:404
  234.9 3.6 %collective-permute-start.18 = (bf16[144,384]{1,0:T(8,128)(2,1)S(1)}, bf16[144,384]{1,0:T(8,128)(2,1)S(1)}, u32[]{:S(2)}, u32[]{:S(2)}) collective-permute-start(bf16[144,384]{1,0:T(8,128)(2,1)S(1)} %get-tuple-element.100), channel_id=1, source_target_pairs={{8,0},{16,8},{24,16},{0,24},{9,1},{17,9},{25,17},{1,25},{10,2},{18... | collective-permute-start | bytes 331784 | tf_op jit(solution)/shard_map/ppermute | solution.py:404
  239.0 5.3 %collective-permute-start.10 = (bf16[160,384]{1,0:T(8,128)(2,1)S(1)}, bf16[160,384]{1,0:T(8,128)(2,1)S(1)}, u32[]{:S(2)}, u32[]{:S(2)}) collective-permute-start(bf16[160,384]{1,0:T(8,128)(2,1)S(1)} %get-tuple-element.98), channel_id=1, source_target_pairs={{64,0},{96,32},{0,64},{32,96},{65,1},{97,33},{1,65},{33,97},{66,2}... | collective-permute-start | bytes 368648 | tf_op jit(solution)/shard_map/ppermute | solution.py:404
  240.6 4.1 %collective-permute-start.11 = (bf16[160,384]{1,0:T(8,128)(2,1)S(1)}, bf16[160,384]{1,0:T(8,128)(2,1)S(1)}, u32[]{:S(2)}, u32[]{:S(2)}) collective-permute-start(bf16[160,384]{1,0:T(8,128)(2,1)S(1)} %get-tuple-element.97), channel_id=1, source_target_pairs={{32,0},{64,32},{96,64},{0,96},{33,1},{65,33},{97,65},{1,97},{34,2}... | collective-permute-start | bytes 368648 | tf_op jit(solution)/shard_map/ppermute | solution.py:404
  242.4 4.9 %collective-permute-start.9 = (bf16[160,384]{1,0:T(8,128)(2,1)S(1)}, bf16[160,384]{1,0:T(8,128)(2,1)S(1)}, u32[]{:S(2)}, u32[]{:S(2)}) collective-permute-start(bf16[160,384]{1,0:T(8,128)(2,1)S(1)} %get-tuple-element.96), channel_id=1, source_target_pairs={{96,0},{0,32},{32,64},{64,96},{97,1},{1,33},{33,65},{65,97},{98,2}... | collective-permute-start | bytes 368648 | tf_op jit(solution)/shard_map/ppermute | solution.py:404
  263.3 12.0 %all-to-all-start.2 = ((bf16[4,2,85,384]{3,1,2,0:T(2,128)(2,1)}), bf16[4,2,85,384]{3,1,2,0:T(2,128)(2,1)S(1)}, u32[]{:S(2)}, u32[]{:S(2)}) async-start(bf16[4,2,85,384]{3,1,2,0:T(2,128)(2,1)} %copy.82), calls=%async_computation.3 | async-start | bytes 1044480 | tf_op jit(solution)/shard_map/all_to_all | solution.py:635
  276.0 4.1 %collective-permute-start.19 = (f32[85,384]{1,0:T(8,128)S(1)}, f32[85,384]{1,0:T(8,128)S(1)}, u32[]{:S(2)}, u32[]{:S(2)}) collective-permute-start(f32[85,384]{1,0:T(8,128)S(1)} %bitcast.96), channel_id=1, source_target_pairs={{0,2},{2,0},{1,3},{3,1},{4,6},{6,4},{5,7},{7,5},{8,10},{10,8},{9,1... | collective-permute-start | bytes 391688 | tf_op jit(solution)/shard_map/ppermute | solution.py:400
Sparse Core Ops, SparseCore 0:
  37.4 83.3 all-gather.1
  165.0 93.2 reduce-scatter.1

commit v3 on v2

v3 whole, which is shorter than its diff:
```python
import functools
import math

import jax
import jax.numpy as jnp
import numpy as np
from jax import lax
from jax.experimental import pallas as pl
from jax.experimental.pallas import tpu as pltpu
from jax.sharding import PartitionSpec as P

D = 768
HEADS = 12
HEAD_DIM = 64
FF = 3072
HALF = D // 2
STRIPS = FF // D
TOKENS = 129
PAD = 144
KEYS = 2 * PAD
PLANES = 16
PLANE = ("y", "x")
COLUMN = ("h", "c", "l")
SKIP, SPOTS, TRIPLE = 0, 96, 112
EXPAND, CONTRACT, MERGE = 0, 192, 384
FIRST_ROWS, SECOND_ROWS = 256, 432
ONE_ROWS, TWO_ROWS = 112, 144
EARLY_ROWS = 448
FIRST_PACK, SECOND_PACK = (12, 1, 6, 6, 6), (6, 6, 6, 6, 24, 6)
PACK = FIRST_PACK + SECOND_PACK
PACK_ROWS = 88
NAMES = ("skip", "triple", "expand", "contract", "merge")
SUM_ROWS = ONE_ROWS + TWO_ROWS + EARLY_ROWS
SUM_STARTS = (0, 96, 112, 160, 208) + tuple(256 + at for at in (0, 48, 96, 144, 192, 384))
epsilon = 1e-05
score_scale = 1.0 / math.sqrt(HEAD_DIM)
BF, F32 = jnp.bfloat16, jnp.float32
ATTEND = FF + FF // 2
NORMED = ATTEND + HALF
GIFT = NORMED + D


def mm(left, right):
    return jnp.dot(left, right, preferred_element_type=F32)


def mm_t(left, right):
    return lax.dot_general(left, right, (((1,), (1,)), ((), ())), preferred_element_type=F32)


def t_mm(left, right):
    return lax.dot_general(left, right, (((0,), (0,)), ((), ())), preferred_element_type=F32)


def order(core, one, two):
    return jnp.where(core == 0, one, two), jnp.where(core == 0, two, one)


def split(core, block):
    return order(core, block[:, :HALF], block[:, HALF:])


def norm_stats(values):
    mean_value = jnp.mean(values, axis=-1, keepdims=True)
    centered = values - mean_value
    variance = jnp.mean(centered * centered, axis=-1, keepdims=True)
    inverse = lax.rsqrt(variance + epsilon)
    return centered * inverse, inverse


def norm_backward(incoming, scaled, inverse, gain):
    weighted = incoming * gain
    first_mean = jnp.mean(weighted, axis=-1, keepdims=True)
    second_mean = jnp.mean(weighted * scaled, axis=-1, keepdims=True)
    value_grad = inverse * (weighted - first_mean - scaled * second_mean)
    return (
        value_grad,
        jnp.sum(incoming * scaled, axis=0, keepdims=True),
        jnp.sum(incoming, axis=0, keepdims=True),
    )


def padded(block):
    return jnp.concatenate([block, jnp.zeros((PAD - TOKENS, block.shape[1]), block.dtype)], axis=0)


def load(pairs, sems):
    copies = [pltpu.make_async_copy(s, d, sems.at[k]) for k, (s, d) in enumerate(pairs)]
    for copy in copies:
        copy.start()
    return copies


def matrix(ref, at, rows):
    return ref[:, at : at + rows, :].reshape(PLANES * rows, HALF)


def spot_masks(width):
    lanes = lax.broadcasted_iota(jnp.int32, (128, D), 0)
    spots = lax.broadcasted_iota(jnp.int32, (128, D), 1)
    return lanes, lax.rem(spots, width), lax.div(spots, width)


def steps_to(place_ref, plane):
    return (plane // 4 - place_ref[1]) & 3, (plane % 4 - place_ref[2]) & 3


def wait(copies):
    for copy in copies:
        copy.wait()


def tiles_of(matrix_name):
    count, strips, across = {"skip": (6, 1, 6), "triple": (18, 1, 6), "merge": (6, 1, 6), "expand": (24, STRIPS, 24), "contract": (6, 1, 6)}[matrix_name]
    for tile in range(count):
        block, inside = divmod(tile, across)
        half, rest = divmod(inside, across // 2)
        yield tile, half, block + rest // 3, rest % 3


def pack_kernel(*refs):
    count = len(NAMES)
    sources, (row_ref, out_ref, rows_ref), scratch = refs[:count], refs[count : count + 3], refs[count + 3 :]
    low, scratch, sems = scratch[:count], scratch[count : 2 * count], scratch[2 * count]
    copies = load(list(zip(sources, low)), sems)
    at = 0
    for name, held, ref, copy in zip(NAMES, scratch, low, copies):
        copy.wait()
        held[...] = ref[...].astype(F32)
        tiles = list(tiles_of(name))
        rows = held.shape[0] // len(tiles)
        for tile, half, strip, spot in tiles:
            first = at + strip * rows
            rows_ref[half, first : first + rows, 128 * spot : 128 * spot + 128] = held[pl.ds(tile, rows, stride=len(tiles)), :]
        at += rows * (1 + max(t[2] for t in tiles))
        if name == "skip":
            rows_ref[0, at : at + 1, :] = row_ref[...]
            rows_ref[1, at : at + 1, :] = row_ref[...]
            at += 1
    rows_ref[:, at:PACK_ROWS, :] = jnp.zeros((2, PACK_ROWS - at, HALF), F32)
    for half in range(2):
        packed = rows_ref[half].astype(BF)
        for device in range(8):
            if device // 2 % 2 == half:
                out_ref[device] = packed


def unpack_kernel(low_ref, high_ref, *refs):
    outs = dict(zip(NAMES, refs))
    at = 0
    for name in NAMES:
        tiles = list(tiles_of(name))
        rows = outs[name].shape[0] // len(tiles)
        for tile, half, strip, spot in tiles:
            first = at + strip * rows
            source = high_ref if half else low_ref
            outs[name][pl.ds(tile, rows, stride=len(tiles)), :] = source[first : first + rows, 128 * spot : 128 * spot + 128]
        at += rows * (1 + max(t[2] for t in tiles))
        if name == "skip":
            refs[5][...] = low_ref[at : at + 1, :128] + high_ref[at : at + 1, :128]
            at += 1


def prepare_kernel(core_ref, scale_ref, in_ref, skip_ref, cotangent_ref, after_ref, gift_ref):
    gift_ref[:, :D] = padded(in_ref[...])
    gift_ref[:, D : 2 * D] = padded(skip_ref[...])
    after = padded(cotangent_ref[...].astype(F32) * scale_ref[0]).astype(BF)
    after_ref[...] = after
    gift_ref[:, 2 * D :] = split(core_ref[0], after)[1]


def spots_kernel(first_ref, out_ref, rows_ref, sems):
    wait(load([(first_ref.at[:, SPOTS : SPOTS + 16, :], rows_ref)], sems))
    held = rows_ref[:, :, :128].astype(F32)[:, :8].reshape(128, 128).astype(BF)
    for j in range(7):
        lanes, place, owner = spot_masks(6)
        one_hot = (lanes - 6 * j == place).astype(BF)
        spread = jnp.where(owner == lanes, mm(held, one_hot), 0.0)
        out_ref[j : j + 1, :] = jnp.sum(spread, axis=0, keepdims=True)
    out_ref[7:8, :] = jnp.zeros((1, D), F32)
    lanes, place, owner = spot_masks(24)
    spread = mm(held, (lanes - 42 == place).astype(BF))
    for m in range(STRIPS):
        out_ref[8 + m : 9 + m, :] = jnp.sum(jnp.where(owner + 32 * m == lanes, spread, 0.0), axis=0, keepdims=True)
    out_ref[12:16, :] = jnp.zeros((4, D), F32)


def first_kernel(core_ref, joined_ref, own_ref, other_ref, spots_ref, united_ref, normed_ref, query_ref, pair_ref, so, ss, to, ts, sems):
    core = core_ref[0]
    copies = load(
        [
            (own_ref.at[:, SKIP : SKIP + 96, :], so),
            (other_ref.at[:, SKIP : SKIP + 96, :], ss),
            (own_ref.at[:, TRIPLE : TRIPLE + 144, :], to),
            (other_ref.at[:, TRIPLE : TRIPLE + 144, :], ts),
        ],
        sems,
    )
    joined = joined_ref[:, : 2 * D]
    copies[0].wait()
    one = mm(joined, matrix(so, 0, 96))
    copies[1].wait()
    two = mm(joined, matrix(ss, 0, 96))
    united = jnp.concatenate(order(core, one, two), axis=1) + spots_ref[0:1, :]
    united_ref[...] = united
    scaled, _ = norm_stats(united)
    normed = (scaled * spots_ref[1:2, :] + spots_ref[2:3, :]).astype(BF)
    normed_ref[...] = normed
    copies[2].wait()
    copies[3].wait()
    for k in range(3):
        one = mm(normed, matrix(to, 48 * k, 48))
        two = mm(normed, matrix(ts, 48 * k, 48))
        block = jnp.concatenate(order(core, one, two), axis=1).astype(BF)
        if k == 0:
            query_ref[...] = block
        else:
            pair_ref[:, (k - 1) * D : k * D] = block


def key_mask():
    spots = lax.broadcasted_iota(jnp.int32, (1, KEYS), 1)
    return (spots < TOKENS) | ((spots >= PAD) & (spots < PAD + TOKENS))


def attend_kernel(query_ref, pair_ref, came_ref, mixed_ref, total_ref):
    mask = key_mask()
    total_ref[...] = jnp.zeros((PAD, 128), F32)
    for pair in range(HEADS // 2):
        at = slice(128 * pair, 128 * pair + 128)
        late = slice(D + 128 * pair, D + 128 * pair + 128)
        query = query_ref[:, at]
        keys = jnp.concatenate([pair_ref[:, at], came_ref[:, at]], axis=0)
        values = jnp.concatenate([pair_ref[:, late], came_ref[:, late]], axis=0)
        done = []
        for side in range(2):
            head = slice(HEAD_DIM * side, HEAD_DIM * side + HEAD_DIM)
            scores = mm_t(query[:, head], keys[:, head]) * score_scale
            scores = jnp.where(mask, scores, -1e30)
            largest = jnp.max(scores, axis=-1, keepdims=True)
            powered = jnp.exp(scores - largest)
            totals = jnp.sum(powered, axis=-1, keepdims=True)
            total_ref[:, 2 * pair + side : 2 * pair + side + 1] = largest + jnp.log(totals)
            soft_low = (powered / totals).astype(BF)
            done.append(mm(soft_low, values[:, head]))
        mixed_ref[:, at] = jnp.concatenate(done, axis=1).astype(BF)


def forward_kernel(core_ref, scale_ref, mixed_ref, united_ref, cotangent_ref, after_ref, own_ref, other_ref, spots_ref, out_ref, middle_grad_ref, vector_ref, gift_ref, kept_ref, eo, es, co, cs, mo, ms, slope_ref, low_ref, sems):
    core = core_ref[0]
    copies = load(
        [
            (own_ref.at[:, MERGE : MERGE + 48, :], mo),
            (other_ref.at[:, MERGE : MERGE + 48, :], ms),
            *[
                (ref.at[:, 48 * k : 48 * k + 48, :], to.at[:, 48 * k : 48 * k + 48, :])
                for k in range(STRIPS)
                for ref, to in ((own_ref, eo), (other_ref, es))
            ],
            (own_ref.at[:, CONTRACT : CONTRACT + 192, :], co),
            (other_ref.at[:, CONTRACT : CONTRACT + 192, :], cs),
        ],
        sems,
    )
    after = after_ref[...]
    vector_ref[...] = jnp.zeros((16, D), F32)
    vector_ref[6:7, :] = jnp.sum(after.astype(F32), axis=0, keepdims=True)
    after_own, after_other = split(core, after)
    mixed = mixed_ref[...]
    wait(copies[:2])
    one, two = mm(mixed, matrix(mo, 0, 48)), mm(mixed, matrix(ms, 0, 48))
    middle = united_ref[...] + jnp.concatenate(order(core, one, two), axis=1) + spots_ref[3:4, :]
    scaled, inverse = norm_stats(middle)
    normed = (scaled * spots_ref[4:5, :] + spots_ref[5:6, :]).astype(BF)
    gift_ref[:, NORMED:] = normed
    for k in range(STRIPS):
        wait(copies[2 + 2 * k : 4 + 2 * k])
        one, two = order(core, mm(normed, matrix(eo, 48 * k, 48)), mm(normed, matrix(es, 48 * k, 48)))
        for side, block in ((0, one), (1, two)):
            at = side * STRIPS * HALF + k * HALF
            bias = spots_ref[8 + at // D : 9 + at // D, at % D : at % D + HALF]
            block = block + bias
            cumulative = 0.5 * (1.0 + lax.erf(block * (1.0 / math.sqrt(2.0))))
            density = jnp.exp(-0.5 * block * block) * (1.0 / math.sqrt(2.0 * math.pi))
            gift_ref[:, at : at + HALF] = (block * cumulative).astype(BF)
            slope_ref[:, at : at + HALF] = cumulative + block * density
    wait(copies[2 + 2 * STRIPS :])
    active = gift_ref[:, :FF]
    one, two = mm(active, matrix(co, 0, 192)), mm(active, matrix(cs, 0, 192))
    output = middle + jnp.concatenate(order(core, one, two), axis=1) + spots_ref[6:7, :]
    out_ref[...] = output[:TOKENS].astype(BF)
    for j in range(2 * STRIPS):
        at, planes = slice(HALF * j, HALF * j + HALF), slice(2 * j, 2 * j + 2)
        back = mm_t(after_own, co[planes, :, :].reshape(HALF, HALF)) + mm_t(after_other, cs[planes, :, :].reshape(HALF, HALF))
        low = (back * slope_ref[:, at]).astype(BF)
        low_ref[:, at] = low
        row = 8 + j // 2
        vector_ref[row : row + 1, HALF * (j % 2) : HALF * (j % 2) + HALF] = jnp.sum(low.astype(F32), axis=0, keepdims=True)
    incoming = jnp.zeros((PAD, D), F32)
    for k in range(STRIPS):
        one, two = order(
            core,
            low_ref[:, k * HALF : (k + 1) * HALF],
            low_ref[:, (STRIPS + k) * HALF : (STRIPS + k + 1) * HALF],
        )
        kept_ref[:, k * HALF : (k + 1) * HALF] = one
        gift_ref[:, FF + k * HALF : FF + (k + 1) * HALF] = two
        incoming = incoming + mm_t(one, matrix(eo, 48 * k, 48)) + mm_t(two, matrix(es, 48 * k, 48))
    back_two, gain_grad, shift_grad = norm_backward(incoming, scaled, inverse, spots_ref[4:5, :])
    vector_ref[4:5, :] = gain_grad
    vector_ref[5:6, :] = shift_grad
    middle_grad = padded(cotangent_ref[...].astype(F32) * scale_ref[0]) + back_two
    middle_grad_ref[...] = middle_grad
    attend = middle_grad.astype(BF)
    vector_ref[3:4, :] = jnp.sum(attend.astype(F32), axis=0, keepdims=True)
    gift_ref[:, ATTEND:NORMED] = split(core, attend)[1]


def early_kernel(core_ref, gift_any, came_any, kept_any, after_ref, first_came_ref, mixed_ref, mixed_came_ref, middle_grad_ref, grad_ref, gift_ref, came_ref, kept_ref, go, sems, out_sems):
    core = core_ref[0]
    copies = load(
        [
            (gift_any.at[:, :FF], gift_ref.at[:, :FF]),
            (came_any.at[:, :FF], came_ref.at[:, :FF]),
            (gift_any.at[:, NORMED:], gift_ref.at[:, NORMED:]),
            (came_any.at[:, FF:], came_ref.at[:, FF:]),
            (kept_any, kept_ref),
        ],
        sems,
    )
    after, after_came = split(core, after_ref[...])[0], first_came_ref[:, 2 * D :]
    wait(copies[:2])
    for j in range(2 * STRIPS):
        at, planes = slice(HALF * j, HALF * j + HALF), slice(2 * j, 2 * j + 2)
        grad = t_mm(gift_ref[:, at], after) + t_mm(came_ref[:, at], after_came)
        go[planes, CONTRACT : CONTRACT + 192, :] = grad.astype(BF).reshape(2, 192, HALF)
    rows = lambda at, to: (go.at[:, at:to, :], grad_ref.at[:, at:to, :])
    sends = load([rows(CONTRACT, CONTRACT + 192)], out_sems)
    wait(copies[2:])
    attend = split(core, middle_grad_ref[...].astype(BF))[0]
    grad = t_mm(mixed_ref[...], attend) + t_mm(mixed_came_ref[...], came_ref[:, ATTEND:NORMED])
    go[:, MERGE : MERGE + 48, :] = grad.astype(BF).reshape(PLANES, 48, HALF)
    go[:, MERGE + 48 :, :] = jnp.zeros((PLANES, EARLY_ROWS - MERGE - 48, HALF), BF)
    sends += load([rows(MERGE, EARLY_ROWS)], out_sems.at[1:])
    normed, normed_came = gift_ref[:, NORMED:], came_ref[:, NORMED:]
    for k in range(STRIPS):
        grad = t_mm(normed, kept_ref[:, k * HALF : (k + 1) * HALF]) + t_mm(
            normed_came, came_ref[:, FF + k * HALF : FF + (k + 1) * HALF]
        )
        go[:, EXPAND + 48 * k : EXPAND + 48 * (k + 1), :] = grad.astype(BF).reshape(PLANES, 48, HALF)
        sends += load([rows(EXPAND + 48 * k, EXPAND + 48 * (k + 1))], out_sems.at[2 + k :])
    wait(sends)


def backward_kernel(core_ref, middle_grad_ref, query_ref, pair_ref, came_ref, total_ref, own_ref, other_ref, query_grad_ref, pair_grad_ref, sent_ref, mixed_grad_ref, mo, ms, sems):
    core = core_ref[0]
    copies = load(
        [(own_ref.at[:, MERGE : MERGE + 48, :], mo), (other_ref.at[:, MERGE : MERGE + 48, :], ms)], sems
    )
    attend_own, attend_other = split(core, middle_grad_ref[...].astype(BF))
    mask = key_mask()
    copies[0].wait()
    copies[1].wait()
    mixed_grad_ref[...] = (mm_t(attend_own, matrix(mo, 0, 48)) + mm_t(attend_other, matrix(ms, 0, 48))).astype(BF)
    for pair in range(HEADS // 2):
        at = slice(128 * pair, 128 * pair + 128)
        late = slice(D + 128 * pair, D + 128 * pair + 128)
        query, mixed_grad = query_ref[:, at], mixed_grad_ref[:, at]
        keys = jnp.concatenate([pair_ref[:, at], came_ref[:, at]], axis=0)
        values = jnp.concatenate([pair_ref[:, late], came_ref[:, late]], axis=0)
        query_parts, key_parts, value_parts = [], [], []
        for side in range(2):
            head = slice(HEAD_DIM * side, HEAD_DIM * side + HEAD_DIM)
            scores = mm_t(query[:, head], keys[:, head]) * score_scale
            scores = jnp.where(mask, scores, -1e30)
            soft = jnp.exp(scores - total_ref[:, 2 * pair + side : 2 * pair + side + 1])
            soft_grad = mm_t(mixed_grad[:, head], values[:, head])
            inner = jnp.sum(soft * soft_grad, axis=-1, keepdims=True)
            scores_grad = (soft * (soft_grad - inner)).astype(BF)
            query_parts.append(mm(scores_grad, keys[:, head]))
            key_parts.append(t_mm(scores_grad, query[:, head]))
            value_parts.append(t_mm(soft.astype(BF), mixed_grad[:, head]))
        query_grad_ref[:, at] = (jnp.concatenate(query_parts, axis=1) * score_scale).astype(BF)
        key_grad = jnp.concatenate(key_parts, axis=1) * score_scale
        value_grad = jnp.concatenate(value_parts, axis=1)
        pair_grad_ref[:, at] = key_grad[:PAD]
        pair_grad_ref[:, late] = value_grad[:PAD]
        sent_ref[:, at] = key_grad[PAD:].astype(BF)
        sent_ref[:, late] = value_grad[PAD:].astype(BF)


def scatter(place_ref, ref, block, at, by_y):
    rows = block.shape[0] // PLANES
    for plane in range(PLANES):
        step_y, step_x = steps_to(place_ref, plane)
        spot = 4 * step_y + step_x if by_y else 4 * step_x + step_y
        ref[spot, at : at + rows, :] = block[plane * rows : (plane + 1) * rows]


def vector_rows(vectors, places):
    rows = jnp.zeros((128, 128), F32)
    for vector, at in zip(vectors, places):
        lanes, place, owner = spot_masks(6)
        spread = jnp.where(owner == lanes, vector, 0.0).astype(BF)
        rows = rows + mm_t(spread, (lanes - at == place).astype(BF))
    return rows


def query_kernel(core_ref, query_grad_ref, early_ref, own_ref, other_ref, incoming_ref, rows_ref, to, ts, sems):
    copies = load(
        [(own_ref.at[:, TRIPLE : TRIPLE + 48, :], to), (other_ref.at[:, TRIPLE : TRIPLE + 48, :], ts)], sems
    )
    rows = vector_rows([early_ref[j : j + 1, :] for j in range(3, 7)], (18, 24, 30, 36))
    lanes, place, owner = spot_masks(24)
    for m in range(STRIPS):
        spread = jnp.where(owner + 32 * m == lanes, early_ref[8 + m : 9 + m, :], 0.0).astype(BF)
        rows = rows + mm_t(spread, (lanes - 42 == place).astype(BF))
    rows_ref[...] = rows
    one, two = split(core_ref[0], query_grad_ref[...])
    wait(copies)
    incoming_ref[...] = mm_t(one, matrix(to, 0, 48)) + mm_t(two, matrix(ts, 0, 48))


def triple_kernel(core_ref, united_ref, middle_grad_ref, query_grad_ref, pair_grad_ref, came_ref, incoming_ref, own_ref, other_ref, spots_ref, low_ref, vector_ref, kept_ref, gift_ref, to, ts, sems):
    core = core_ref[0]
    copies = load(
        [(own_ref.at[:, TRIPLE + 48 : TRIPLE + 144, :], to), (other_ref.at[:, TRIPLE + 48 : TRIPLE + 144, :], ts)], sems
    )
    scaled, inverse = norm_stats(united_ref[...])
    incoming = incoming_ref[...]
    wait(copies)
    for k in range(3):
        if k == 0:
            block = query_grad_ref[...]
        else:
            at = slice((k - 1) * D, k * D)
            block = (pair_grad_ref[:, at] + came_ref[:, at].astype(F32)).astype(BF)
        one, two = split(core, block)
        kept_ref[:, k * HALF : (k + 1) * HALF] = one
        gift_ref[:, k * HALF : (k + 1) * HALF] = two
        if k:
            incoming = incoming + mm_t(one, matrix(to, 48 * (k - 1), 48)) + mm_t(two, matrix(ts, 48 * (k - 1), 48))
    back_one, gain_grad, shift_grad = norm_backward(incoming, scaled, inverse, spots_ref[1:2, :])
    united_low = (middle_grad_ref[...] + back_one).astype(BF)
    low_ref[...] = united_low
    gift_ref[:, 3 * HALF :] = split(core, united_low)[1]
    vector_ref[0:1, :] = jnp.sum(united_low.astype(F32), axis=0, keepdims=True)
    vector_ref[1:2, :] = gain_grad
    vector_ref[2:3, :] = shift_grad
    vector_ref[3:8, :] = jnp.zeros((5, D), F32)


def skip_kernel(core_ref, low_ref, own_ref, other_ref, in_grad_ref, skip_grad_ref, so, ss, sems):
    copies = load(
        [(own_ref.at[:, SKIP : SKIP + 96, :], so), (other_ref.at[:, SKIP : SKIP + 96, :], ss)], sems
    )
    low_own, low_other = split(core_ref[0], low_ref[...])
    wait(copies)
    for half, grad_ref in ((0, in_grad_ref), (1, skip_grad_ref)):
        planes = slice(8 * half, 8 * half + 8)
        back = mm_t(low_own, so[planes, :, :].reshape(D, HALF)) + mm_t(low_other, ss[planes, :, :].reshape(D, HALF))
        grad_ref[...] = back[:TOKENS].astype(BF)


def late_kernel(place_ref, joined_ref, first_came_ref, normed_ref, normed_came_ref, low_ref, kept_ref, came_ref, early_ref, vector_ref, *refs):
    one_refs, two_refs, (go, gt, sems) = refs[:4], refs[4:8], refs[8:]
    for k in range(3):
        at = slice(k * HALF, (k + 1) * HALF)
        grad = t_mm(normed_ref[...], kept_ref[:, at]) + t_mm(normed_came_ref[...], came_ref[:, at])
        scatter(place_ref, gt, grad.astype(BF), 48 * k, True)
    sends = load([(gt.at[4 * k : 4 * k + 4], two_refs[k]) for k in range(4)], sems.at[:4])
    low, low_came = split(place_ref[0], low_ref[...])[0], came_ref[:, 3 * HALF :]
    grad = t_mm(joined_ref[:, : 2 * D], low) + t_mm(first_came_ref[:, : 2 * D], low_came)
    scatter(place_ref, go, grad.astype(BF), SKIP, False)
    rows = early_ref[...] + vector_rows([vector_ref[j : j + 1, :] for j in range(3)], (0, 6, 12))
    rows = jnp.concatenate([rows.reshape(PLANES, 8, 128), jnp.zeros((PLANES, 8, 128), F32)], axis=1)
    rows = jnp.concatenate([rows, jnp.zeros((PLANES, 16, HALF - 128), F32)], axis=2)
    scatter(place_ref, go, rows.reshape(PLANES * 16, HALF).astype(BF), 96, False)
    wait(sends)
    wait(load([(go.at[4 * k : 4 * k + 4], one_refs[k]) for k in range(4)], sems.at[4:]))


def column_kernel(one_ref, two_ref, early_ref, moves_ref, out_ref, rows_ref):
    rows_ref[:ONE_ROWS] = one_ref[...]
    rows_ref[ONE_ROWS : ONE_ROWS + TWO_ROWS] = two_ref[...]
    rows_ref[ONE_ROWS + TWO_ROWS :] = early_ref[...]
    out_ref[...] = mm(moves_ref[...], rows_ref[...]).astype(BF).reshape(4, 2 * PACK_ROWS, HALF)


def column_moves():
    moves = np.zeros((8 * PACK_ROWS, SUM_ROWS), np.float32)
    for high in range(2):
        for low in range(2):
            for core in range(2):
                at = ((2 * high + low) * 2 + core) * PACK_ROWS
                device = (2 * high + core) * 2 + low
                for rows, start in zip(PACK, SUM_STARTS):
                    for row in range(rows):
                        moves[at + row, start + device * rows + row] = 1.0
                    at += rows
    return moves


def call(kernel, name, args, outs, scratch, flops, room):
    place = {
        "s": pl.BlockSpec(memory_space=pltpu.SMEM),
        "v": pl.BlockSpec(memory_space=pltpu.VMEM),
        "a": pl.BlockSpec(memory_space=pl.ANY),
    }
    moved = sum(a.size * a.dtype.itemsize for a, _ in args)
    return pl.pallas_call(
        kernel,
        out_shape=[jax.ShapeDtypeStruct(shape, dtype) for shape, dtype, _ in outs],
        in_specs=[place[w] for _, w in args],
        out_specs=[place[w] for _, _, w in outs],
        scratch_shapes=scratch,
        compiler_params=pltpu.CompilerParams(vmem_limit_bytes=room * 2**20),
        cost_estimate=pl.CostEstimate(flops=int(flops), bytes_accessed=int(moved), transcendentals=0),
        name=name,
    )(*[a for a, _ in args])


def swap(block, axis):
    return lax.ppermute(block, axis, [(0, 1), (1, 0)])


def step(block, axis, steps):
    return lax.ppermute(block, axis, [((i + steps) % 4, i) for i in range(4)])


def sum_part(blocks, first, second):
    line = blocks[0].astype(F32)
    for k in (1, 2, 3):
        line = line + step(blocks[k], first, 4 - k).astype(F32)
    total = line[0]
    for k in (1, 2, 3):
        total = total + step(line[k].astype(BF), second, 4 - k).astype(F32)
    return total.astype(BF)


def regroup(block, pack):
    at, parts = 0, []
    for rows in pack:
        parts.append(block[:, at : at + rows].reshape(-1, HALF))
        at += rows
    return parts


def pick_table(indices, table):
    match = indices[:, None] == jnp.arange(table.shape[0], dtype=jnp.int32)[None, :]
    return jnp.sum(jnp.where(match, table[None, :], 0.0), axis=1)


def per_device(
    inputs,
    skipped,
    cotangent,
    timestep,
    class_ids,
    time_weight,
    class_weight,
    skip_weight,
    skip_bias,
    first_gain,
    first_shift,
    triple_weight,
    merge_weight,
    merge_bias,
    second_gain,
    second_shift,
    expand_weight,
    expand_bias,
    contract_weight,
    contract_bias,
):
    core_index = lax.axis_index("c").astype(jnp.int32)
    core = core_index[None]
    place = jnp.stack([core_index, lax.axis_index("y").astype(jnp.int32), lax.axis_index("x").astype(jnp.int32)])


    inputs, skipped, cotangent = (a.reshape(TOKENS, D) for a in (inputs, skipped, cotangent))
    sem = pltpu.SemaphoreType.DMA
    weight = lambda rows: pltpu.VMEM((PLANES, rows, HALF), BF)
    tokens = lambda width, dtype=BF, where="v": ((PAD, width), dtype, where)
    plane = lambda rows: ((PLANES, rows, HALF), BF, "a")

    vectors = (skip_bias, first_gain, first_shift, merge_bias, second_gain, second_shift, contract_bias, expand_bias)
    row, at = jnp.zeros((HALF,), F32), 0
    for vector in vectors:
        row = row + jnp.pad(vector.astype(F32), (at, HALF - at - vector.shape[0]))
        at += vector.shape[0]
    flat = dict(
        skip=skip_weight, triple=triple_weight, merge=merge_weight, expand=expand_weight, contract=contract_weight
    )
    flat = {name: a.reshape(-1, 128) for name, a in flat.items()}

    (packed,) = call(
        pack_kernel,
        "pack",
        [(flat[n], "a") for n in NAMES] + [(row[None], "v")],
        [((8, PACK_ROWS, HALF), BF, "v")],
        [pltpu.VMEM((2, PACK_ROWS, HALF), F32)]
        + [pltpu.VMEM(flat[n].shape, dtype) for dtype in (BF, F32) for n in NAMES]
        + [sem((len(NAMES),))],
        1e6,
        58,
    )
    column = regroup(lax.all_to_all(packed, COLUMN, 0, 0, tiled=True), PACK)
    first = jnp.concatenate(column[:2] + [jnp.zeros((8, HALF), BF)] + column[2:5], axis=0)
    second = jnp.concatenate(column[5:], axis=0)
    second_own = lax.all_gather(second, PLANE, axis=0, tiled=True).reshape(PLANES, SECOND_ROWS, HALF)
    first_own = lax.all_to_all(
        jnp.broadcast_to(first[None], (PLANES, FIRST_ROWS, HALF)), PLANE, 0, 0, tiled=True
    )
    first_own, timestep = lax.optimization_barrier((first_own, timestep))
    scale = pick_table(timestep, time_weight) * pick_table(class_ids, class_weight)
    first_other = swap(first_own, "c")
    after, gift = call(
        prepare_kernel,
        "prepare",
        [(core, "s"), (scale, "s"), (inputs, "v"), (skipped, "v"), (cotangent, "v")],
        [tokens(D), tokens(2 * D + HALF)],
        [],
        1e6,
        8,
    )
    gift_came = swap(gift, "c")

    (spots,) = call(
        spots_kernel, "vectors", [(first_own, "a")], [((16, D), F32, "v")], [weight(16), sem((1,))], 2e8, 8
    )
    united, normed, query, pair = call(
        first_kernel,
        "skip_and_triple",
        [(core, "s"), (gift, "v"), (first_own, "a"), (first_other, "a"), (spots, "v")],
        [tokens(D, F32), tokens(D), tokens(D), tokens(2 * D)],
        [weight(96), weight(96), weight(144), weight(144), sem((4,))],
        2 * PAD * D * (2 * D + 3 * D),
        16,
    )
    pair_came = swap(pair, "l")
    second_own, pair_came = lax.optimization_barrier((second_own, pair_came))
    second_other = swap(second_own, "c")
    normed_came = swap(normed, "c")
    mixed, totals = call(
        attend_kernel,
        "attention",
        [(query, "v"), (pair, "v"), (pair_came, "v")],
        [tokens(D), tokens(128, F32)],
        [],
        2 * PAD * D * 2 * KEYS,
        58,
    )
    mixed_came = swap(mixed, "c")
    output, middle_grad, early_vectors, forward_gift, forward_kept = call(
        forward_kernel,
        "feed_forward",
        [
            (core, "s"),
            (scale, "s"),
            (mixed, "v"),
            (united, "v"),
            (cotangent, "v"),
            (after, "v"),
            (second_own, "a"),
            (second_other, "a"),
            (spots, "v"),
        ],
        [((TOKENS, D), BF, "v"), tokens(D, F32), ((16, D), F32, "v"), tokens(GIFT), tokens(FF // 2)],
        [weight(192)] * 4
        + [weight(48)] * 2
        + [pltpu.VMEM((PAD, FF), F32), pltpu.VMEM((PAD, FF), BF), sem((12,))],
        2 * PAD * D * FF * 4,
        58,
    )
    forward_came = swap(forward_gift, "c")
    query_grad, pair_grad, pair_sent = call(
        backward_kernel,
        "attention_backward",
        [
            (core, "s"),
            (middle_grad, "v"),
            (query, "v"),
            (pair, "v"),
            (pair_came, "v"),
            (totals, "v"),
            (second_own, "a"),
            (second_other, "a"),
        ],
        [tokens(D), tokens(2 * D, F32), tokens(2 * D)],
        [pltpu.VMEM((PAD, D), BF), weight(48), weight(48), sem((2,))],
        2 * PAD * D * (D + 5 * KEYS),
        58,
    )
    grad_came = swap(pair_sent, "l")
    (early_grads,) = call(
        early_kernel,
        "early_gradients",
        [
            (core, "s"),
            (forward_gift, "a"),
            (forward_came, "a"),
            (forward_kept, "a"),
            (after, "v"),
            (gift_came, "v"),
            (mixed, "v"),
            (mixed_came, "v"),
            (middle_grad, "v"),
        ],
        [plane(EARLY_ROWS)],
        [pltpu.VMEM((PAD, GIFT), BF)] * 2
        + [pltpu.VMEM((PAD, FF // 2), BF), weight(EARLY_ROWS), sem((5,)), sem((6,))],
        2 * PAD * D * FF * 2,
        58,
    )
    early_sum = lax.psum_scatter(early_grads.reshape(PLANES * EARLY_ROWS, HALF), PLANE, scatter_dimension=0, tiled=True)
    early_vectors, query_grad = lax.optimization_barrier((early_vectors, query_grad))
    query_incoming, early_rows = call(
        query_kernel,
        "query_backward",
        [(core, "s"), (query_grad, "v"), (early_vectors, "v"), (first_own, "a"), (first_other, "a")],
        [tokens(D, F32), ((128, 128), F32, "v")],
        [weight(48)] * 2 + [sem((2,))],
        2 * PAD * D * D,
        12,
    )
    united_low, late_vectors, triple_kept, late_gift = call(
        triple_kernel,
        "triple_backward",
        [
            (core, "s"),
            (united, "v"),
            (middle_grad, "v"),
            (query_grad, "v"),
            (pair_grad, "v"),
            (grad_came, "v"),
            (query_incoming, "v"),
            (first_own, "a"),
            (first_other, "a"),
            (spots, "v"),
        ],
        [tokens(D), ((8, D), F32, "v"), tokens(3 * HALF), tokens(4 * HALF)],
        [weight(96)] * 2 + [sem((2,))],
        2 * PAD * D * (2 * D),
        16,
    )
    late_came = swap(late_gift, "c")
    input_grad, skip_grad = call(
        skip_kernel,
        "skip_backward",
        [(core, "s"), (united_low, "v"), (first_own, "a"), (first_other, "a")],
        [((TOKENS, D), BF, "v"), ((TOKENS, D), BF, "v")],
        [weight(96), weight(96), sem((2,))],
        2 * PAD * D * (2 * D),
        12,
    )
    late_came, input_grad, skip_grad = lax.optimization_barrier((late_came, input_grad, skip_grad))
    late = call(
        late_kernel,
        "late_gradients",
        [
            (place, "s"),
            (gift, "v"),
            (gift_came, "v"),
            (normed, "v"),
            (normed_came, "v"),
            (united_low, "v"),
            (triple_kept, "v"),
            (late_came, "v"),
            (early_rows, "v"),
            (late_vectors, "v"),
        ],
        [((4, ONE_ROWS, HALF), BF, "a")] * 4 + [((4, TWO_ROWS, HALF), BF, "a")] * 4,
        [weight(ONE_ROWS), weight(TWO_ROWS), sem((8,))],
        2 * PAD * D * (5 * D),
        58,
    )
    one_sum, two_sum = sum_part(late[:4], "x", "y"), sum_part(late[4:], "y", "x")

    (column,) = call(
        column_kernel,
        "by_device",
        [(one_sum, "v"), (two_sum, "v"), (early_sum, "v"), (jnp.asarray(column_moves(), BF), "v")],
        [((4, 2 * PACK_ROWS, HALF), BF, "v")],
        [pltpu.VMEM((SUM_ROWS, HALF), BF)],
        2 * SUM_ROWS * SUM_ROWS * HALF,
        12,
    )
    total = jnp.sum(lax.all_to_all(column, ("h", "l"), 0, 0, tiled=True).astype(F32), axis=0)
    mine, sent = order(core_index, total[:PACK_ROWS], total[PACK_ROWS:])
    low, high = order(core_index, mine, swap(sent, "c"))
    rows_of = lambda name: ((flat[name].shape[0], 128), F32, "v")
    skip_out, triple_out, expand_out, contract_out, merge_out, vector_out = call(
        unpack_kernel,
        "by_weight",
        [(low, "v"), (high, "v")],
        [rows_of(name) for name in NAMES] + [((1, 128), F32, "v")],
        [],
        1e6,
        8,
    )
    vector_out = vector_out[0]
    spot = lambda j: vector_out[6 * j : 6 * j + 6]
    return (
        output[None],
        input_grad[None],
        skip_grad[None],
        skip_out.reshape(-1),
        spot(0),
        spot(1),
        spot(2),
        triple_out.reshape(-1),
        merge_out.reshape(-1),
        spot(3),
        spot(4),
        spot(5),
        expand_out.reshape(-1),
        vector_out[42:66],
        contract_out.reshape(-1),
        spot(6),
    )


def solution(mesh):
    fine = jax.sharding.Mesh(mesh.devices.reshape(4, 4, 2, 2, 2), ("y", "x", "h", "c", "l"))
    images = ("y", "x", "h", "c")
    everything = images + ("l",)
    tokens, shard = P(images, "l", None), P(everything)
    return jax.shard_map(
        per_device,
        mesh=fine,
        in_specs=(tokens,) * 3 + (P(images),) * 2 + (P(),) * 2 + (shard,) * 13,
        out_specs=(tokens,) * 3 + (shard,) * 13,
        check_vma=False,
    )
```

time: 298 us -> 265 us (0.89); the launches traced: 292 us -> 264 us
  local copies, waits for them, and re-layouts: 27.1 us -> 12.6 us
  blocking collectives: 56.2 us -> 67.6 us
  starting transfers between devices: 36.7 us -> 27.1 us
  waiting for transfers between devices: 83.9 us -> 75.5 us
  other arithmetic: 11.3 us -> 4.24 us
    all_to_all x0 -> x1, blocking collectives: none -> 16.9 us  [per_device(): column = regroup(lax.all_to_all(packed, COLUMN, 0, 0, tiled=True), PACK)]
    concatenate x7 -> x2, local copies, waits for them, and re-layouts: 9.13 us -> 0.02 us  [the longest x1 0.01 us: per_device(): second = jnp.concatenate(column[5:], axis=0)]
    reshape x21 -> x0, local copies, waits for them, and re-layouts: 8.48 us -> none  [the longest x1 1.2 us: per_device(): column = column.reshape((4, 2) + column.shape[3:])]
    ppermute x12, waiting for transfers between devices: 33.5 us -> 25.1 us  [step(): return lax.ppermute(block, axis, [((i + steps) % 4, i) for i in range(4)])]
    all_to_all x1 -> x0, starting transfers between devices: 6.81 us -> none  [column_gather(): return lax.all_to_all(to_all, COLUMN, 0, 0, tiled=True)]
    convert_element_type x3 -> x0, other arithmetic: 6.62 us -> none  [the longest x1 5.95 us: per_device(): (second_kept.astype(F32) + second_came.astype(F32)).astype(BF)]
    all_to_all x1, blocking collectives: 56.2 us -> 50.7 us  [per_device(): lax.all_to_all(jnp.broadcast_to(first[None], (PLANES, FIRST_ROWS, HALF)),...]
    unnamed x36 -> x70, local copies, waits for them, and re-layouts: 4.86 us -> 10.1 us
  transfers between devices with their start and end apart: 24 -> 25, of which waited for: 17 -> 16; matrix products, arithmetic and copies ran while one was open for 2% -> 1% of each run, Pallas kernels for 15% -> 14%
where the time goes in v3:
time: 265 us; the launch traced here: 264 us
  waiting for transfers between devices  75.5 us (28%)
  blocking collectives  67.6 us (26%)
  Pallas kernels  59.8 us (23%)
  starting transfers between devices  27.1 us (10%)
  between operations  17.2 us (6%)
  local copies, waits for them, and re-layouts  12.6 us (5%)
  other arithmetic  4.24 us (2%)
    pallas_call x14, Pallas kernels, call(): pl.pallas_call(kernel, out_shape=[jax.ShapeDtypeStruct(shape, dtype) for...  59.8 us
    all_to_all x1, blocking collectives, per_device(): lax.all_to_all(jnp.broadcast_to(first[None], (PLANES, FIRST_ROWS, HALF)),...  50.7 us
    ppermute x10, waiting for transfers between devices, swap(): return lax.ppermute(block, axis, [(0, 1), (1, 0)])  25.7 us
    ppermute x12, waiting for transfers between devices, step(): return lax.ppermute(block, axis, [((i + steps) % 4, i) for i in range(4)])  25.1 us
    all_to_all x1, blocking collectives, per_device(): column = regroup(lax.all_to_all(packed, COLUMN, 0, 0, tiled=True), PACK)  16.9 us
    ppermute x12, starting transfers between devices, step(): return lax.ppermute(block, axis, [((i + steps) % 4, i) for i in range(4)])  13.8 us
    reduce_scatter x1, waiting for transfers between devices, per_device(): lax.psum_scatter(early_grads.reshape(PLANES * EARLY_ROWS, HALF), PLANE, s...  13.4 us
    unnamed x70, local copies, waits for them, and re-layouts  10.1 us
  transfers between devices with their start and end apart: 25, of which 16 were waited for; matrix products, arithmetic and copies ran while one was open for 1% of the time, Pallas kernels for 14%

profile of v3, /device:TPU:1, one launch (start us, length us, event | category | flops | bytes accessed | tf_op | source)
XLA Modules:
  0.0 264.0 jit_solution(10495202378188525360)
XLA Ops:
  8.6 2.4 pack.1
  11.1 16.9 %all_to_all.15 = bf16[8,88,384]{2,1,0:T(8,128)(2,1)S(1)} all-to-all(bf16[8,88,384]{2,1,0:T(8,128)(2,1)} %pack.1), channel_id=1, replica_groups=mesh['y'=4,'x'=4,'h'=2,'c'=2,'l'=2] {'h','c','l'}, dimensions={0} | all-to-all | bytes 1081344 | tf_op jit(solution)/shard_map/all_to_all | solution.py:608
  29.8 50.7 %all_to_all.16.first_ref.own_ref = bf16[16,256,384]{2,1,0:T(8,128)(2,1)S(1)} all-to-all(bf16[16,256,384]{2,1,0:T(8,128)(2,1)S(1)} %broadcast_in_dim.41), channel_id=1, replica_groups=mesh['y'=4,'x'=4,'h'=2,'c'=2,'l'=2] {'y','x'}, dimensions={0} | all-to-all | bytes 6291456 | tf_op jit(solution)/shard_map/all_to_all | solution.py:612
  80.5 1.9 collective-permute-start
  89.2 2.9 %skip_and_triple.1 = (f32[144,768]{1,0:T(8,128)S(1)}, bf16[144,768]{1,0:T(8,128)(2,1)}, bf16[144,768]{1,0:T(8,128)(2,1)S(1)}, bf16[144,1536]{1,0:T(8,128)(2,1)S(1)}) custom-call(s32[1]{0:T(128)} %bitcast.core_ref, bf16[144,1920]{1,0:T(8,128)(2,1)S(1)} %get-tuple-element.64.joined_ref, bf16[16,256,384]{2,1,0:T(8,128)(2,1)S(1)} %all_to_all.16.first_ref.own_ref, ...), custom_call_target="tpu_custom_call" | custom-call | flops 849346560 | bytes 6893572 | tf_op jit(solution)/shard_map/skip_and_triple/pallas_call | solution.py:511
  94.9 11.5 %collective-permute-done.1.came_ref = bf16[144,1536]{1,0:T(8,128)(2,1)} collective-permute-done((bf16[144,1536]{1,0:T(8,128)(2,1)S(1)}, bf16[144,1536]{1,0:T(8,128)(2,1)}, u32[]{:S(2)}, u32[]{:S(2)}) %collective-permute-start.1) | collective-permute-done | bytes 442400 | tf_op jit(solution)/shard_map/ppermute | solution.py:524
  106.4 3.6 %all-gather.2.cloned.1.call-done = bf16[6912,384]{1,0:T(8,128)(2,1)} async-done(((bf16[432,384]{1,0:T(8,128)(2,1)}), bf16[6912,384]{1,0:T(8,128)(2,1)}) %all-gather.2.cloned.1.call-update) | async-done | bytes 5308432 | tf_op jit(solution)/shard_map/all_gather | solution.py:611
  110.6 6.8 %attention.1 = (bf16[144,768]{1,0:T(8,128)(2,1)}, f32[144,128]{1,0:T(8,128)}) custom-call(bf16[144,768]{1,0:T(8,128)(2,1)} %copy-done.5, bf16[144,1536]{1,0:T(8,128)(2,1)} %copy-done.1, bf16[144,1536]{1,0:T(8,128)(2,1)} %collective-permute-done.1.came_ref), custom_call_target="tpu_custom_call" | custom-call | flops 127401984 | bytes 1105920 | tf_op jit(solution)/shard_map/attention/pallas_call | solution.py:511
  117.4 1.9 collective-permute-done.2.other_ref
  119.3 11.5 %feed_forward.1 = (bf16[129,768]{1,0:T(8,128)(2,1)}, f32[144,768]{1,0:T(8,128)}, f32[16,768]{1,0:T(8,128)}, bf16[144,5760]{1,0:T(8,128)(2,1)}, bf16[144,1536]{1,0:T(8,128)(2,1)}) custom-call(s32[1]{0:T(128)} %bitcast.core_ref, f32[1]{0:T(128)} %bitcast.8.scale_ref, bf16[144,768]{1,0:T(8,128)(2,1)} %get-tuple-element.69.mixed_ref, f32[144,768]{1,0:T(8,128)} %copy-done.2, ...), custom_call_target="tpu_custom_call" | custom-call | flops 2717908992 | bytes 11748872 | tf_op jit(solution)/shard_map/feed_forward/pallas_call | solution.py:511
  131.8 3.4 %collective-permute-done.5.first_came_ref = bf16[144,1920]{1,0:T(8,128)(2,1)S(1)} collective-permute-done((bf16[144,1920]{1,0:T(8,128)(2,1)S(1)}, bf16[144,1920]{1,0:T(8,128)(2,1)S(1)}, u32[]{:S(2)}, u32[]{:S(2)}) %collective-permute-start.5) | collective-permute-done | bytes 552992 | tf_op jit(solution)/shard_map/ppermute | solution.py:524
  137.2 7.9 %early_gradients.1 = bf16[16,448,384]{2,1,0:T(8,128)(2,1)} custom-call(s32[1]{0:T(128)} %bitcast.core_ref, bf16[144,5760]{1,0:T(8,128)(2,1)} %get-tuple-element.102.gift_any, bf16[144,5760]{1,0:T(8,128)(2,1)} %copy-done.22, bf16[144,1536]{1,0:T(8,128)(2,1)} %get-tuple-element.103.kept_any, bf16[144,768]{1,0:T(8,128)(2,1)} %copy-done.6, ...), custom_call_target="tpu_custom_call" | custom-call | flops 1358954496 | bytes 5419012 | tf_op jit(solution)/shard_map/early_gradients/pallas_call | solution.py:511
  145.2 10.3 %attention_backward.1 = (bf16[144,768]{1,0:T(8,128)(2,1)}, f32[144,1536]{1,0:T(8,128)}, bf16[144,1536]{1,0:T(8,128)(2,1)}) custom-call(s32[1]{0:T(128)} %bitcast.core_ref, f32[144,768]{1,0:T(8,128)} %get-tuple-element.74.middle_grad_ref, bf16[144,768]{1,0:T(8,128)(2,1)} %copy-done.5, bf16[144,1536]{1,0:T(8,128)(2,1)} %copy-done.1, ...), custom_call_target="tpu_custom_call" | custom-call | flops 488374272 | bytes 12238852 | tf_op jit(solution)/shard_map/attention_backward/pallas_call | solution.py:511
  157.8 2.0 query_backward.1
  159.8 7.5 %collective-permute-done.3.came_ref = bf16[144,1536]{1,0:T(8,128)(2,1)S(1)} collective-permute-done((bf16[144,1536]{1,0:T(8,128)(2,1)}, bf16[144,1536]{1,0:T(8,128)(2,1)S(1)}, u32[]{:S(2)}, u32[]{:S(2)}) %collective-permute-start.3) | collective-permute-done | bytes 442400 | tf_op jit(solution)/shard_map/ppermute | solution.py:524
  167.3 3.2 %triple_backward.1 = (bf16[144,768]{1,0:T(8,128)(2,1)S(1)}, f32[8,768]{1,0:T(8,128)S(1)}, bf16[144,1152]{1,0:T(8,128)(2,1)S(1)}, bf16[144,1536]{1,0:T(8,128)(2,1)}) custom-call(s32[1]{0:T(128)} %bitcast.core_ref, f32[144,768]{1,0:T(8,128)S(1)} %copy-done.3, f32[144,768]{1,0:T(8,128)S(1)} %copy-done, bf16[144,768]{1,0:T(8,128)(2,1)S(1)} %copy-done.8, ...), custom_call_target="tpu_custom_call" | custom-call | flops 339738624 | bytes 9216004 | tf_op jit(solution)/shard_map/triple_backward/pallas_call | solution.py:511
  173.6 3.0 %skip_backward.1 = (bf16[129,768]{1,0:T(8,128)(2,1)}, bf16[129,768]{1,0:T(8,128)(2,1)}) custom-call(s32[1]{0:T(128)} %bitcast.core_ref, bf16[144,768]{1,0:T(8,128)(2,1)S(1)} %get-tuple-element.84.low_ref, bf16[16,256,384]{2,1,0:T(8,128)(2,1)S(1)} %all_to_all.16.first_ref.own_ref, bf16[16,256,384]{2,1,0:T(8,128)(2,1)} %collective-permute-done.other_ref), custom_call_target="tpu_custom_call" | custom-call | flops 339738624 | bytes 6512644 | tf_op jit(solution)/shard_map/skip_backward/pallas_call | solution.py:511
  176.6 6.4 %late_gradients.1 = (bf16[4,112,384]{2,1,0:T(8,128)(2,1)}, bf16[4,112,384]{2,1,0:T(8,128)(2,1)}, bf16[4,112,384]{2,1,0:T(8,128)(2,1)}, bf16[4,112,384]{2,1,0:T(8...) custom-call(s32[3]{0:T(128)} %pad_add_fusion.place_ref, ...), custom_call_target="tpu_custom_call" | custom-call | flops 849346560 | bytes 2633740 | tf_op jit(solution)/shard_map/late_gradients/pallas_call | solution.py:511
  183.0 2.5 collective-permute-start.9
  188.4 9.3 %collective-permute-done.9 = bf16[4,112,384]{2,1,0:T(8,128)(2,1)S(1)} collective-permute-done((bf16[4,112,384]{2,1,0:T(8,128)(2,1)}, bf16[4,112,384]{2,1,0:T(8,128)(2,1)S(1)}, u32[]{:S(2)}, u32[]{:S(2)}) %collective-permute-start.9) | collective-permute-done | bytes 344096 | tf_op jit(solution)/shard_map/ppermute | solution.py:528
  198.2 2.0 collective-permute-done.8
  200.1 7.9 %collective-permute-done.7 = bf16[4,112,384]{2,1,0:T(8,128)(2,1)S(1)} collective-permute-done((bf16[4,112,384]{2,1,0:T(8,128)(2,1)}, bf16[4,112,384]{2,1,0:T(8,128)(2,1)S(1)}, u32[]{:S(2)}, u32[]{:S(2)}) %collective-permute-start.7) | collective-permute-done | bytes 344096 | tf_op jit(solution)/shard_map/ppermute | solution.py:528
  211.9 1.5 collective-permute-done.13
  213.7 3.3 %collective-permute-start.18 = (bf16[144,384]{1,0:T(8,128)(2,1)S(1)}, bf16[144,384]{1,0:T(8,128)(2,1)S(1)}, u32[]{:S(2)}, u32[]{:S(2)}) collective-permute-start(bf16[144,384]{1,0:T(8,128)(2,1)S(1)} %get-tuple-element.123), channel_id=1, source_target_pairs={{8,0},{16,8},{24,16},{0,24},{9,1},{17,9},{25,17},{1,25},{10,2},{18... | collective-permute-start | bytes 331784 | tf_op jit(solution)/shard_map/ppermute | solution.py:528
  217.0 1.7 collective-permute-start.17
  219.6 2.5 collective-permute-done.17
  222.1 1.4 collective-permute-done.16
  223.6 13.4 %reduce-scatter.2.cloned.1.call-done.early_ref = bf16[448,384]{1,0:T(8,128)(2,1)} async-done(((bf16[7168,384]{1,0:T(8,128)(2,1)}), bf16[448,384]{1,0:T(8,128)(2,1)}) %reduce-scatter.2.cloned.1.call-update) | async-done | bytes 344080 | tf_op jit(solution)/shard_map/reduce_scatter | solution.py:716
  237.9 1.6 by_device.1
  239.5 3.9 %all-to-all-start.2 = ((bf16[4,176,384]{2,1,0:T(8,128)(2,1)}), bf16[4,176,384]{2,1,0:T(8,128)(2,1)S(1)}, u32[]{:S(2)}, u32[]{:S(2)}) async-start(bf16[4,176,384]{2,1,0:T(8,128)(2,1)} %by_device.1), calls=%async_computation.3 | async-start | bytes 1081344 | tf_op jit(solution)/shard_map/all_to_all | solution.py:789
  243.4 7.7 %all-to-all-done.2 = bf16[4,176,384]{2,1,0:T(8,128)(2,1)S(1)} async-done(((bf16[4,176,384]{2,1,0:T(8,128)(2,1)}), bf16[4,176,384]{2,1,0:T(8,128)(2,1)S(1)}, u32[]{:S(2)}, u32[]{:S(2)}) %all-to-all-start.2) | async-done | bytes 540704 | tf_op jit(solution)/shard_map/all_to_all | solution.py:789
  251.2 3.0 %collective-permute-start.21 = (f32[88,384]{1,0:T(8,128)S(1)}, f32[88,384]{1,0:T(8,128)S(1)}, u32[]{:S(2)}, u32[]{:S(2)}) collective-permute-start(f32[88,384]{1,0:T(8,128)S(1)} %slice_select_fusion), channel_id=1, source_target_pairs={{0,2},{2,0},{1,3},{3,1},{4,6},{6,4},{5,7},{7,5},{8,10},{10,8},{9,1... | collective-permute-start | bytes 405512 | tf_op jit(solution)/shard_map/ppermute | solution.py:524
  (138 shorter events, 31.5 us)
Async XLA Ops:
  7.2 102.8 %all-gather.2.cloned.1.call-start = ((), (), s32[]{:S(2)}) async-start(), calls=%async_computation.4 | async-start | bytes 5640192 | tf_op jit(solution)/shard_map/all_gather | solution.py:611
  29.1 207.9 %reduce-scatter.2.cloned.1.call-start = ((), (), s32[]{:S(2)}) async-start(), calls=%async_computation.5 | async-start | bytes 5849088 | tf_op jit(solution)/shard_map/reduce_scatter | solution.py:716
  29.8 53.9 %copy-start.28 = (f32[1000]{0:T(1024)S(1)}, f32[1000]{0:T(1024)}, u32[]{:S(2)}) copy-start(f32[1000]{0:T(1024)} %param.26) | copy-start | bytes 12004
  29.8 54.5 %copy-start.29 = (f32[1001]{0:T(1024)S(1)}, f32[1001]{0:T(1024)}, u32[]{:S(2)}) copy-start(f32[1001]{0:T(1024)} %param.27) | copy-start | bytes 12016
  29.8 56.4 %copy-start.9 = (bf16[1,129,768]{2,1,0:T(8,128)(2,1)S(1)}, bf16[1,129,768]{2,1,0:T(8,128)(2,1)}, u32[]{:S(2)}) copy-start(bf16[1,129,768]{2,1,0:T(8,128)(2,1)} %param.23) | copy-start | bytes 594436
  80.5 8.7 %collective-permute-start = (bf16[16,256,384]{2,1,0:T(8,128)(2,1)S(1)}, bf16[16,256,384]{2,1,0:T(8,128)(2,1)}, u32[]{:S(2)}, u32[]{:S(2)}) collective-permute-start(bf16[16,256,384]{2,1,0:T(8,128)(2,1)S(1)} %all_to_all.16.first_ref.own_ref), channel_id=1, source_target_pairs={{0,2},{2,0},{1,3},{3,1},{4,6},{6,4},{5,7},{7,5},{8,10},{10,8},{9,1... | collective-permute-start | bytes 9437192 | tf_op jit(solution)/shard_map/ppermute | solution.py:524
  94.5 11.9 %collective-permute-start.1 = (bf16[144,1536]{1,0:T(8,128)(2,1)S(1)}, bf16[144,1536]{1,0:T(8,128)(2,1)}, u32[]{:S(2)}, u32[]{:S(2)}) collective-permute-start(bf16[144,1536]{1,0:T(8,128)(2,1)S(1)} %get-tuple-element.67.pair_ref), channel_id=1, source_target_pairs={{0,1},{1,0},{2,3},{3,2},{4,5},{5,4},{6,7},{7,6},{8,9},{9,8},{10,11... | collective-permute-start | bytes 1327112 | tf_op jit(solution)/shard_map/ppermute | solution.py:524
  109.9 9.4 %collective-permute-start.2 = (bf16[16,432,384]{2,1,0:T(8,128)(2,1)}, bf16[16,432,384]{2,1,0:T(8,128)(2,1)}, u32[]{:S(2)}, u32[]{:S(2)}) collective-permute-start(bf16[16,432,384]{2,1,0:T(8,128)(2,1)} %bitcast.82), channel_id=1, source_target_pairs={{0,2},{2,0},{1,3},{3,1},{4,6},{6,4},{5,7},{7,5},{8,10},{10,8},{9,1... | collective-permute-start | bytes 15925256 | tf_op jit(solution)/shard_map/ppermute | solution.py:524
  119.3 11.9 %copy-start.13 = (bf16[144,1920]{1,0:T(8,128)(2,1)S(1)}, bf16[144,1920]{1,0:T(8,128)(2,1)}, u32[]{:S(2)}) copy-start(bf16[144,1920]{1,0:T(8,128)(2,1)} %copy-done.12) | copy-start | bytes 1658884
  119.3 12.1 %copy-start.23 = (bf16[144,768]{1,0:T(8,128)(2,1)S(1)}, bf16[144,768]{1,0:T(8,128)(2,1)}, u32[]{:S(2)}) copy-start(bf16[144,768]{1,0:T(8,128)(2,1)} %get-tuple-element.69.mixed_ref) | copy-start | bytes 663556
  130.8 4.7 %collective-permute-start.19 = (bf16[144,5760]{1,0:T(8,128)(2,1)}, bf16[144,5760]{1,0:T(8,128)(2,1)S(1)}, u32[]{:S(2)}, u32[]{:S(2)}) collective-permute-start(bf16[144,5760]{1,0:T(8,128)(2,1)} %get-tuple-element.102.gift_any), channel_id=1, source_target_pairs={{0,2},{2,0},{1,3},{3,1},{4,6},{6,4},{5,7},{7,5},{8,10},{10,8},{9,1... | collective-permute-start | bytes 4976648 | tf_op jit(solution)/shard_map/ppermute | solution.py:524
  131.3 4.0 %collective-permute-start.5 = (bf16[144,1920]{1,0:T(8,128)(2,1)S(1)}, bf16[144,1920]{1,0:T(8,128)(2,1)S(1)}, u32[]{:S(2)}, u32[]{:S(2)}) collective-permute-start(bf16[144,1920]{1,0:T(8,128)(2,1)S(1)} %copy-done.13), channel_id=1, source_target_pairs={{0,2},{2,0},{1,3},{3,1},{4,6},{6,4},{5,7},{7,5},{8,10},{10,8},{9,1... | collective-permute-start | bytes 1658888 | tf_op jit(solution)/shard_map/ppermute | solution.py:524
  131.4 4.1 %collective-permute-start.20 = (bf16[144,768]{1,0:T(8,128)(2,1)S(1)}, bf16[144,768]{1,0:T(8,128)(2,1)S(1)}, u32[]{:S(2)}, u32[]{:S(2)}) collective-permute-start(bf16[144,768]{1,0:T(8,128)(2,1)S(1)} %copy-done.23), channel_id=1, source_target_pairs={{0,2},{2,0},{1,3},{3,1},{4,6},{6,4},{5,7},{7,5},{8,10},{10,8},{9,1... | collective-permute-start | bytes 663560 | tf_op jit(solution)/shard_map/ppermute | solution.py:524
  155.5 11.8 %collective-permute-start.3 = (bf16[144,1536]{1,0:T(8,128)(2,1)}, bf16[144,1536]{1,0:T(8,128)(2,1)S(1)}, u32[]{:S(2)}, u32[]{:S(2)}) collective-permute-start(bf16[144,1536]{1,0:T(8,128)(2,1)} %get-tuple-element.80), channel_id=1, source_target_pairs={{0,1},{1,0},{2,3},{3,2},{4,5},{5,4},{6,7},{7,6},{8,9},{9,8},{10,11... | collective-permute-start | bytes 1327112 | tf_op jit(solution)/shard_map/ppermute | solution.py:524
  171.9 4.7 %collective-permute-start.4 = (bf16[144,1536]{1,0:T(8,128)(2,1)}, bf16[144,1536]{1,0:T(8,128)(2,1)}, u32[]{:S(2)}, u32[]{:S(2)}) collective-permute-start(bf16[144,1536]{1,0:T(8,128)(2,1)} %get-tuple-element.83), channel_id=1, source_target_pairs={{0,2},{2,0},{1,3},{3,1},{4,6},{6,4},{5,7},{7,5},{8,10},{10,8},{9,1... | collective-permute-start | bytes 1327112 | tf_op jit(solution)/shard_map/ppermute | solution.py:524
  173.0 3.6 %collective-permute-start.6 = (bf16[144,768]{1,0:T(8,128)(2,1)}, bf16[144,768]{1,0:T(8,128)(2,1)}, u32[]{:S(2)}, u32[]{:S(2)}) collective-permute-start(bf16[144,768]{1,0:T(8,128)(2,1)} %get-tuple-element.89.normed_ref), channel_id=1, source_target_pairs={{0,2},{2,0},{1,3},{3,1},{4,6},{6,4},{5,7},{7,5},{8,10},{10,8},{9,1... | collective-permute-start | bytes 663560 | tf_op jit(solution)/shard_map/ppermute | solution.py:524
  183.0 30.4 %copy-start.25 = (bf16[4,144,384]{2,1,0:T(8,128)(2,1)S(1)}, bf16[4,144,384]{2,1,0:T(8,128)(2,1)}, u32[]{:S(2)}) copy-start(bf16[4,144,384]{2,1,0:T(8,128)(2,1)} %get-tuple-element.98) | copy-start | bytes 1327108
  183.0 14.6 %collective-permute-start.9 = (bf16[4,112,384]{2,1,0:T(8,128)(2,1)}, bf16[4,112,384]{2,1,0:T(8,128)(2,1)S(1)}, u32[]{:S(2)}, u32[]{:S(2)}) collective-permute-start(bf16[4,112,384]{2,1,0:T(8,128)(2,1)} %get-tuple-element.97), channel_id=1, source_target_pairs={{8,0},{16,8},{24,16},{0,24},{9,1},{17,9},{25,17},{1,25},{10,2},{18... | collective-permute-start | bytes 1032200 | tf_op jit(solution)/shard_map/ppermute | solution.py:528
  185.5 14.6 %collective-permute-start.8 = (bf16[4,112,384]{2,1,0:T(8,128)(2,1)}, bf16[4,112,384]{2,1,0:T(8,128)(2,1)S(1)}, u32[]{:S(2)}, u32[]{:S(2)}) collective-permute-start(bf16[4,112,384]{2,1,0:T(8,128)(2,1)} %get-tuple-element.96), channel_id=1, source_target_pairs={{16,0},{24,8},{0,16},{8,24},{17,1},{25,9},{1,17},{9,25},{18,2},{26... | collective-permute-start | bytes 1032200 | tf_op jit(solution)/shard_map/ppermute | solution.py:528
  186.1 22.0 %collective-permute-start.7 = (bf16[4,112,384]{2,1,0:T(8,128)(2,1)}, bf16[4,112,384]{2,1,0:T(8,128)(2,1)S(1)}, u32[]{:S(2)}, u32[]{:S(2)}) collective-permute-start(bf16[4,112,384]{2,1,0:T(8,128)(2,1)} %get-tuple-element.95), channel_id=1, source_target_pairs={{24,0},{0,8},{8,16},{16,24},{25,1},{1,9},{9,17},{17,25},{26,2},{2,... | collective-permute-start | bytes 1032200 | tf_op jit(solution)/shard_map/ppermute | solution.py:528
  186.6 25.3 %collective-permute-start.15 = (bf16[4,144,384]{2,1,0:T(8,128)(2,1)}, bf16[4,144,384]{2,1,0:T(8,128)(2,1)S(1)}, u32[]{:S(2)}, u32[]{:S(2)}) collective-permute-start(bf16[4,144,384]{2,1,0:T(8,128)(2,1)} %get-tuple-element.101), channel_id=1, source_target_pairs={{32,0},{64,32},{96,64},{0,96},{33,1},{65,33},{97,65},{1,97},{34,2}... | collective-permute-start | bytes 1327112 | tf_op jit(solution)/shard_map/ppermute | solution.py:528
  187.5 24.4 %collective-permute-start.14 = (bf16[4,144,384]{2,1,0:T(8,128)(2,1)}, bf16[4,144,384]{2,1,0:T(8,128)(2,1)S(1)}, u32[]{:S(2)}, u32[]{:S(2)}) collective-permute-start(bf16[4,144,384]{2,1,0:T(8,128)(2,1)} %get-tuple-element.100), channel_id=1, source_target_pairs={{64,0},{96,32},{0,64},{32,96},{65,1},{97,33},{1,65},{33,97},{66,2}... | collective-permute-start | bytes 1327112 | tf_op jit(solution)/shard_map/ppermute | solution.py:528
  197.7 15.8 %collective-permute-start.13 = (bf16[4,144,384]{2,1,0:T(8,128)(2,1)}, bf16[4,144,384]{2,1,0:T(8,128)(2,1)S(1)}, u32[]{:S(2)}, u32[]{:S(2)}) collective-permute-start(bf16[4,144,384]{2,1,0:T(8,128)(2,1)} %get-tuple-element.99), channel_id=1, source_target_pairs={{96,0},{0,32},{32,64},{64,96},{97,1},{1,33},{33,65},{65,97},{98,2}... | collective-permute-start | bytes 1327112 | tf_op jit(solution)/shard_map/ppermute | solution.py:528
  209.2 27.8 %copy-start.4 = (bf16[704,704]{1,0:T(8,128)(2,1)S(1)}, bf16[704,704]{1,0:T(8,128)(2,1)}, u32[]{:S(2)}) copy-start(bf16[704,704]{1,0:T(8,128)(2,1)} %constant.23.clone.moves_ref) | copy-start | bytes 2973700
  209.2 9.4 %collective-permute-start.12 = (bf16[112,384]{1,0:T(8,128)(2,1)S(1)}, bf16[112,384]{1,0:T(8,128)(2,1)S(1)}, u32[]{:S(2)}, u32[]{:S(2)}) collective-permute-start(bf16[112,384]{1,0:T(8,128)(2,1)S(1)} %get-tuple-element.128), channel_id=1, source_target_pairs={{32,0},{64,32},{96,64},{0,96},{33,1},{65,33},{97,65},{1,97},{34,2}... | collective-permute-start | bytes 258056 | tf_op jit(solution)/shard_map/ppermute | solution.py:528
  210.6 8.4 %collective-permute-start.11 = (bf16[112,384]{1,0:T(8,128)(2,1)S(1)}, bf16[112,384]{1,0:T(8,128)(2,1)S(1)}, u32[]{:S(2)}, u32[]{:S(2)}) collective-permute-start(bf16[112,384]{1,0:T(8,128)(2,1)S(1)} %get-tuple-element.129), channel_id=1, source_target_pairs={{64,0},{96,32},{0,64},{32,96},{65,1},{97,33},{1,65},{33,97},{66,2}... | collective-permute-start | bytes 258056 | tf_op jit(solution)/shard_map/ppermute | solution.py:528
  211.9 7.0 %collective-permute-start.10 = (bf16[112,384]{1,0:T(8,128)(2,1)S(1)}, bf16[112,384]{1,0:T(8,128)(2,1)S(1)}, u32[]{:S(2)}, u32[]{:S(2)}) collective-permute-start(bf16[112,384]{1,0:T(8,128)(2,1)S(1)} %get-tuple-element.127), channel_id=1, source_target_pairs={{96,0},{0,32},{32,64},{64,96},{97,1},{1,33},{33,65},{65,97},{98,2}... | collective-permute-start | bytes 258056 | tf_op jit(solution)/shard_map/ppermute | solution.py:528
  213.7 5.9 %collective-permute-start.18 = (bf16[144,384]{1,0:T(8,128)(2,1)S(1)}, bf16[144,384]{1,0:T(8,128)(2,1)S(1)}, u32[]{:S(2)}, u32[]{:S(2)}) collective-permute-start(bf16[144,384]{1,0:T(8,128)(2,1)S(1)} %get-tuple-element.123), channel_id=1, source_target_pairs={{8,0},{16,8},{24,16},{0,24},{9,1},{17,9},{25,17},{1,25},{10,2},{18... | collective-permute-start | bytes 331784 | tf_op jit(solution)/shard_map/ppermute | solution.py:528
  217.0 5.1 %collective-permute-start.17 = (bf16[144,384]{1,0:T(8,128)(2,1)S(1)}, bf16[144,384]{1,0:T(8,128)(2,1)S(1)}, u32[]{:S(2)}, u32[]{:S(2)}) collective-permute-start(bf16[144,384]{1,0:T(8,128)(2,1)S(1)} %get-tuple-element.124), channel_id=1, source_target_pairs={{16,0},{24,8},{0,16},{8,24},{17,1},{25,9},{1,17},{9,25},{18,2},{26... | collective-permute-start | bytes 331784 | tf_op jit(solution)/shard_map/ppermute | solution.py:528
  218.7 4.8 %collective-permute-start.16 = (bf16[144,384]{1,0:T(8,128)(2,1)S(1)}, bf16[144,384]{1,0:T(8,128)(2,1)S(1)}, u32[]{:S(2)}, u32[]{:S(2)}) collective-permute-start(bf16[144,384]{1,0:T(8,128)(2,1)S(1)} %get-tuple-element.122), channel_id=1, source_target_pairs={{24,0},{0,8},{8,16},{16,24},{25,1},{1,9},{9,17},{17,25},{26,2},{2,... | collective-permute-start | bytes 331784 | tf_op jit(solution)/shard_map/ppermute | solution.py:528
  239.5 11.6 %all-to-all-start.2 = ((bf16[4,176,384]{2,1,0:T(8,128)(2,1)}), bf16[4,176,384]{2,1,0:T(8,128)(2,1)S(1)}, u32[]{:S(2)}, u32[]{:S(2)}) async-start(bf16[4,176,384]{2,1,0:T(8,128)(2,1)} %by_device.1), calls=%async_computation.3 | async-start | bytes 1081344 | tf_op jit(solution)/shard_map/all_to_all | solution.py:789
  251.2 4.0 %collective-permute-start.21 = (f32[88,384]{1,0:T(8,128)S(1)}, f32[88,384]{1,0:T(8,128)S(1)}, u32[]{:S(2)}, u32[]{:S(2)}) collective-permute-start(f32[88,384]{1,0:T(8,128)S(1)} %slice_select_fusion), channel_id=1, source_target_pairs={{0,2},{2,0},{1,3},{3,1},{4,6},{6,4},{5,7},{7,5},{8,10},{10,8},{9,1... | collective-permute-start | bytes 405512 | tf_op jit(solution)/shard_map/ppermute | solution.py:524
  (23 other events, 84.0 us)
Sparse Core Ops, SparseCore 0:
  29.2 80.6 all-gather.1
  145.3 91.6 reduce-scatter.1
